TPU v7x, 32 devices: a whole 2x2x4 slice. The times are simulated.
32 devices in a mesh: seq: 8 (over y, x, core), tp: 4 (over z).
Axes of the slice: x: 2, y: 2, z: 4, core: 2. Of those that a mesh axis runs over, the one named last changes fastest.
Arguments:
- tokens: bfloat16 [8192, 1536], P(('seq', 'tp')), may hold values from -6 to 6
- lengths: int32 [6], replicated, may hold values from 1 to 6144, as said below
- first_gain: float32 [1536], replicated, may hold values from 0.5 to 1.5
- w_query: bfloat16 [1536, 1536], P(None, 'tp'), may hold values from -0.15625 to 0.15625
- w_keyval: bfloat16 [1536, 2, 768], P(None, None, 'tp'), may hold values from -0.15625 to 0.15625
- w_output: bfloat16 [1536, 1536], P('tp'), may hold values from -0.875 to 0.875
- second_gain: float32 [1536], replicated, may hold values from 0.5 to 1.5
- w_gateup: bfloat16 [1536, 2, 4096], P(None, None, 'tp'), may hold values from -0.15625 to 0.15625
- w_down: bfloat16 [4096, 1536], P('tp'), may hold values from -0.09375 to 0.09375
- cotangent: bfloat16 [8192, 1536], P(('seq', 'tp')), may hold values from -6 to 6
Outputs:
- result: bfloat16 [8192, 1536], P(('seq', 'tp'))
- tokens_grad: float32 [8192, 1536], P(('seq', 'tp'))
- first_gain_grad: float32 [1536], P(('seq', 'tp'))
- query_grad: float32 [1536, 1536], P('seq', 'tp')
- keyval_grad: float32 [1536, 2, 768], P('seq', None, 'tp')
- output_grad: float32 [1536, 1536], P('tp', 'seq')
- second_gain_grad: float32 [1536], P(('seq', 'tp'))
- gateup_grad: float32 [1536, 2, 4096], P('seq', None, 'tp')
- down_grad: float32 [4096, 1536], P('tp', 'seq')
Inputs may be any that keep to these rules, and one draw needn't show every extreme that they name: 6 lengths in pack order summing to 8192; no document begins at a nonzero multiple of 1024; exactly one document has 6144 tokens and every other one fewer than 1024.
All inputs are finite; a program needn't handle non-finite values.
Results may differ from a plain program's by a relative error of at most 0.02.
Values may be sent and summed in bfloat16 or wider, within the bound.
No kernel may reach another device: no remote copies, remote signals or barrier semaphores. Data moves between devices by JAX's collectives and lax.ppermute only.
A program may use at most 192 MiB of HBM per device.

v0:
```python
import jax
import jax.numpy as jnp
from jax import lax
from jax.sharding import PartitionSpec as P

HEAD_DIM = 96
WINDOW = 1024


EPSILON = 1e-05
THETA = 100000.0


def passed_along(shard, axis, by):
    size = lax.axis_size(axis)
    pairs = [(i, i + by) for i in range(size) if 0 <= i + by < size]
    return lax.ppermute(shard, axis, pairs)


def doc_places(lengths, token_ids):
    bounds = jnp.cumsum(lengths)
    passed = token_ids[:, None] >= bounds[None, :]
    segment = jnp.sum(passed.astype(jnp.int32), axis=1)
    begins = jnp.sum(jnp.where(passed, lengths[None, :], 0), axis=1)
    return (segment, token_ids - begins)


def rotate(values, places):
    half = values.shape[-1] // 2
    freqs = THETA ** (-2.0 * jnp.arange(half, dtype=jnp.float32) / values.shape[-1])
    angles = places.astype(jnp.float32)[:, None] * freqs[None, :]
    cosine = jnp.cos(angles)[:, None, :]
    sine = jnp.sin(angles)[:, None, :]
    first = values[..., :half]
    second = values[..., half:]
    return jnp.concatenate(
        [first * cosine - second * sine, second * cosine + first * sine], axis=-1
    )


def rms_scale(rows, gain):
    return rows * lax.rsqrt(jnp.mean(rows * rows, axis=-1, keepdims=True) + EPSILON) * gain


def swiglu(both):
    return jax.nn.silu(both[:, 0]) * both[:, 1]


def window_mask(query_ids, query_seg, key_ids, key_seg):
    return (
        (query_seg[:, None] == key_seg[None, :])
        & (key_ids[None, :] <= query_ids[:, None])
        & (query_ids[:, None] - key_ids[None, :] < WINDOW)
        & (key_ids[None, :] >= 0)
    )


def body(
    tokens,
    lengths,
    first_gain,
    w_query,
    w_keyval,
    w_output,
    second_gain,
    w_gateup,
    w_down,
    cotangent,
):
    owned = tokens.shape[0]
    rows = owned * lax.axis_size("tp")
    width = tokens.shape[1]
    qheads = w_query.shape[1] // HEAD_DIM
    kvheads = w_keyval.shape[2] // HEAD_DIM
    group = qheads // kvheads
    kvwidth = kvheads * HEAD_DIM
    units = w_down.shape[0]
    block = min(512, rows)
    span = WINDOW + block
    reach = -(-WINDOW // rows)
    blocks = rows // block
    scale = HEAD_DIM ** (-0.5)
    start_id = lax.axis_index("seq") * rows
    query_ids = start_id + jnp.arange(rows, dtype=jnp.int32)
    key_ids = start_id - reach * rows + jnp.arange((reach + 1) * rows, dtype=jnp.int32)
    query_seg, query_pos = doc_places(lengths, query_ids)
    key_seg, unused = doc_places(lengths, key_ids)
    resid = tokens.astype(jnp.float32)
    normed_one, first_back = jax.vjp(rms_scale, resid, first_gain)
    inputs_one = lax.all_gather(normed_one.astype(jnp.bfloat16), "tp", axis=0, tiled=True)
    query_flat = jnp.dot(inputs_one, w_query, preferred_element_type=jnp.float32)
    keyval_weight = w_keyval.reshape(width, 2 * kvwidth)
    keyval_flat = jnp.dot(inputs_one, keyval_weight, preferred_element_type=jnp.float32)
    queries = rotate(query_flat.reshape(rows, qheads, HEAD_DIM), query_pos).astype(jnp.bfloat16)
    keys_local = rotate(keyval_flat[:, :kvwidth].reshape(rows, kvheads, HEAD_DIM), query_pos)
    local_pair = jnp.concatenate(
        [keys_local.reshape(rows, kvwidth), keyval_flat[:, kvwidth:]], axis=1
    ).astype(jnp.bfloat16)
    earlier = [passed_along(local_pair, "seq", reach - 0)]
    pairs = jnp.concatenate(earlier + [local_pair], axis=0)

    def block_parts(pairs_all, index):
        first_row = index * block
        key_first = reach * rows - WINDOW + first_row
        query_block = lax.dynamic_slice_in_dim(queries, first_row, block, 0).reshape(
            block, kvheads, group, HEAD_DIM
        )
        pair_block = lax.dynamic_slice_in_dim(pairs_all, key_first, span, 0)
        key_block = pair_block[:, :kvwidth].reshape(span, kvheads, HEAD_DIM)
        value_block = pair_block[:, kvwidth:].reshape(span, kvheads, HEAD_DIM)
        mask = window_mask(
            lax.dynamic_slice_in_dim(query_ids, first_row, block, 0),
            lax.dynamic_slice_in_dim(query_seg, first_row, block, 0),
            lax.dynamic_slice_in_dim(key_ids, key_first, span, 0),
            lax.dynamic_slice_in_dim(key_seg, key_first, span, 0),
        )
        scores = (
            jnp.einsum("qkgd,skd->kgqs", query_block, key_block, preferred_element_type=jnp.float32)
            * scale
        )
        scores = jnp.where(mask, scores, -1e30)
        return (query_block, key_block, value_block, scores, first_row, key_first)

    def forward_block(index):
        query_block, key_block, value_block, scores, first_row, key_first = block_parts(
            pairs, index
        )
        top = jnp.max(scores, axis=-1, keepdims=True)
        weights = jnp.exp(scores - top)
        total = jnp.sum(weights, axis=-1, keepdims=True)
        probs = (weights / total).astype(jnp.bfloat16)
        mixed = jnp.einsum("kgqs,skd->qkgd", probs, value_block, preferred_element_type=jnp.float32)
        return (mixed.reshape(block, qheads * HEAD_DIM), top + jnp.log(total))

    mixed_all, log_totals = lax.map(forward_block, jnp.arange(blocks, dtype=jnp.int32))
    heads_out = mixed_all.reshape(rows, qheads * HEAD_DIM).astype(jnp.bfloat16)
    branch_one = lax.psum_scatter(
        jnp.dot(heads_out, w_output, preferred_element_type=jnp.float32).astype(jnp.bfloat16),
        "tp",
        scatter_dimension=0,
        tiled=True,
    ).astype(jnp.float32)
    resid_two = resid + branch_one
    normed_two, second_back = jax.vjp(rms_scale, resid_two, second_gain)
    inputs_two = lax.all_gather(normed_two.astype(jnp.bfloat16), "tp", axis=0, tiled=True)
    gateup_weight = w_gateup.reshape(width, 2 * units)
    gateup = jnp.dot(inputs_two, gateup_weight, preferred_element_type=jnp.float32).reshape(
        rows, 2, units
    )
    activated, swiglu_back = jax.vjp(swiglu, gateup)
    hidden = activated.astype(jnp.bfloat16)
    branch_two = lax.psum_scatter(
        jnp.dot(hidden, w_down, preferred_element_type=jnp.float32).astype(jnp.bfloat16),
        "tp",
        scatter_dimension=0,
        tiled=True,
    ).astype(jnp.float32)
    result = (resid_two + branch_two).astype(jnp.bfloat16)
    cotangent_all = lax.all_gather(cotangent, "tp", axis=0, tiled=True)
    hidden_grad = jnp.einsum("nd,fd->nf", cotangent_all, w_down, preferred_element_type=jnp.float32)
    down_grad = jnp.einsum("nf,nd->fd", hidden, cotangent_all, preferred_element_type=jnp.float32)
    (gateup_grad_full,) = swiglu_back(hidden_grad)
    gateup_low = gateup_grad_full.reshape(rows, 2 * units).astype(jnp.bfloat16)
    gateup_grad = jnp.einsum(
        "nd,nf->df", inputs_two, gateup_low, preferred_element_type=jnp.float32
    ).reshape(width, 2, units)
    second_input = lax.psum_scatter(
        jnp.einsum(
            "nf,df->nd", gateup_low, gateup_weight, preferred_element_type=jnp.float32
        ).astype(jnp.bfloat16),
        "tp",
        scatter_dimension=0,
        tiled=True,
    ).astype(jnp.float32)
    resid_two_part, second_gain_grad = second_back(second_input)
    resid_two_grad = cotangent.astype(jnp.float32) + resid_two_part
    branch_low = resid_two_grad.astype(jnp.bfloat16)
    branch_all = lax.all_gather(branch_low, "tp", axis=0, tiled=True)
    heads_grad = jnp.einsum(
        "nd,hd->nh", branch_all, w_output, preferred_element_type=jnp.float32
    ).astype(jnp.bfloat16)
    output_grad = jnp.einsum("nh,nd->hd", heads_out, branch_all, preferred_element_type=jnp.float32)

    def backward_block(carry, index):
        key_acc, value_acc = carry
        query_block, key_block, value_block, scores, first_row, key_first = block_parts(
            pairs, index
        )
        probs = jnp.exp(scores - lax.dynamic_index_in_dim(log_totals, index, 0, keepdims=False))
        out_grad = lax.dynamic_slice_in_dim(heads_grad, first_row, block, 0).reshape(
            block, kvheads, group, HEAD_DIM
        )
        prob_grad = jnp.einsum(
            "qkgd,skd->kgqs", out_grad, value_block, preferred_element_type=jnp.float32
        )
        center = jnp.sum(probs * prob_grad, axis=-1, keepdims=True)
        score_grad = (probs * (prob_grad - center)).astype(jnp.bfloat16)
        query_part = (
            jnp.einsum("kgqs,skd->qkgd", score_grad, key_block, preferred_element_type=jnp.float32)
            * scale
        )
        key_part = (
            jnp.einsum(
                "kgqs,qkgd->skd", score_grad, query_block, preferred_element_type=jnp.float32
            )
            * scale
        )
        value_part = jnp.einsum(
            "kgqs,qkgd->skd",
            probs.astype(jnp.bfloat16),
            out_grad,
            preferred_element_type=jnp.float32,
        )
        key_acc = lax.dynamic_update_slice_in_dim(
            key_acc, lax.dynamic_slice_in_dim(key_acc, key_first, span, 0) + key_part, key_first, 0
        )
        value_acc = lax.dynamic_update_slice_in_dim(
            value_acc,
            lax.dynamic_slice_in_dim(value_acc, key_first, span, 0) + value_part,
            key_first,
            0,
        )
        return ((key_acc, value_acc), query_part.reshape(block, qheads * HEAD_DIM))

    zeros = jnp.zeros(((reach + 1) * rows, kvheads, HEAD_DIM), jnp.float32)
    (key_acc, value_acc), query_parts = lax.scan(
        backward_block, (zeros, zeros), jnp.arange(blocks, dtype=jnp.int32)
    )
    pair_grads = jnp.concatenate(
        [key_acc.reshape(-1, kvwidth), value_acc.reshape(-1, kvwidth)], axis=1
    )
    returned = passed_along(
        pair_grads[0 * rows : (0 + 1) * rows].astype(jnp.bfloat16), "seq", 0 - reach
    ).astype(jnp.float32)
    local_grads = pair_grads[reach * rows :]
    local_grads = local_grads + returned
    query_low = (
        rotate(query_parts.reshape(rows, qheads, HEAD_DIM), -query_pos)
        .reshape(rows, -1)
        .astype(jnp.bfloat16)
    )
    key_grad = rotate(
        local_grads[:, :kvwidth].reshape(rows, kvheads, HEAD_DIM), -query_pos
    ).reshape(rows, kvwidth)
    keyval_low = jnp.concatenate([key_grad, local_grads[:, kvwidth:]], axis=1).astype(jnp.bfloat16)
    query_grad = jnp.einsum("nd,nh->dh", inputs_one, query_low, preferred_element_type=jnp.float32)
    keyval_grad = jnp.einsum(
        "nd,nh->dh", inputs_one, keyval_low, preferred_element_type=jnp.float32
    ).reshape(width, 2, kvwidth)
    first_input = lax.psum_scatter(
        (
            jnp.einsum("nh,dh->nd", query_low, w_query, preferred_element_type=jnp.float32)
            + jnp.einsum("nh,dh->nd", keyval_low, keyval_weight, preferred_element_type=jnp.float32)
        ).astype(jnp.bfloat16),
        "tp",
        scatter_dimension=0,
        tiled=True,
    ).astype(jnp.float32)
    resid_part, first_gain_grad = first_back(first_input)
    tokens_grad = resid_two_grad + resid_part
    first_gain_sum, second_gain_sum = (
        lax.psum_scatter(first_gain_grad, ("seq", "tp"), scatter_dimension=0, tiled=True),
        lax.psum_scatter(second_gain_grad, ("seq", "tp"), scatter_dimension=0, tiled=True),
    )
    query_shard, keyval_shard, output_shard, gateup_shard, down_shard = (
        lax.psum_scatter(query_grad, "seq", scatter_dimension=0, tiled=True),
        lax.psum_scatter(keyval_grad, "seq", scatter_dimension=0, tiled=True),
        lax.psum_scatter(output_grad, "seq", scatter_dimension=1, tiled=True),
        lax.psum_scatter(gateup_grad, "seq", scatter_dimension=0, tiled=True),
        lax.psum_scatter(down_grad, "seq", scatter_dimension=1, tiled=True),
    )
    return (
        result,
        tokens_grad,
        first_gain_sum,
        query_shard,
        keyval_shard,
        output_shard,
        second_gain_sum,
        gateup_shard,
        down_shard,
    )


def solution(mesh):
    return jax.shard_map(
        body,
        mesh=mesh,
        in_specs=(
            P(("seq", "tp"), None),
            P(),
            P(),
            P(None, "tp"),
            P(None, None, "tp"),
            P("tp", None),
            P(),
            P(None, None, "tp"),
            P("tp", None),
            P(("seq", "tp"), None),
        ),
        out_specs=(
            P(("seq", "tp"), None),
            P(("seq", "tp"), None),
            P(("seq", "tp")),
            P("seq", "tp"),
            P("seq", None, "tp"),
            P("tp", "seq"),
            P(("seq", "tp")),
            P("seq", None, "tp"),
            P("tp", "seq"),
        ),
        check_vma=False,
    )
```

profile of v0, /device:TPU:0, one launch (start us, length us, event | category | flops | bytes accessed | tf_op | source)
XLA Modules:
  0.0 1133.3 jit_solution(8708399442576339682)
XLA Ops:
  16.7 61.8 %all-gather.5.cloned.1.call-done = bf16[1024,1536]{1,0:T(8,128)(2,1)} async-done(((bf16[256,1536]{1,0:T(8,128)(2,1)}), bf16[1024,1536]{1,0:T(8,128)(2,1)}) %all-gather.5.cloned.1.call-update) | async-done | bytes 3145744 | tf_op jit(solution)/shard_map/all_gather | solution.py:90
  89.1 41.6 %while.26 = (s32[]{:T(128)}, bf16[2,512,384]{2,1,0:T(8,128)(2,1)}, f32[2,2,2,512,1]{3,2,1,4,0:T(2,128)}, s32[2]{0:T(128)}, bf16[2048,384]{0,1:T(8,128)(2,1)}, /*...) while((s32[]{:T(128)}, bf16[2,512,384]{2,1,0:T(8,128)(2,1)}, ...), condition=%wide.region_8.9_spmd, body=%wide.region_5.8_spmd.sunk | while | flops 1251212800 | bytes 50843948 | solution.py:135
  136.2 67.4 %reduce-scatter.9.cloned.1.call-done = bf16[256,1536]{1,0:T(8,128)(2,1)} async-done(((bf16[1024,1536]{1,0:T(8,128)(2,1)}), bf16[256,1536]{1,0:T(8,128)(2,1)}) %reduce-scatter.9.cloned.1.call-update) | async-done | bytes 786448 | tf_op jit(solution)/shard_map/reduce_scatter | solution.py:137
  208.6 8.0 copy.97
  216.6 8.8 copy.63
  225.4 46.3 %all-gather.7.cloned.1.call-done = bf16[1024,1536]{1,0:T(8,128)(2,1)} async-done(((bf16[256,1536]{1,0:T(8,128)(2,1)}), bf16[1024,1536]{1,0:T(8,128)(2,1)}) %all-gather.7.cloned.1.call-update) | async-done | bytes 3145744 | tf_op jit(solution)/shard_map/all_gather | solution.py:145
  271.6 11.8 %fusion.40 = f32[1024,2,1024]{0,2,1:T(8,128)} fusion(bf16[2,1024,1536]{2,1,0:T(8,128)(2,1)} %bitcast.260, bf16[1024,1536]{1,0:T(8,128)(2,1)} %all-gather.7.cloned.1.call-done), kind=kOutput, calls=%fused_computation.65 | convolution fusion | flops 6442450944 | bytes 17825792 | tf_op jit(solution)/shard_map/dot_general | solution.py:147
  283.4 51.9 %all-gather.9.cloned.1.call-done = bf16[1024,1536]{1,0:T(8,128)(2,1)} async-done(((bf16[256,1536]{1,0:T(8,128)(2,1)}), bf16[1024,1536]{1,0:T(8,128)(2,1)}) %all-gather.9.cloned.1.call-update) | async-done | bytes 3145744 | tf_op jit(solution)/shard_map/all_gather | solution.py:159
  335.3 9.1 multiply_bitcast_fusion
  347.6 10.6 bitcast_convert_fusion
  358.3 59.0 %reduce-scatter.13.cloned.1.call-done = bf16[256,1536]{1,0:T(8,128)(2,1)} async-done(((bf16[1024,1536]{1,0:T(8,128)(2,1)}), bf16[256,1536]{1,0:T(8,128)(2,1)}) %reduce-scatter.13.cloned.1.call-update) | async-done | bytes 786448 | tf_op jit(solution)/shard_map/reduce_scatter | solution.py:167
  423.6 63.6 %all-gather.11.cloned.1.call-done = bf16[1024,1536]{1,0:T(8,128)(2,1)} async-done(((bf16[256,1536]{1,0:T(8,128)(2,1)}), bf16[1024,1536]{1,0:T(8,128)(2,1)}) %all-gather.11.cloned.1.call-update) | async-done | bytes 3145744 | tf_op jit(solution)/shard_map/all_gather | solution.py:178
  495.3 153.2 %while.27 = (s32[]{:T(128)}, f32[2048,2,96]{0,2,1:T(8,128)}, f32[2048,2,96]{0,2,1:T(8,128)}, f32[2,512,384]{1,0,2:T(2,128)}, s32[2]{0:T(128)}, /*index=5*/bf16[1...) while((s32[]{:T(128)}, f32[2048,2,96]{0,2,1:T(8,128)}, ...), condition=%wide.region_16.17_spmd, body=%wide.region_14.16_spmd.sunk | while | flops 3054796288 | bytes 181169648 | solution.py:226
  502.6 7.5 fusion.152
  517.6 14.0 %fusion.154 = (f32[2,2,512]{2,1,0:T(2,128)S(1)}, f32[2,2,512,1536]{2,3,1,0:T(8,128)}) fusion(f32[2,1536,512,2]{2,1,3,0:T(8,128)} %fusion.152, f32[2,2,512]{2,1,0:T(2,128)S(1)} %dynamic-slice_bitcast_fusion.2, bf16[1536,2,96,1]{0,2,3,1:T(8,128)(2,1)} %bitcast.244, bf16[512,2,2,96]{0,3,2,1:T(8,128)(2,1)} %bitcast.248, pred[512,1536]{0,1:T(8,128)(4,1)} %fusion.153), kind=kOutput, calls=%fused_computation.18.clone.1 | convolution fusion | flops 619706368 | bytes 26951680 | tf_op jit(solution)/shard_map/while/body/eval_jaxpr/qkgd,skd->kgqs/dot_general | solution.py:118
  542.8 14.9 %dynamic_update_slice.30 = f32[2,512,384]{1,0,2:T(2,128)} dynamic-update-slice(f32[2,512,384]{1,0,2:T(2,128)} %get-tuple-element.546, f32[1,512,384]{1,0,2:T(1,128)} %copy.107, s32[]{:T(128)} %get-tuple-element.543, s32[]{:T(128)} %constant.55.clone.1..sunk.1, s32[]{:T(128)} %constant.55.clone.1..sunk.1) | dynamic-update-slice | bytes 1572868 | tf_op jit(solution)/shard_map/while/body/jit(dynamic_update_index_in_dim)/dynamic_update_slice | solution.py:135
  563.9 7.9 fusion.157
  579.0 7.5 fusion.152
  594.0 14.0 %fusion.154 = (f32[2,2,512]{2,1,0:T(2,128)S(1)}, f32[2,2,512,1536]{2,3,1,0:T(8,128)}) fusion(f32[2,1536,512,2]{2,1,3,0:T(8,128)} %fusion.152, f32[2,2,512]{2,1,0:T(2,128)S(1)} %dynamic-slice_bitcast_fusion.2, bf16[1536,2,96,1]{0,2,3,1:T(8,128)(2,1)} %bitcast.244, bf16[512,2,2,96]{0,3,2,1:T(8,128)(2,1)} %bitcast.248, pred[512,1536]{0,1:T(8,128)(4,1)} %fusion.153), kind=kOutput, calls=%fused_computation.18.clone.1 | convolution fusion | flops 619706368 | bytes 26951680 | tf_op jit(solution)/shard_map/while/body/eval_jaxpr/qkgd,skd->kgqs/dot_general | solution.py:118
  608.1 6.8 fusion.155
  619.2 14.9 %dynamic_update_slice.30 = f32[2,512,384]{1,0,2:T(2,128)} dynamic-update-slice(f32[2,512,384]{1,0,2:T(2,128)} %get-tuple-element.546, f32[1,512,384]{1,0,2:T(1,128)} %copy.107, s32[]{:T(128)} %get-tuple-element.543, s32[]{:T(128)} %constant.55.clone.1..sunk.1, s32[]{:T(128)} %constant.55.clone.1..sunk.1) | dynamic-update-slice | bytes 1572868 | tf_op jit(solution)/shard_map/while/body/jit(dynamic_update_index_in_dim)/dynamic_update_slice | solution.py:135
  640.4 7.9 fusion.157
  682.9 14.0 %fusion.34 = f32[1536,2,1024]{2,0,1:T(8,128)} fusion(bf16[1024,1536]{1,0:T(8,128)(2,1)} %all-gather.7.cloned.1.call-done, f32[1024,1,1024]{0,2,1:T(8,128)} %copy-done.32, f32[1024,1,1024]{0,2,1:T(8,128)} %copy-done.31), kind=kOutput, calls=%fused_computation.54 | convolution fusion | flops 6446645248 | bytes 24117248 | tf_op jit(solution)/shard_map/nd,nf->df/dot_general | solution.py:164
  696.9 8.6 fusion.74
  717.8 26.8 %all-reduce.8.cloned.1.call-done = f32[1536,2,192]{2,1,0:T(2,128)} async-done(((f32[1536,2,192]{2,1,0:T(2,128)}), f32[1536,2,192]{2,1,0:T(2,128)}) %all-reduce.8.cloned.1.call-update) | async-done | bytes 2359312
  746.5 60.9 %reduce-scatter.15.cloned.1.call-done = bf16[256,1536]{1,0:T(8,128)(2,1)} async-done(((bf16[1024,1536]{1,0:T(8,128)(2,1)}), bf16[256,1536]{1,0:T(8,128)(2,1)}) %reduce-scatter.15.cloned.1.call-update) | async-done | bytes 786448 | tf_op jit(solution)/shard_map/reduce_scatter | solution.py:250
  809.5 45.1 %all-reduce.5 = (f32[1536]{0:T(1024)S(1)}, f32[1536]{0:T(1024)S(1)}) all-reduce(f32[1536]{0:T(1024)S(1)} %get-tuple-element.226, f32[1536]{0:T(1024)S(1)} %copy-done.18), channel_id=6, replica_groups=mesh['seq'=8,'tp'=4] {'seq','tp'}, use_global_device_ids=true, to_apply=%region_20.21.clone | all-reduce | flops 3072 | bytes 24576
  855.7 15.5 %reduce-scatter.11.cloned.1.call-done = bf16[256,1536]{1,0:T(8,128)(2,1)} async-done(((bf16[1024,1536]{1,0:T(8,128)(2,1)}), bf16[256,1536]{1,0:T(8,128)(2,1)}) %reduce-scatter.11.cloned.1.call-update) | async-done | bytes 786448 | tf_op jit(solution)/shard_map/reduce_scatter | solution.py:152
  876.0 91.4 %reduce-scatter.21.cloned.1.call-done = f32[192,2,1024]{2,0,1:T(8,128)} async-done(((f32[1536,2,1024]{2,0,1:T(8,128)}), f32[192,2,1024]{2,0,1:T(8,128)}) %reduce-scatter.21.cloned.1.call-update) | async-done | bytes 1572880 | tf_op jit(solution)/shard_map/reduce_scatter | solution.py:269
  971.2 62.3 %reduce-scatter.23.cloned.1.call-done = f32[1024,192]{0,1:T(8,128)} async-done(((f32[1024,1536]{0,1:T(8,128)}), f32[1024,192]{0,1:T(8,128)}) %reduce-scatter.23.cloned.1.call-update) | async-done | bytes 786448 | tf_op jit(solution)/shard_map/reduce_scatter | solution.py:270
  1033.5 46.2 %reduce-scatter.19.cloned.1.call-done = f32[384,192]{0,1:T(8,128)} async-done(((f32[384,1536]{0,1:T(8,128)}), f32[384,192]{0,1:T(8,128)}) %reduce-scatter.19.cloned.1.call-update) | async-done | bytes 294928 | tf_op jit(solution)/shard_map/reduce_scatter | solution.py:268
  1079.7 46.8 %reduce-scatter.17.cloned.1.call-done = f32[192,384]{1,0:T(8,128)} async-done(((f32[1536,384]{1,0:T(8,128)}), f32[192,384]{1,0:T(8,128)}) %reduce-scatter.17.cloned.1.call-update) | async-done | bytes 294928 | tf_op jit(solution)/shard_map/reduce_scatter | solution.py:266
  (235 shorter events, 200.4 us)
Async XLA Ops:
  7.2 328.1 %copy-start = (bf16[1024,1536]{1,0:T(8,128)(2,1)S(1)}, bf16[1024,1536]{1,0:T(8,128)(2,1)}, u32[]{:S(2)}) copy-start(bf16[1024,1536]{1,0:T(8,128)(2,1)} %param.22) | copy-start | bytes 9437188
  7.2 71.4 %all-gather.5.cloned.1.call-start = ((), (), s32[]{:S(2)}) async-start(), calls=%async_computation.8 | async-start | bytes 3932160 | tf_op jit(solution)/shard_map/all_gather | solution.py:90
  12.2 191.5 %reduce-scatter.9.cloned.1.call-start = ((), (), s32[]{:S(2)}) async-start(), calls=%async_computation.9 | async-start | bytes 3932160 | tf_op jit(solution)/shard_map/reduce_scatter | solution.py:137
  82.6 4.7 collective-permute-start
  135.7 69.7 %copy-start.15 = (f32[1536]{0:T(1024)S(1)}, f32[1536]{0:T(1024)}, u32[]{:S(2)}) copy-start(f32[1536]{0:T(1024)} %param.20) | copy-start | bytes 18436
  135.7 135.9 %all-gather.7.cloned.1.call-start = ((), (), s32[]{:S(2)}) async-start(), calls=%async_computation.10 | async-start | bytes 3932160 | tf_op jit(solution)/shard_map/all_gather | solution.py:145
  205.4 214.8 %copy-start.19 = (f32[256]{0:T(256)}, f32[256]{0:T(256)S(1)}, u32[]{:S(2)}) copy-start(f32[256]{0:T(256)S(1)} %fusion.61) | copy-start | bytes 3076
  208.0 127.3 %all-gather.9.cloned.1.call-start = ((), (), s32[]{:S(2)}) async-start(), calls=%async_computation.12 | async-start | bytes 3932160 | tf_op jit(solution)/shard_map/all_gather | solution.py:159
  208.5 208.7 %reduce-scatter.13.cloned.1.call-start = ((), (), s32[]{:S(2)}) async-start(), calls=%async_computation.13 | async-start | bytes 3932160 | tf_op jit(solution)/shard_map/reduce_scatter | solution.py:167
  358.2 129.0 %all-gather.11.cloned.1.call-start = ((), (), s32[]{:S(2)}) async-start(), calls=%async_computation.14 | async-start | bytes 3932160 | tf_op jit(solution)/shard_map/all_gather | solution.py:178
  420.2 72.0 %copy-start.23 = (f32[256]{0:T(256)}, f32[256]{0:T(256)S(1)}, u32[]{:S(2)}) copy-start(f32[256]{0:T(256)S(1)} %multiply_multiply_fusion.1) | copy-start | bytes 3076
  423.5 321.1 %all-reduce.8.cloned.1.call-start = ((), (), s32[]{:S(2)}) async-start(), calls=%async_computation.20 | async-start | bytes 6291456
  516.7 14.9 %slice-start = ((s8[12582912]{0:T(1024)(128)(4,1)}), s8[4194304]{0:T(1024)(128)(4,1)S(1)}, s32[]{:S(2)}) async-start(s8[12582912]{0:T(1024)(128)(4,1)} %bitcast.242), calls=%async_computation.21 | async-start | bytes 8388608 | tf_op jit(solution)/shard_map/while
  517.6 14.0 %slice-start.1 = ((s8[12582912]{0:T(1024)(128)(4,1)}), s8[4194304]{0:T(1024)(128)(4,1)S(1)}, s32[]{:S(2)}) async-start(s8[12582912]{0:T(1024)(128)(4,1)} %bitcast.242), calls=%async_computation.22 | async-start | bytes 8388608 | tf_op jit(solution)/shard_map/while
  517.6 14.0 %slice-start.2 = ((s8[12582912]{0:T(1024)(128)(4,1)}), s8[4194304]{0:T(1024)(128)(4,1)S(1)}, s32[]{:S(2)}) async-start(s8[12582912]{0:T(1024)(128)(4,1)} %bitcast.242), calls=%async_computation.23 | async-start | bytes 8388608 | tf_op jit(solution)/shard_map/while
  593.1 14.9 %slice-start = ((s8[12582912]{0:T(1024)(128)(4,1)}), s8[4194304]{0:T(1024)(128)(4,1)S(1)}, s32[]{:S(2)}) async-start(s8[12582912]{0:T(1024)(128)(4,1)} %bitcast.242), calls=%async_computation.21 | async-start | bytes 8388608 | tf_op jit(solution)/shard_map/while
  594.0 14.0 %slice-start.1 = ((s8[12582912]{0:T(1024)(128)(4,1)}), s8[4194304]{0:T(1024)(128)(4,1)S(1)}, s32[]{:S(2)}) async-start(s8[12582912]{0:T(1024)(128)(4,1)} %bitcast.242), calls=%async_computation.22 | async-start | bytes 8388608 | tf_op jit(solution)/shard_map/while
  594.0 14.0 %slice-start.2 = ((s8[12582912]{0:T(1024)(128)(4,1)}), s8[4194304]{0:T(1024)(128)(4,1)S(1)}, s32[]{:S(2)}) async-start(s8[12582912]{0:T(1024)(128)(4,1)} %bitcast.242), calls=%async_computation.23 | async-start | bytes 8388608 | tf_op jit(solution)/shard_map/while
  650.9 4.7 collective-permute-start.1
  667.9 139.4 %reduce-scatter.15.cloned.1.call-start = ((), (), s32[]{:S(2)}) async-start(), calls=%async_computation.15 | async-start | bytes 3932160 | tf_op jit(solution)/shard_map/reduce_scatter | solution.py:250
  676.1 195.0 %reduce-scatter.11.cloned.1.call-start = ((), (), s32[]{:S(2)}) async-start(), calls=%async_computation.11 | async-start | bytes 3932160 | tf_op jit(solution)/shard_map/reduce_scatter | solution.py:152
  682.8 284.6 %reduce-scatter.21.cloned.1.call-start = ((), (), s32[]{:S(2)}) async-start(), calls=%async_computation.18 | async-start | bytes 14155776 | tf_op jit(solution)/shard_map/reduce_scatter | solution.py:269
  696.9 336.6 %reduce-scatter.23.cloned.1.call-start = ((), (), s32[]{:S(2)}) async-start(), calls=%async_computation.19 | async-start | bytes 7077888 | tf_op jit(solution)/shard_map/reduce_scatter | solution.py:270
  705.5 374.2 %reduce-scatter.19.cloned.1.call-start = ((), (), s32[]{:S(2)}) async-start(), calls=%async_computation.17 | async-start | bytes 2654208 | tf_op jit(solution)/shard_map/reduce_scatter | solution.py:268
  711.1 415.4 %reduce-scatter.17.cloned.1.call-start = ((), (), s32[]{:S(2)}) async-start(), calls=%async_computation.16 | async-start | bytes 2654208 | tf_op jit(solution)/shard_map/reduce_scatter | solution.py:266
  716.5 90.9 %copy-start.17 = (f32[1536]{0:T(1024)S(1)}, f32[1536]{0:T(1024)}, u32[]{:S(2)}) copy-start(f32[1536]{0:T(1024)} %param.16) | copy-start | bytes 18436
  716.5 90.9 %copy-start.22 = (f32[256]{0:T(256)S(1)}, f32[256]{0:T(256)}, u32[]{:S(2)}) copy-start(f32[256]{0:T(256)} %copy-done.21) | copy-start | bytes 3076
  716.5 92.9 %copy-start.18 = (f32[1536]{0:T(1024)S(1)}, f32[1536]{0:T(1024)}, u32[]{:S(2)}) copy-start(f32[1536]{0:T(1024)} %get-tuple-element.224) | copy-start | bytes 18436
  716.5 139.2 %copy-start.26 = (f32[256]{0:T(256)S(1)}, f32[256]{0:T(256)}, u32[]{:S(2)}) copy-start(f32[256]{0:T(256)} %copy-done.25) | copy-start | bytes 3076
  716.5 154.6 %copy-start.16 = (f32[1536]{0:T(1024)S(1)}, f32[1536]{0:T(1024)}, u32[]{:S(2)}) copy-start(f32[1536]{0:T(1024)} %param.20) | copy-start | bytes 18436
  716.5 154.6 %copy-start.20 = (f32[256]{0:T(256)S(1)}, f32[256]{0:T(256)}, u32[]{:S(2)}) copy-start(f32[256]{0:T(256)} %copy-done.19) | copy-start | bytes 3076
  716.5 154.6 %copy-start.24 = (f32[256]{0:T(256)S(1)}, f32[256]{0:T(256)}, u32[]{:S(2)}) copy-start(f32[256]{0:T(256)} %copy-done.23) | copy-start | bytes 3076
  (26 other events, 93.8 us)
Sparse Core Ops, SparseCore 0:
  12.3 66.1 all-gather.4
  135.8 67.7 reduce-scatter.8
  208.1 63.5 all-gather.6
  273.1 62.1 all-gather.8
  358.3 58.8 reduce-scatter.12
  423.6 63.5 all-gather.10
  668.1 76.5 all-reduce.7
  747.0 60.2 reduce-scatter.14
  809.8 61.3 reduce-scatter.10
  874.9 92.4 reduce-scatter.20
  971.7 61.7 reduce-scatter.22
  1037.3 42.4 reduce-scatter.18
  1084.0 42.4 reduce-scatter.16
where the time goes:
time: 1150 us; the launch traced here: 1130 us
  waiting for transfers between devices  701 us (61%)
  matrix products  182 us (16%)
  local copies, waits for them, and re-layouts  114 us (10%)
  other arithmetic  64.9 us (6%)
  blocking collectives  45.1 us (4%)
  between operations  15.2 us (1%)
    reduce_scatter x1, waiting for transfers between devices, body(): lax.psum_scatter(gateup_grad, 'seq', scatter_dimension=0, tiled=True)  91.4 us
    reduce_scatter x1, waiting for transfers between devices, body(): lax.psum_scatter(jnp.dot(heads_out, w_output, preferred_element_type=jnp....  67.4 us
    all_gather x1, waiting for transfers between devices, body(): branch_all = lax.all_gather(branch_low, 'tp', axis=0, tiled=True)  63.6 us
    reduce_scatter x1, waiting for transfers between devices, body(): lax.psum_scatter(down_grad, 'seq', scatter_dimension=1, tiled=True)  62.3 us
    all_gather x1, waiting for transfers between devices, body(): lax.all_gather(normed_one.astype(jnp.bfloat16), 'tp', axis=0, tiled=True)  61.8 us
    reduce_scatter x1, waiting for transfers between devices, body(): lax.psum_scatter((jnp.einsum('nh,dh->nd', query_low, w_query, preferred_e...  60.9 us
    reduce_scatter x1, waiting for transfers between devices, body(): lax.psum_scatter(jnp.einsum('nf,df->nd', gateup_low, gateup_weight, prefe...  59 us
    all_gather x1, waiting for transfers between devices, body(): cotangent_all = lax.all_gather(cotangent, 'tp', axis=0, tiled=True)  51.9 us
  transfers between devices with their start and end apart: 15, of which 13 were waited for; matrix products, arithmetic and copies ran while one was open for 9% of the time, Pallas kernels for 0%

commit v1 on v0

v1 whole, which is shorter than its diff:
```python
import jax
import jax.numpy as jnp
from jax import lax
from jax.experimental import pallas as pl
from jax.experimental.pallas import tpu as pltpu
from jax.sharding import PartitionSpec as P

HEAD_DIM = 96
HALF = HEAD_DIM // 2
LANES = 128
WINDOW = 1024
TILE = 256
EPSILON = 1e-05
THETA = 100000.0
SCALE = HEAD_DIM ** (-0.5)
LOG2E = 1.4426950408889634
SCALE2 = SCALE * LOG2E
BF = jnp.bfloat16
F32 = jnp.float32
NT = (((1,), (1,)), ((), ()))
NN = (((1,), (0,)), ((), ()))
TN = (((0,), (0,)), ((), ()))
MIB = 1 << 20


def dot(a, b, dims=NN):
    return lax.dot_general(a, b, dims, preferred_element_type=F32)


def doc_places(lengths, token_ids):
    bounds = jnp.cumsum(lengths)
    passed = token_ids[:, None] >= bounds[None, :]
    return jnp.sum(jnp.where(passed, lengths[None, :], 0), axis=1)


def spread_halves(w):
    n = w.shape[0]
    parts = w.reshape(n, -1, 2, HALF)
    parts = jnp.pad(parts, ((0, 0), (0, 0), (0, 0), (0, LANES // 2 - HALF)))
    return parts.reshape(n, -1)


def gather_halves(w):
    n = w.shape[0]
    return w.reshape(n, -1, 2, LANES // 2)[..., :HALF].reshape(n, -1)


def spread_heads(w):
    n = w.shape[0]
    parts = w.reshape(n, -1, HEAD_DIM)
    return jnp.pad(parts, ((0, 0), (0, 0), (0, LANES - HEAD_DIM))).reshape(n, -1)


def gather_heads(w):
    n = w.shape[0]
    return w.reshape(n, -1, LANES)[..., :HEAD_DIM].reshape(n, -1)


def rotation_tables(places):
    freqs = THETA ** (-2.0 * jnp.arange(HALF, dtype=F32) / HEAD_DIM)
    angles = places.astype(F32)[:, None] * freqs[None, :]
    cosine = jnp.pad(jnp.cos(angles), ((0, 0), (0, LANES // 2 - HALF)))
    sine = jnp.pad(jnp.sin(angles), ((0, 0), (0, LANES // 2 - HALF)))
    return (
        jnp.concatenate([cosine, cosine], axis=1),
        jnp.concatenate([-sine, sine], axis=1),
    )


def turn(u, cosine, sine):
    return u * cosine + pltpu.roll(u, LANES // 2, 1) * sine


def project_kernel(heads, x_ref, g_ref, w_ref, c_ref, s_ref, h_ref, q_ref, kv_ref):
    qheads, kvheads = heads
    x = x_ref[...].astype(F32)
    scale = lax.rsqrt(jnp.mean(x * x, axis=-1, keepdims=True) + EPSILON)
    h = (x * scale * g_ref[...]).astype(BF)
    h_ref[...] = h
    flat = dot(h, w_ref[...])
    cosine, sine = c_ref[...], s_ref[...]
    for n in range(qheads):
        q_ref[:, n * LANES : (n + 1) * LANES] = turn(
            flat[:, n * LANES : (n + 1) * LANES], cosine, sine
        ).astype(BF)
    for n in range(kvheads):
        at = (qheads + n) * LANES
        kv_ref[:, n * LANES : (n + 1) * LANES] = turn(
            flat[:, at : at + LANES], cosine, sine
        ).astype(BF)
    kv_ref[:, kvheads * LANES :] = flat[:, (qheads + kvheads) * LANES :].astype(BF)


def project(x_all, gain, weight, cosine, sine, qheads, kvheads):
    rows, width = x_all.shape
    tile = min(TILE, rows)
    wide = weight.shape[1]
    row = lambda n: pl.BlockSpec((tile, n), lambda i: (i, 0))
    whole = lambda m, n: pl.BlockSpec((m, n), lambda i: (0, 0))
    return pl.pallas_call(
        lambda *refs: project_kernel((qheads, kvheads), *refs),
        grid=(rows // tile,),
        in_specs=[row(width), whole(1, width), whole(width, wide), row(LANES), row(LANES)],
        out_specs=[row(width), row(qheads * LANES), row(2 * kvheads * LANES)],
        out_shape=[
            jax.ShapeDtypeStruct((rows, width), BF),
            jax.ShapeDtypeStruct((rows, qheads * LANES), BF),
            jax.ShapeDtypeStruct((rows, 2 * kvheads * LANES), BF),
        ],
        compiler_params=pltpu.CompilerParams(vmem_limit_bytes=40 * MIB),
        cost_estimate=pl.CostEstimate(
            flops=2 * rows * width * wide, bytes_accessed=4 * rows * width, transcendentals=0
        ),
    )(x_all, gain.reshape(1, width), weight, cosine, sine)


def masked(raw, first_key, lo, diagonal, query_ids):
    keys = first_key + lax.broadcasted_iota(jnp.int32, raw.shape, 0)
    ok = keys >= lo
    if diagonal:
        ok = ok & (keys <= query_ids)
    return jnp.where(ok, raw, -1e30)


def attend_kernel(q_ref, kp_ref, ko_ref, vp_ref, vo_ref, lo_ref, o_ref, l_ref, k_s, v_s):
    head, t = pl.program_id(0), pl.program_id(1)
    rows = ko_ref.shape[0]
    chunks = WINDOW // TILE + 1

    @pl.when(t == 0)
    def _():
        k_s[:rows] = kp_ref[...]
        k_s[rows:] = ko_ref[...]
        v_s[:rows] = vp_ref[...]
        v_s[rows:] = vo_ref[...]

    q = jnp.concatenate([q_ref[:, :LANES], q_ref[:, LANES:]], axis=0)
    lo = jnp.concatenate([lo_ref[...], lo_ref[...]], axis=1)
    ids = rows + t * TILE + lax.broadcasted_iota(jnp.int32, (1, TILE), 1)
    ids = jnp.concatenate([ids, ids], axis=1)
    scores = []
    for c in range(chunks):
        first = pl.multiple_of((t + c) * TILE, TILE)
        raw = dot(k_s[pl.ds(first, TILE)], q, NT)
        scores.append(masked(raw, first, lo, c == chunks - 1, ids))
    top = scores[0].max(axis=0, keepdims=True)
    for s in scores[1:]:
        top = jnp.maximum(top, s.max(axis=0, keepdims=True))
    top = top * SCALE2
    total = jnp.zeros_like(top)
    mixed = jnp.zeros((LANES, 2 * TILE), F32)
    for c in range(chunks):
        first = pl.multiple_of((t + c) * TILE, TILE)
        p = jnp.exp2(scores[c] * SCALE2 - top)
        total = total + jnp.sum(p, axis=0, keepdims=True)
        mixed = mixed + dot(v_s[pl.ds(first, TILE)], p.astype(BF), TN)
    l_ref[0, 0] = top + jnp.log2(total)
    out = jnp.transpose(mixed / total).astype(BF)
    first_row = pl.multiple_of(t * TILE, TILE)
    for n in range(2):

        @pl.when(head == n)
        def _():
            for g in range(2):
                at = (2 * n + g) * HEAD_DIM
                o_ref[pl.ds(first_row, TILE), at : at + HEAD_DIM] = out[
                    g * TILE : (g + 1) * TILE, :HEAD_DIM
                ]


def attend(queries, pair_before, pair_here, lo, kvheads):
    rows = queries.shape[0]
    tiles = rows // TILE
    key = lambda off: pl.BlockSpec((rows, LANES), lambda h, t: (0, h + off))
    return pl.pallas_call(
        attend_kernel,
        grid=(kvheads, tiles),
        in_specs=[
            pl.BlockSpec((TILE, 2 * LANES), lambda h, t: (t, h)),
            key(0),
            key(0),
            key(kvheads),
            key(kvheads),
            pl.BlockSpec((1, TILE), lambda h, t: (0, t)),
        ],
        out_specs=[
            pl.BlockSpec((rows, 2 * kvheads * HEAD_DIM), lambda h, t: (0, 0)),
            pl.BlockSpec((1, 1, 1, 2 * TILE), lambda h, t: (h, t, 0, 0)),
        ],
        out_shape=[
            jax.ShapeDtypeStruct((rows, 2 * kvheads * HEAD_DIM), BF),
            jax.ShapeDtypeStruct((kvheads, tiles, 1, 2 * TILE), F32),
        ],
        scratch_shapes=[pltpu.VMEM((2 * rows, LANES), BF), pltpu.VMEM((2 * rows, LANES), BF)],
        compiler_params=pltpu.CompilerParams(vmem_limit_bytes=40 * MIB),
        cost_estimate=pl.CostEstimate(
            flops=16 * MIB * 400, bytes_accessed=6 * MIB, transcendentals=5 * MIB
        ),
    )(queries, pair_before, pair_here, pair_before, pair_here, lo)


def attend_back_kernel(
    q_ref, kp_ref, ko_ref, vp_ref, vo_ref, lo_ref, o_ref, l_ref, do_ref, c_ref, s_ref,
    dq_ref, dkp_ref, dvp_ref, dk_ref, dv_ref, k_s, v_s, dk_s, dv_s,
):
    head, t = pl.program_id(0), pl.program_id(1)
    rows = ko_ref.shape[0]
    chunks = WINDOW // TILE + 1

    @pl.when(t == 0)
    def _():
        k_s[:rows] = kp_ref[...]
        k_s[rows:] = ko_ref[...]
        v_s[:rows] = vp_ref[...]
        v_s[rows:] = vo_ref[...]
        dk_s[...] = jnp.zeros_like(dk_s)
        dv_s[...] = jnp.zeros_like(dv_s)

    def heads_of(ref):
        both = ref[...]
        pair = jnp.where(head == 0, both[:, : 2 * HEAD_DIM], both[:, 2 * HEAD_DIM :])
        fill = jnp.zeros((TILE, LANES - HEAD_DIM), BF)
        return jnp.concatenate(
            [
                jnp.concatenate([pair[:, :HEAD_DIM], fill], axis=1),
                jnp.concatenate([pair[:, HEAD_DIM:], fill], axis=1),
            ],
            axis=0,
        )

    q = jnp.concatenate([q_ref[:, :LANES], q_ref[:, LANES:]], axis=0)
    lo = jnp.concatenate([lo_ref[...], lo_ref[...]], axis=1)
    ids = rows + t * TILE + lax.broadcasted_iota(jnp.int32, (1, TILE), 1)
    ids = jnp.concatenate([ids, ids], axis=1)
    grad = heads_of(do_ref)
    prod = grad.astype(F32) * heads_of(o_ref).astype(F32)
    center = jnp.sum(jnp.transpose(prod), axis=0, keepdims=True)
    logs = l_ref[0, 0]
    dq = jnp.zeros((LANES, 2 * TILE), F32)
    for c in range(chunks):
        first = pl.multiple_of((t + c) * TILE, TILE)
        here = pl.ds(first, TILE)
        keys = k_s[here]
        raw = masked(dot(keys, q, NT), first, lo, c == chunks - 1, ids)
        p = jnp.exp2(raw * SCALE2 - logs)
        dp = dot(v_s[here], grad, NT)
        ds = (p * (dp - center)).astype(BF)
        dv_s[here] += dot(p.astype(BF), grad)
        dk_s[here] += dot(ds, q)
        dq = dq + dot(keys, ds, TN)
    dq = jnp.transpose(dq) * SCALE
    cosine, sine = c_ref[...], -s_ref[...]
    for g in range(2):
        dq_ref[:, g * LANES : (g + 1) * LANES] = turn(
            dq[g * TILE : (g + 1) * TILE], cosine, sine
        ).astype(BF)

    @pl.when(t == pl.num_programs(1) - 1)
    def _():
        dkp_ref[...] = (dk_s[:rows] * SCALE).astype(BF)
        dvp_ref[...] = dv_s[:rows].astype(BF)
        dk_ref[...] = dk_s[rows:] * SCALE
        dv_ref[...] = dv_s[rows:]


def attend_back(queries, pair_before, pair_here, lo, heads_out, logs, grads, cosine, sine, kvheads):
    rows = queries.shape[0]
    tiles = rows // TILE
    key = lambda off: pl.BlockSpec((rows, LANES), lambda h, t: (0, h + off))
    tile_of = lambda n: pl.BlockSpec((TILE, n), lambda h, t: (t, 0))
    qtile = pl.BlockSpec((TILE, 2 * LANES), lambda h, t: (t, h))
    wide = kvheads * LANES
    return pl.pallas_call(
        attend_back_kernel,
        grid=(kvheads, tiles),
        in_specs=[
            qtile,
            key(0),
            key(0),
            key(kvheads),
            key(kvheads),
            pl.BlockSpec((1, TILE), lambda h, t: (0, t)),
            tile_of(2 * kvheads * HEAD_DIM),
            pl.BlockSpec((1, 1, 1, 2 * TILE), lambda h, t: (h, t, 0, 0)),
            tile_of(2 * kvheads * HEAD_DIM),
            tile_of(LANES),
            tile_of(LANES),
        ],
        out_specs=[qtile, key(0), key(0), key(0), key(0)],
        out_shape=[
            jax.ShapeDtypeStruct((rows, 2 * wide), BF),
            jax.ShapeDtypeStruct((rows, wide), BF),
            jax.ShapeDtypeStruct((rows, wide), BF),
            jax.ShapeDtypeStruct((rows, wide), F32),
            jax.ShapeDtypeStruct((rows, wide), F32),
        ],
        scratch_shapes=[
            pltpu.VMEM((2 * rows, LANES), BF),
            pltpu.VMEM((2 * rows, LANES), BF),
            pltpu.VMEM((2 * rows, LANES), F32),
            pltpu.VMEM((2 * rows, LANES), F32),
        ],
        compiler_params=pltpu.CompilerParams(vmem_limit_bytes=48 * MIB),
        cost_estimate=pl.CostEstimate(
            flops=16 * MIB * 1000, bytes_accessed=12 * MIB, transcendentals=5 * MIB
        ),
    )(
        queries, pair_before, pair_here, pair_before, pair_here, lo, heads_out, logs, grads,
        cosine, sine,
    )


def passed_along(shard, axis, by):
    size = lax.axis_size(axis)
    pairs = [(i, i + by) for i in range(size) if 0 <= i + by < size]
    return lax.ppermute(shard, axis, pairs)


def rms_scale(rows, gain):
    return rows * lax.rsqrt(jnp.mean(rows * rows, axis=-1, keepdims=True) + EPSILON) * gain


def swiglu(both):
    return jax.nn.silu(both[:, 0]) * both[:, 1]


def body(
    tokens, lengths, first_gain, w_query, w_keyval, w_output, second_gain, w_gateup, w_down,
    cotangent,
):
    owned, width = tokens.shape
    rows = owned * lax.axis_size("tp")
    qheads = w_query.shape[1] // HEAD_DIM
    kvheads = w_keyval.shape[2] // HEAD_DIM
    units = w_down.shape[0]
    start_id = lax.axis_index("seq") * rows
    query_ids = start_id + jnp.arange(rows, dtype=jnp.int32)
    begins = doc_places(lengths, query_ids)
    cosine, sine = rotation_tables(query_ids - begins)
    lo = jnp.maximum(query_ids - (WINDOW - 1), begins) - (start_id - rows)
    lo = lo.reshape(1, rows)
    weight_one = jnp.concatenate(
        [spread_halves(w_query), spread_halves(w_keyval[:, 0]), spread_heads(w_keyval[:, 1])],
        axis=1,
    )
    resid = tokens.astype(F32)
    x_all = lax.all_gather(tokens, "tp", axis=0, tiled=True)
    inputs_one, queries, pair_here = project(
        x_all, first_gain, weight_one, cosine, sine, qheads, kvheads
    )
    pair_before = passed_along(pair_here, "seq", 1)
    heads_out, logs = attend(queries, pair_before, pair_here, lo, kvheads)
    branch_one = lax.psum_scatter(
        dot(heads_out, w_output).astype(BF), "tp", scatter_dimension=0, tiled=True
    ).astype(F32)
    resid_two = resid + branch_one
    normed_two, second_back = jax.vjp(rms_scale, resid_two, second_gain)
    inputs_two = lax.all_gather(normed_two.astype(BF), "tp", axis=0, tiled=True)
    gateup_weight = w_gateup.reshape(width, 2 * units)
    gateup = dot(inputs_two, gateup_weight).reshape(rows, 2, units)
    activated, swiglu_back = jax.vjp(swiglu, gateup)
    hidden = activated.astype(BF)
    branch_two = lax.psum_scatter(
        dot(hidden, w_down).astype(BF), "tp", scatter_dimension=0, tiled=True
    ).astype(F32)
    result = (resid_two + branch_two).astype(BF)
    cotangent_all = lax.all_gather(cotangent, "tp", axis=0, tiled=True)
    hidden_grad = dot(cotangent_all, w_down, NT)
    down_grad = dot(hidden, cotangent_all, TN)
    (gateup_grad_full,) = swiglu_back(hidden_grad)
    gateup_low = gateup_grad_full.reshape(rows, 2 * units).astype(BF)
    gateup_grad = dot(inputs_two, gateup_low, TN).reshape(width, 2, units)
    second_input = lax.psum_scatter(
        dot(gateup_low, gateup_weight, NT).astype(BF), "tp", scatter_dimension=0, tiled=True
    ).astype(F32)
    resid_two_part, second_gain_grad = second_back(second_input)
    resid_two_grad = cotangent.astype(F32) + resid_two_part
    branch_all = lax.all_gather(resid_two_grad.astype(BF), "tp", axis=0, tiled=True)
    heads_grad = dot(branch_all, w_output, NT).astype(BF)
    output_grad = dot(heads_out, branch_all, TN)

    dq, dk_before, dv_before, dk_here, dv_here = attend_back(
        queries, pair_before, pair_here, lo, heads_out, logs, heads_grad, cosine, sine, kvheads
    )
    returned = passed_along(
        jnp.concatenate([dk_before, dv_before], axis=1), "seq", -1
    ).astype(F32)
    wide = kvheads * LANES
    dk = (dk_here + returned[:, :wide]).reshape(rows, kvheads, LANES)
    dk = dk * cosine[:, None, :] - jnp.roll(dk, LANES // 2, axis=2) * sine[:, None, :]
    dv = dv_here + returned[:, wide:]
    grads_one = jnp.concatenate(
        [dq, dk.reshape(rows, wide).astype(BF), dv.astype(BF)], axis=1
    )
    weight_grad = dot(inputs_one, grads_one, TN).astype(BF)
    query_grad = gather_halves(weight_grad[:, : qheads * LANES])
    keyval_grad = jnp.stack(
        [
            gather_halves(weight_grad[:, qheads * LANES : qheads * LANES + wide]),
            gather_heads(weight_grad[:, qheads * LANES + wide :]),
        ],
        axis=1,
    )
    first_input = lax.psum_scatter(
        dot(grads_one, weight_one, NT).astype(BF), "tp", scatter_dimension=0, tiled=True
    ).astype(F32)
    _, first_back = jax.vjp(rms_scale, resid, first_gain)
    resid_part, first_gain_grad = first_back(first_input)
    tokens_grad = resid_two_grad + resid_part
    both_axes = ("seq", "tp")
    scatter = lambda a, axis, dim: lax.psum_scatter(a, axis, scatter_dimension=dim, tiled=True)
    return (
        result,
        tokens_grad,
        scatter(first_gain_grad, both_axes, 0),
        scatter(query_grad, "seq", 0).astype(F32),
        scatter(keyval_grad, "seq", 0).astype(F32),
        scatter(output_grad.astype(BF), "seq", 1).astype(F32),
        scatter(second_gain_grad, both_axes, 0),
        scatter(gateup_grad.astype(BF), "seq", 0).astype(F32),
        scatter(down_grad.astype(BF), "seq", 1).astype(F32),
    )


def solution(mesh):
    both = ("seq", "tp")
    return jax.shard_map(
        body,
        mesh=mesh,
        in_specs=(
            P(both, None), P(), P(), P(None, "tp"), P(None, None, "tp"), P("tp", None), P(),
            P(None, None, "tp"), P("tp", None), P(both, None),
        ),
        out_specs=(
            P(both, None), P(both, None), P(both), P("seq", "tp"), P("seq", None, "tp"),
            P("tp", "seq"), P(both), P("seq", None, "tp"), P("tp", "seq"),
        ),
        check_vma=False,
    )
```

time: 1150 us -> 851 us (0.74)
  waiting for transfers between devices: 701 us -> 547 us
  matrix products: 182 us -> 80.9 us
  Pallas kernels: 0 us -> 41.7 us
  local copies, waits for them, and re-layouts: 114 us -> 74.7 us
  other arithmetic: 64.9 us -> 33.4 us
    reduce_scatter x8 -> x7, waiting for transfers between devices: 449 us -> 283 us  [the longest x3 76.9 us: body(): lax.psum_scatter(a, axis, scatter_dimension=dim, tiled=True)]
    dot_general x29 -> x11, matrix products: 182 us -> 80.9 us  [dot(): return lax.dot_general(a, b, dims, preferred_element_type=F32)]
    unnamed x14 -> x15, waiting for transfers between devices: 27.5 us -> 78.1 us
    pallas_call x0 -> x3, Pallas kernels: none -> 41.7 us  [the longest x1 22.3 us: attend_back(): pl.pallas_call(attend_back_kernel, grid=(kvheads, tiles), in_specs=[qtile...]
    all_gather x3, waiting for transfers between devices: 172 us -> 132 us  [the longest x1 46.1 us: body(): inputs_two = lax.all_gather(normed_two.astype(BF), 'tp', axis=0, tiled=True)]
    dynamic_update_slice x8 -> x0, local copies, waits for them, and re-layouts: 37.1 us -> none  [body(): lax.map(forward_block, jnp.arange(blocks, dtype=jnp.int32))]
    dynamic_slice x24 -> x0, local copies, waits for them, and re-layouts: 20.8 us -> none  [the longest x4 5.89 us: backward_block(): lax.dynamic_slice_in_dim(heads_grad, first_row, block, 0)]
    unnamed x64 -> x84, local copies, waits for them, and re-layouts: 22.6 us -> 41.6 us
  transfers between devices with their start and end apart: 15 -> 15, of which waited for: 13 -> 14; matrix products, arithmetic and copies ran while one was open for 9% -> 16% of each run, Pallas kernels for 0% -> 3%
where the time goes in v1:
time: 851 us; the launch traced here: 842 us
  waiting for transfers between devices  547 us (64%)
  matrix products  80.9 us (10%)
  local copies, waits for them, and re-layouts  74.7 us (9%)
  blocking collectives  45 us (5%)
  Pallas kernels  41.7 us (5%)
  other arithmetic  33.4 us (4%)
  between operations  14.6 us (2%)
    dot_general x11, matrix products, dot(): return lax.dot_general(a, b, dims, preferred_element_type=F32)  80.9 us
    unnamed x15, waiting for transfers between devices  78.1 us
    reduce_scatter x3, waiting for transfers between devices, body(): lax.psum_scatter(a, axis, scatter_dimension=dim, tiled=True)  76.9 us
    reduce_scatter x1, waiting for transfers between devices, body(): lax.psum_scatter(dot(heads_out, w_output).astype(BF), 'tp', scatter_dimen...  71.1 us
    reduce_scatter x1, waiting for transfers between devices, body(): lax.psum_scatter(dot(grads_one, weight_one, NT).astype(BF), 'tp', scatter...  60.7 us
    reduce_scatter x1, waiting for transfers between devices, body(): lax.psum_scatter(dot(gateup_low, gateup_weight, NT).astype(BF), 'tp', sca...  58.6 us
    all_gather x1, waiting for transfers between devices, body(): cotangent_all = lax.all_gather(cotangent, 'tp', axis=0, tiled=True)  51.8 us
    all_gather x1, waiting for transfers between devices, body(): inputs_two = lax.all_gather(normed_two.astype(BF), 'tp', axis=0, tiled=True)  46.1 us
  transfers between devices with their start and end apart: 15, of which 14 were waited for; matrix products, arithmetic and copies ran while one was open for 16% of the time, Pallas kernels for 3%

profile of v1, /device:TPU:0, one launch (start us, length us, event | category | flops | bytes accessed | tf_op | source)
XLA Modules:
  0.0 842.5 jit_solution(17069793004642663300)
XLA Ops:
  10.5 3.0 copy.52
  32.8 43.0 %all-gather.5.cloned.1.call-done.refs_0_ = bf16[1024,1536]{1,0:T(8,128)(2,1)} async-done(((bf16[256,1536]{1,0:T(8,128)(2,1)}), bf16[1024,1536]{1,0:T(8,128)(2,1)}) %all-gather.5.cloned.1.call-update) | async-done | bytes 3145744 | tf_op jit(solution)/shard_map/all_gather | solution.py:347
  81.7 5.7 shard_map.169
  95.5 13.8 %shard_map.170 = (bf16[1024,384]{1,0:T(8,128)(2,1)S(1)}, f32[2,4,1,512]{3,2,1,0:T(1,128)S(1)}) custom-call(bf16[1024,512]{1,0:T(8,128)(2,1)S(1)} %copy-done.16, bf16[1024,512]{1,0:T(8,128)(2,1)} %collective-permute-done.kp_ref.vp_ref, bf16[1024,512]{1,0:T(8,128)(2,1)} %get-tuple-element.20.ko_ref.vo_ref, ...), custom_call_target="tpu_custom_call" | custom-call | flops 6710886400 | bytes 6291456 | tf_op jit(solution)/shard_map/pallas_call | solution.py:175
  109.3 3.4 convolution_convert_fusion.1
  113.7 71.1 %reduce-scatter.14.cloned.1.call-done = bf16[256,1536]{1,0:T(8,128)(2,1)} async-done(((bf16[1024,1536]{1,0:T(8,128)(2,1)}), bf16[256,1536]{1,0:T(8,128)(2,1)}) %reduce-scatter.14.cloned.1.call-update) | async-done | bytes 786448 | tf_op jit(solution)/shard_map/reduce_scatter | solution.py:353
  190.0 8.0 copy.72
  198.0 8.7 %copy.55 = bf16[2048,1536]{1,0:T(8,128)(2,1)} copy(bf16[2048,1536]{0,1:T(8,128)(2,1)} %bitcast.86) | data formatting | bytes 12582912 | tf_op jit(solution)/shard_map/dot_general | solution.py:27
  206.7 46.1 %all-gather.7.cloned.1.call-done = bf16[1024,1536]{1,0:T(8,128)(2,1)} async-done(((bf16[256,1536]{1,0:T(8,128)(2,1)}), bf16[1024,1536]{1,0:T(8,128)(2,1)}) %all-gather.7.cloned.1.call-update) | async-done | bytes 3145744 | tf_op jit(solution)/shard_map/all_gather | solution.py:358
  252.8 11.8 %fusion.10 = f32[1024,2,1024]{0,2,1:T(8,128)} fusion(bf16[2,1024,1536]{2,1,0:T(8,128)(2,1)} %bitcast.88, bf16[1024,1536]{1,0:T(8,128)(2,1)} %all-gather.7.cloned.1.call-done), kind=kOutput, calls=%fused_computation.23 | convolution fusion | flops 6442450944 | bytes 17825792 | tf_op jit(solution)/shard_map/dot_general | solution.py:27
  264.6 51.8 %all-gather.9.cloned.1.call-done = bf16[1024,1536]{1,0:T(8,128)(2,1)} async-done(((bf16[256,1536]{1,0:T(8,128)(2,1)}), bf16[1024,1536]{1,0:T(8,128)(2,1)}) %all-gather.9.cloned.1.call-update) | async-done | bytes 3145744 | tf_op jit(solution)/shard_map/all_gather | solution.py:367
  316.4 9.1 %multiply_bitcast_fusion = (f32[1024,1,1024]{0,2,1:T(8,128)S(1)}, f32[1024,1,1024]{0,2,1:T(8,128)S(1)}, bf16[1024,1024]{0,1:T(8,128)(2,1)}) fusion(f32[1024,2,1024]{0,2,1:T(8,128)} %fusion.10, bf16[1024,1536]{1,0:T(8,128)(2,1)} %all-gather.9.cloned.1.call-done, bf16[1024,1536]{1,0:T(8,128)(2,1)S(1)} %copy-done), kind=kOutput, calls=%fused_computation.12 | convolution fusion | flops 3235905536 | bytes 25165824 | tf_op jit(solution)/shard_map/dot_general | solution.py:27
  328.8 10.5 %bitcast_convert_fusion = bf16[1024,1536]{1,0:T(8,128)(2,1)} fusion(bf16[1536,2,1024]{2,1,0:T(2,128)(2,1)} %param.17, f32[1024,1,1024]{0,2,1:T(8,128)S(1)} %get-tuple-element.73, f32[1024,1,1024]{0,2,1:T(8,128)S(1)} %get-tuple-element.72), kind=kOutput, calls=%fused_computation.1 | convolution fusion | flops 6448218112 | bytes 17825792 | tf_op jit(solution)/shard_map/dot_general | solution.py:27
  339.8 58.6 %reduce-scatter.18.cloned.1.call-done = bf16[256,1536]{1,0:T(8,128)(2,1)} async-done(((bf16[1024,1536]{1,0:T(8,128)(2,1)}), bf16[256,1536]{1,0:T(8,128)(2,1)}) %reduce-scatter.18.cloned.1.call-update) | async-done | bytes 786448 | tf_op jit(solution)/shard_map/reduce_scatter | solution.py:373
  400.9 3.4 fusion.30
  404.4 7.6 convolution_convert_fusion.2
  412.1 12.9 %convolution_convert_fusion = bf16[1536,2,1024]{2,0,1:T(8,128)(2,1)} fusion(bf16[1024,1536]{1,0:T(8,128)(2,1)} %all-gather.7.cloned.1.call-done, f32[1024,1,1024]{0,2,1:T(8,128)} %copy-done.35, f32[1024,1,1024]{0,2,1:T(8,128)} %copy-done.34), kind=kOutput, calls=%fused_computation.5 | convolution fusion | flops 6449790976 | bytes 17825792 | tf_op jit(solution)/shard_map/dot_general | solution.py:27
  425.1 42.9 %all-gather.11.cloned.1.call-done = bf16[1024,1536]{1,0:T(8,128)(2,1)} async-done(((bf16[256,1536]{1,0:T(8,128)(2,1)}), bf16[1024,1536]{1,0:T(8,128)(2,1)}) %all-gather.11.cloned.1.call-update) | async-done | bytes 3145744 | tf_op jit(solution)/shard_map/all_gather | solution.py:378
  468.0 4.1 convolution_convert_fusion.7.do_ref
  472.2 22.3 %shard_map.171 = (bf16[1024,512]{1,0:T(8,128)(2,1)S(1)}, bf16[1024,256]{1,0:T(8,128)(2,1)S(1)}, bf16[1024,256]{1,0:T(8,128)(2,1)S(1)}, f32[1024,256]{1,0:T(8,128)S(1)}, f32[1024,256]{1,0:T(8,128)}) custom-call(bf16[1024,512]{1,0:T(8,128)(2,1)} %copy-done.15, bf16[1024,512]{1,0:T(8,128)(2,1)} %collective-permute-done.kp_ref.vp_ref, ...), custom_call_target="tpu_custom_call" | custom-call | flops 16777216000 | bytes 12582912 | tf_op jit(solution)/shard_map/pallas_call | solution.py:273
  514.0 3.9 convolution_convert_fusion.3
  527.4 7.8 convolution_convert_fusion.4
  535.5 6.9 convolution_convert_fusion.5
  544.4 39.9 %reduce-scatter.24.cloned.1.call-done = bf16[192,2,1024]{2,0,1:T(8,128)(2,1)} async-done(((bf16[1536,2,1024]{2,0,1:T(8,128)(2,1)}), bf16[192,2,1024]{2,0,1:T(8,128)(2,1)}) %reduce-scatter.24.cloned.1.call-update) | async-done | bytes 786448 | tf_op jit(solution)/shard_map/reduce_scatter | solution.py:411
  584.3 3.1 copy.61
  587.4 37.0 %reduce-scatter.22.cloned.1.call-done = bf16[384,192]{0,1:T(8,128)(2,1)} async-done(((bf16[384,1536]{0,1:T(8,128)(2,1)}), bf16[384,192]{0,1:T(8,128)(2,1)}) %reduce-scatter.22.cloned.1.call-update) | async-done | bytes 147472 | tf_op jit(solution)/shard_map/reduce_scatter | solution.py:411
  626.0 38.6 %reduce-scatter.30.cloned.1.call-done = bf16[192,384]{1,0:T(8,128)(2,1)} async-done(((bf16[1536,384]{1,0:T(8,128)(2,1)}), bf16[192,384]{1,0:T(8,128)(2,1)}) %reduce-scatter.30.cloned.1.call-update) | async-done | bytes 147472
  666.5 38.1 %reduce-scatter.28.cloned.1.call-done = bf16[192,384]{1,0:T(8,128)(2,1)} async-done(((bf16[1536,384]{1,0:T(8,128)(2,1)}), bf16[192,384]{1,0:T(8,128)(2,1)}) %reduce-scatter.28.cloned.1.call-update) | async-done | bytes 147472
  706.5 60.7 %reduce-scatter.20.cloned.1.call-done = bf16[256,1536]{1,0:T(8,128)(2,1)} async-done(((bf16[1024,1536]{1,0:T(8,128)(2,1)}), bf16[256,1536]{1,0:T(8,128)(2,1)}) %reduce-scatter.20.cloned.1.call-update) | async-done | bytes 786448 | tf_op jit(solution)/shard_map/reduce_scatter | solution.py:404
  769.2 45.0 %all-reduce.9 = (f32[1536]{0:T(1024)S(1)}, f32[1536]{0:T(1024)S(1)}) all-reduce(f32[1536]{0:T(1024)S(1)} %get-tuple-element.67, f32[1536]{0:T(1024)S(1)} %get-tuple-element.65), channel_id=6, replica_groups=mesh['seq'=8,'tp'=4] {'seq','tp'}, use_global_device_ids=true, to_apply=%region_11.12.clone | all-reduce | flops 3072 | bytes 24576
  815.4 15.5 %reduce-scatter.16.cloned.1.call-done = bf16[256,1536]{1,0:T(8,128)(2,1)} async-done(((bf16[1024,1536]{1,0:T(8,128)(2,1)}), bf16[256,1536]{1,0:T(8,128)(2,1)}) %reduce-scatter.16.cloned.1.call-update) | async-done | bytes 786448 | tf_op jit(solution)/shard_map/reduce_scatter | solution.py:363
  830.9 4.9 fusion.19
  (157 shorter events, 88.8 us)
Async XLA Ops:
  7.2 309.2 %copy-start = (bf16[1024,1536]{1,0:T(8,128)(2,1)S(1)}, bf16[1024,1536]{1,0:T(8,128)(2,1)}, u32[]{:S(2)}) copy-start(bf16[1024,1536]{1,0:T(8,128)(2,1)} %param.18) | copy-start | bytes 9437188
  7.2 68.6 %all-gather.5.cloned.1.call-start = ((), (), s32[]{:S(2)}) async-start(), calls=%async_computation.9 | async-start | bytes 3932160 | tf_op jit(solution)/shard_map/all_gather | solution.py:347
  7.9 176.9 %reduce-scatter.14.cloned.1.call-start = ((), (), s32[]{:S(2)}) async-start(), calls=%async_computation.10 | async-start | bytes 3932160 | tf_op jit(solution)/shard_map/reduce_scatter | solution.py:353
  13.4 2.9 copy-start.24
  22.0 5.2 copy-start.29
  22.0 5.2 copy-start.31
  27.5 3.4 copy-start.20
  27.5 3.4 copy-start.22
  27.5 3.4 copy-start.23
  90.0 4.3 collective-permute-start
  95.5 13.8 %copy-start.33 = (bf16[384,1536]{1,0:T(8,128)(2,1)S(1)}, bf16[384,1536]{1,0:T(8,128)(2,1)}, u32[]{:S(2)}) copy-start(bf16[384,1536]{1,0:T(8,128)(2,1)} %param.15) | copy-start | bytes 3538948
  113.6 72.9 %copy-start.28 = (f32[1536]{0:T(1024)S(1)}, f32[1536]{0:T(1024)}, u32[]{:S(2)}) copy-start(f32[1536]{0:T(1024)} %param.16) | copy-start | bytes 18436
  113.6 139.2 %all-gather.7.cloned.1.call-start = ((), (), s32[]{:S(2)}) async-start(), calls=%async_computation.11 | async-start | bytes 3932160 | tf_op jit(solution)/shard_map/all_gather | solution.py:358
  189.1 127.3 %all-gather.9.cloned.1.call-start = ((), (), s32[]{:S(2)}) async-start(), calls=%async_computation.13 | async-start | bytes 3932160 | tf_op jit(solution)/shard_map/all_gather | solution.py:367
  189.7 208.7 %reduce-scatter.18.cloned.1.call-start = ((), (), s32[]{:S(2)}) async-start(), calls=%async_computation.14 | async-start | bytes 3932160 | tf_op jit(solution)/shard_map/reduce_scatter | solution.py:373
  325.5 3.3 copy-start.35
  339.4 128.6 %all-gather.11.cloned.1.call-start = ((), (), s32[]{:S(2)}) async-start(), calls=%async_computation.15 | async-start | bytes 3932160 | tf_op jit(solution)/shard_map/all_gather | solution.py:378
  404.3 138.1 %reduce-scatter.26.cloned.1.call-start = ((), (), s32[]{:S(2)}) async-start(), calls=%async_computation.19 | async-start | bytes 3538944 | tf_op jit(solution)/shard_map/reduce_scatter | solution.py:411
  412.0 172.3 %reduce-scatter.24.cloned.1.call-start = ((), (), s32[]{:S(2)}) async-start(), calls=%async_computation.18 | async-start | bytes 7077888 | tf_op jit(solution)/shard_map/reduce_scatter | solution.py:411
  425.0 199.3 %reduce-scatter.22.cloned.1.call-start = ((), (), s32[]{:S(2)}) async-start(), calls=%async_computation.17 | async-start | bytes 1327104 | tf_op jit(solution)/shard_map/reduce_scatter | solution.py:411
  468.0 4.2 copy-start.3
  468.0 4.2 copy-start.6
  468.0 4.2 copy-start.12
  472.2 25.9 %copy-start.32 = (bf16[1024,1536]{1,0:T(8,128)(2,1)S(1)}, bf16[1024,1536]{1,0:T(8,128)(2,1)}, u32[]{:S(2)}) copy-start(bf16[1024,1536]{1,0:T(8,128)(2,1)} %all-gather.11.cloned.1.call-done) | copy-start | bytes 9437188
  496.8 4.9 collective-permute-start.1
  501.0 163.6 %reduce-scatter.30.cloned.1.call-start = ((), (), s32[]{:S(2)}) async-start(), calls=%async_computation.21 | async-start | bytes 1327104
  507.5 4.1 copy-start.4
  512.3 5.6 copy-start.26
  522.4 182.2 %reduce-scatter.28.cloned.1.call-start = ((), (), s32[]{:S(2)}) async-start(), calls=%async_computation.20 | async-start | bytes 1327104
  527.3 239.8 %reduce-scatter.20.cloned.1.call-start = ((), (), s32[]{:S(2)}) async-start(), calls=%async_computation.16 | async-start | bytes 3932160 | tf_op jit(solution)/shard_map/reduce_scatter | solution.py:404
  535.3 295.6 %reduce-scatter.16.cloned.1.call-start = ((), (), s32[]{:S(2)}) async-start(), calls=%async_computation.12 | async-start | bytes 3932160 | tf_op jit(solution)/shard_map/reduce_scatter | solution.py:363
  542.4 224.8 %copy-start.30 = (f32[1536]{0:T(1024)S(1)}, f32[1536]{0:T(1024)}, u32[]{:S(2)}) copy-start(f32[1536]{0:T(1024)} %param.12) | copy-start | bytes 18436
  (20 other events, 34.2 us)
Sparse Core Ops, SparseCore 0:
  9.6 66.1 all-gather.4
  113.8 71.0 reduce-scatter.13
  189.2 63.5 all-gather.6
  254.2 62.1 all-gather.8
  339.5 58.8 reduce-scatter.17
  404.4 63.5 all-gather.10
  471.4 47.3 reduce-scatter.25
  522.5 61.7 reduce-scatter.23
  587.5 36.7 reduce-scatter.21
  627.7 36.7 reduce-scatter.29
  667.8 36.7 reduce-scatter.27
  706.9 60.2 reduce-scatter.19
  769.5 61.2 reduce-scatter.15

commit v2 on v1

v2 whole, which is shorter than its diff:
```python
import jax
import jax.numpy as jnp
from jax import lax
from jax.experimental import pallas as pl
from jax.experimental.pallas import tpu as pltpu
from jax.sharding import PartitionSpec as P

HEAD_DIM = 96
HALF = HEAD_DIM // 2
LANES = 128
WINDOW = 1024
TILE = 256
EPSILON = 1e-05
THETA = 100000.0
SCALE = HEAD_DIM ** (-0.5)
LOG2E = 1.4426950408889634
SCALE2 = SCALE * LOG2E
BF = jnp.bfloat16
F32 = jnp.float32
NT = (((1,), (1,)), ((), ()))
NN = (((1,), (0,)), ((), ()))
TN = (((0,), (0,)), ((), ()))
MIB = 1 << 20
AXES = ("seq", "tp")
ANY = pl.BlockSpec(memory_space=pl.ANY)


def dot(a, b, dims=NN):
    return lax.dot_general(a, b, dims, preferred_element_type=F32)


def shape(dims, dtype):
    return jax.ShapeDtypeStruct(dims, dtype)


def cost(flops, moved, exps=0):
    return pl.CostEstimate(flops=flops, bytes_accessed=moved, transcendentals=exps)


def params(mib):
    return pltpu.CompilerParams(vmem_limit_bytes=mib * MIB)


def send(a, to):
    size, ways = lax.axis_size("seq"), lax.axis_size("tp")
    pairs = []
    for s in range(size):
        for t in range(ways):
            there = to(s, t)
            if there is not None and 0 <= there[0] < size and 0 <= there[1] < ways:
                pairs.append((s * ways + t, there[0] * ways + there[1]))
    return lax.ppermute(a, AXES, pairs)


def doc_places(lengths, token_ids):
    bounds = jnp.cumsum(lengths)
    passed = token_ids[:, None] >= bounds[None, :]
    return jnp.sum(jnp.where(passed, lengths[None, :], 0), axis=1)


def spread_halves(w):
    n = w.shape[0]
    parts = w.reshape(n, -1, 2, HALF)
    parts = jnp.pad(parts, ((0, 0), (0, 0), (0, 0), (0, LANES // 2 - HALF)))
    return parts.reshape(n, -1)


def rotation_tables(places):
    freqs = THETA ** (-2.0 * jnp.arange(HALF, dtype=F32) / HEAD_DIM)
    angles = places.astype(F32)[:, None] * freqs[None, :]
    return jnp.cos(angles), jnp.sin(angles)


def lane_tables(cosine, sine):
    fill = ((0, 0), (0, LANES // 2 - HALF))
    cosine, sine = jnp.pad(cosine, fill), jnp.pad(sine, fill)
    return (
        jnp.concatenate([cosine, cosine], axis=1),
        jnp.concatenate([-sine, sine], axis=1),
    )


def project_kernel(
    sizes, sc_ref, own, r1, r2, r3, l1, l2, l3, g_ref, w_ref, c_ref, s_ref,
    h_ref, q_ref, kv_ref, x_s, sem,
):
    qheads, kvheads, ways = sizes
    o = pl.program_id(0)
    j = sc_ref[0]
    sources = {0: own, -1: r1, -2: r2, -3: r3, 1: l1, 2: l2, 3: l3}

    def fetch(at, slot):
        for d, ref in sources.items():

            @pl.when(at - j == d)
            def _():
                pltpu.make_async_copy(ref, x_s.at[slot], sem.at[slot]).start()

    @pl.when(o == 0)
    def _():
        fetch(0, 0)

    slot = lax.rem(o, 2)

    @pl.when(o + 1 < ways)
    def _():
        fetch(o + 1, 1 - slot)

    pltpu.make_async_copy(own, x_s.at[slot], sem.at[slot]).wait()
    x = x_s[slot].astype(F32)
    scale = lax.rsqrt(jnp.mean(x * x, axis=-1, keepdims=True) + EPSILON)
    h = (x * scale * g_ref[...]).astype(BF)
    h_ref[...] = h
    flat = dot(h, w_ref[...])
    cosine, sine = c_ref[...], s_ref[...]

    def turned(n):
        u = flat[:, n * LANES : (n + 1) * LANES]
        u = u * cosine + pltpu.roll(u, LANES // 2, 1) * sine
        return jnp.concatenate([u[:, :HALF], u[:, LANES // 2 : LANES // 2 + HALF]], axis=1)

    fill = jnp.zeros((x.shape[0], LANES - HEAD_DIM), F32)
    for n in range(qheads):
        q_ref[:, n * LANES : (n + 1) * LANES] = jnp.concatenate([turned(n), fill], axis=1).astype(
            BF
        )
    keys = [turned(qheads + n) for n in range(kvheads)]
    values = [flat[:, (qheads + kvheads) * LANES :]]
    kv_ref[...] = jnp.concatenate(keys + values, axis=1).astype(BF)


def project(sc, shards, gain, weight, cosine, sine, qheads, kvheads):
    owned, width = shards[0].shape
    ways = 4
    rows = owned * ways
    wide = weight.shape[1]
    kvwide = 2 * kvheads * HEAD_DIM
    row = lambda n: pl.BlockSpec((owned, n), lambda o, sc: (o, 0))
    whole = lambda m, n: pl.BlockSpec((m, n), lambda o, sc: (0, 0))
    return pl.pallas_call(
        lambda *refs: project_kernel((qheads, kvheads, ways), *refs),
        grid_spec=pltpu.PrefetchScalarGridSpec(
            num_scalar_prefetch=1,
            grid=(ways,),
            in_specs=[ANY] * 7 + [whole(1, width), whole(width, wide), row(LANES), row(LANES)],
            out_specs=[row(width), row(qheads * LANES), row(kvwide)],
            scratch_shapes=[pltpu.VMEM((2, owned, width), BF), pltpu.SemaphoreType.DMA((2,))],
        ),
        out_shape=[
            shape((rows, width), BF),
            shape((rows, qheads * LANES), BF),
            shape((rows, kvwide), BF),
        ],
        compiler_params=params(32),
        cost_estimate=cost(2 * rows * width * wide, 4 * rows * width),
    )(sc, *shards, gain.reshape(1, width), weight, cosine, sine)


def masked(raw, first_key, lo, diagonal, query_ids):
    keys = first_key + lax.broadcasted_iota(jnp.int32, raw.shape, 0)
    ok = keys >= lo
    if diagonal:
        ok = ok & (keys <= query_ids)
    return jnp.where(ok, raw, -1e30)


def load_pairs(kp_ref, ko_ref, k_s, v_s, head, kvheads):
    rows = ko_ref.shape[0]

    @pl.when(head == 0)
    def _():
        k_s[...] = jnp.zeros_like(k_s)
        v_s[...] = jnp.zeros_like(v_s)

    for n in range(kvheads):

        @pl.when(head == n)
        def _():
            for place, ref in ((0, kp_ref), (rows, ko_ref)):
                at = n * HEAD_DIM
                k_s[place : place + rows, :HEAD_DIM] = ref[:, at : at + HEAD_DIM]
                at = (kvheads + n) * HEAD_DIM
                v_s[place : place + rows, :HEAD_DIM] = ref[:, at : at + HEAD_DIM]


def tile_parts(q_ref, lo_ref, rows, t):
    q = jnp.concatenate([q_ref[:, :LANES], q_ref[:, LANES:]], axis=0)
    lo = jnp.concatenate([lo_ref[...], lo_ref[...]], axis=1)
    ids = rows + t * TILE + lax.broadcasted_iota(jnp.int32, (1, TILE), 1)
    return q, lo, jnp.concatenate([ids, ids], axis=1)


def attend_kernel(kvheads, q_ref, kp_ref, ko_ref, lo_ref, o_ref, l_ref, k_s, v_s):
    head, t = pl.program_id(0), pl.program_id(1)
    rows = ko_ref.shape[0]
    chunks = WINDOW // TILE + 1

    @pl.when(t == 0)
    def _():
        load_pairs(kp_ref, ko_ref, k_s, v_s, head, kvheads)

    q, lo, ids = tile_parts(q_ref, lo_ref, rows, t)
    scores = []
    for c in range(chunks):
        first = pl.multiple_of((t + c) * TILE, TILE)
        raw = dot(k_s[pl.ds(first, TILE)], q, NT)
        scores.append(masked(raw, first, lo, c == chunks - 1, ids))
    top = scores[0].max(axis=0, keepdims=True)
    for s in scores[1:]:
        top = jnp.maximum(top, s.max(axis=0, keepdims=True))
    top = top * SCALE2
    total = jnp.zeros_like(top)
    mixed = jnp.zeros((LANES, 2 * TILE), F32)
    for c in range(chunks):
        first = pl.multiple_of((t + c) * TILE, TILE)
        p = jnp.exp2(scores[c] * SCALE2 - top)
        total = total + jnp.sum(p, axis=0, keepdims=True)
        mixed = mixed + dot(v_s[pl.ds(first, TILE)], p.astype(BF), TN)
    l_ref[0, 0] = top + jnp.log2(total)
    out = jnp.transpose(mixed / total).astype(BF)
    here = pl.ds(pl.multiple_of(t * TILE, TILE), TILE)
    for n in range(kvheads):

        @pl.when(head == n)
        def _():
            for g in range(2):
                at = (2 * n + g) * HEAD_DIM
                o_ref[here, at : at + HEAD_DIM] = out[g * TILE : (g + 1) * TILE, :HEAD_DIM]


def attend(queries, pair_before, pair_here, lo, kvheads):
    rows = queries.shape[0]
    tiles = rows // TILE
    whole = pl.BlockSpec((rows, 2 * kvheads * HEAD_DIM), lambda h, t: (0, 0))
    return pl.pallas_call(
        lambda *refs: attend_kernel(kvheads, *refs),
        grid=(kvheads, tiles),
        in_specs=[
            pl.BlockSpec((TILE, 2 * LANES), lambda h, t: (t, h)),
            whole,
            whole,
            pl.BlockSpec((1, TILE), lambda h, t: (0, t)),
        ],
        out_specs=[whole, pl.BlockSpec((1, 1, 1, 2 * TILE), lambda h, t: (h, t, 0, 0))],
        out_shape=[
            shape((rows, 2 * kvheads * HEAD_DIM), BF),
            shape((kvheads, tiles, 1, 2 * TILE), F32),
        ],
        scratch_shapes=[pltpu.VMEM((2 * rows, LANES), BF), pltpu.VMEM((2 * rows, LANES), BF)],
        compiler_params=params(32),
        cost_estimate=cost(6400 * MIB, 5 * MIB, 5 * MIB),
    )(queries, pair_before, pair_here, lo)


def attend_back_kernel(
    kvheads, sc_ref, q_ref, kp_ref, ko_ref, lo_ref, o_ref, l_ref, g0_ref, g1_ref, g2_ref, g3_ref,
    c_ref, s_ref, dq_ref, dp_ref, dkv_ref, k_s, v_s, dk_s, dv_s,
):
    head, t = pl.program_id(0), pl.program_id(1)
    rows = ko_ref.shape[0]
    chunks = WINDOW // TILE + 1

    @pl.when(t == 0)
    def _():
        load_pairs(kp_ref, ko_ref, k_s, v_s, head, kvheads)
        dk_s[...] = jnp.zeros_like(dk_s)
        dv_s[...] = jnp.zeros_like(dv_s)

    def heads_of(both):
        pair = both[:, : 2 * HEAD_DIM]
        for n in range(1, kvheads):
            pair = jnp.where(
                head == n, both[:, 2 * n * HEAD_DIM : 2 * (n + 1) * HEAD_DIM], pair
            )
        fill = jnp.zeros((TILE, LANES - HEAD_DIM), BF)
        first = jnp.concatenate([pair[:, :HEAD_DIM], fill], axis=1)
        second = jnp.concatenate([pair[:, HEAD_DIM:], fill], axis=1)
        return jnp.concatenate([first, second], axis=0)

    q, lo, ids = tile_parts(q_ref, lo_ref, rows, t)
    apart = t ^ sc_ref[0]
    grad = g0_ref[0]
    for d, ref in ((1, g1_ref), (2, g2_ref), (3, g3_ref)):
        grad = jnp.where(apart == d, ref[...], grad)
    grad = heads_of(grad)
    prod = grad.astype(F32) * heads_of(o_ref[...]).astype(F32)
    center = jnp.sum(jnp.transpose(prod), axis=0, keepdims=True)
    logs = l_ref[0, 0]
    dq = jnp.zeros((LANES, 2 * TILE), F32)
    for c in range(chunks):
        first = pl.multiple_of((t + c) * TILE, TILE)
        here = pl.ds(first, TILE)
        keys = k_s[here]
        raw = masked(dot(keys, q, NT), first, lo, c == chunks - 1, ids)
        p = jnp.exp2(raw * SCALE2 - logs)
        dp = dot(v_s[here], grad, NT)
        ds = (p * (dp - center)).astype(BF)
        dv_s[here] += dot(p.astype(BF), grad)
        dk_s[here] += dot(ds, q)
        dq = dq + dot(keys, ds, TN)
    cosine = jnp.concatenate([c_ref[...], c_ref[...]], axis=1)
    sine = jnp.concatenate([s_ref[...], s_ref[...]], axis=1)
    a, b = dq[:HALF] * SCALE, dq[HALF:HEAD_DIM] * SCALE
    fill = jnp.zeros((LANES - HEAD_DIM, 2 * TILE), F32)
    dq = jnp.concatenate([a * cosine + b * sine, b * cosine - a * sine, fill], axis=0)
    dq = jnp.transpose(dq).astype(BF)
    mine = pl.ds(pl.multiple_of(t * TILE, TILE), TILE)
    last = t == pl.num_programs(1) - 1
    for n in range(kvheads):

        @pl.when(head == n)
        def _():
            for g in range(2):
                at = (2 * n + g) * HEAD_DIM
                dq_ref[mine, at : at + HEAD_DIM] = dq[g * TILE : (g + 1) * TILE, :HEAD_DIM]

        @pl.when((head == n) & last)
        def _():
            at = n * HEAD_DIM
            dp_ref[:, at : at + HEAD_DIM] = (dk_s[:rows, :HEAD_DIM] * SCALE).astype(BF)
            dkv_ref[:, at : at + HEAD_DIM] = dk_s[rows:, :HEAD_DIM] * SCALE
            at = (kvheads + n) * HEAD_DIM
            dp_ref[:, at : at + HEAD_DIM] = dv_s[:rows, :HEAD_DIM].astype(BF)
            dkv_ref[:, at : at + HEAD_DIM] = dv_s[rows:, :HEAD_DIM]


def attend_back(sc, queries, pair_before, pair_here, lo, heads_out, logs, grads, tables, kvheads):
    rows = queries.shape[0]
    tiles = rows // TILE
    wide = 2 * kvheads * HEAD_DIM
    whole = pl.BlockSpec((rows, wide), lambda h, t, sc: (0, 0))
    table = pl.BlockSpec((HALF, TILE), lambda h, t, sc: (0, t))
    piece = pl.BlockSpec((TILE, wide), lambda h, t, sc: (0, 0))
    return pl.pallas_call(
        lambda *refs: attend_back_kernel(kvheads, *refs),
        grid_spec=pltpu.PrefetchScalarGridSpec(
            num_scalar_prefetch=1,
            grid=(kvheads, tiles),
            in_specs=[
                pl.BlockSpec((TILE, 2 * LANES), lambda h, t, sc: (t, h)),
                whole,
                whole,
                pl.BlockSpec((1, TILE), lambda h, t, sc: (0, t)),
                pl.BlockSpec((TILE, wide), lambda h, t, sc: (t, 0)),
                pl.BlockSpec((1, 1, 1, 2 * TILE), lambda h, t, sc: (h, t, 0, 0)),
                pl.BlockSpec((1, TILE, wide), lambda h, t, sc: (sc[0], 0, 0)),
                piece,
                piece,
                piece,
                table,
                table,
            ],
            out_specs=[whole, whole, whole],
            scratch_shapes=[
                pltpu.VMEM((2 * rows, LANES), BF),
                pltpu.VMEM((2 * rows, LANES), BF),
                pltpu.VMEM((2 * rows, LANES), F32),
                pltpu.VMEM((2 * rows, LANES), F32),
            ],
        ),
        out_shape=[shape((rows, wide), BF), shape((rows, wide), BF), shape((rows, wide), F32)],
        compiler_params=params(40),
        cost_estimate=cost(16000 * MIB, 8 * MIB, 5 * MIB),
    )(sc, queries, pair_before, pair_here, lo, heads_out, logs, *grads, *tables)


def mix_kernel(
    sc_ref, o0_ref, o1_ref, o2_ref, o3_ref, w_ref, x_ref, xr_ref, xl_ref, g_ref,
    x2_ref, h2_ref, row_ref,
):
    m = pl.program_id(0)
    j = sc_ref[0]
    parts = [o0_ref[...], o1_ref[...], o2_ref[...], o3_ref[...]]
    acc = dot(parts[0], w_ref[j])
    for d in (1, 2, 3):
        acc = acc + dot(parts[d], w_ref[j ^ d])
    other = jnp.where((j & 1) == 1, xr_ref[...], xl_ref[...])
    x2 = jnp.where(m == 1, x_ref[...], other).astype(F32) + acc
    x2_ref[0] = x2
    scale = lax.rsqrt(jnp.mean(x2 * x2, axis=-1, keepdims=True) + EPSILON)
    h2_ref[0] = (x2 * scale * g_ref[...]).astype(BF)

    @pl.when(m == 1)
    def _():
        row_ref[...] = jnp.concatenate(parts, axis=1)


def mix(sc, heads_out, others, weight, tokens, right, left, gain):
    owned, width = tokens.shape
    local = heads_out.shape[1]
    ways = weight.shape[0]
    part = pl.BlockSpec((owned, local), lambda m, sc: ((sc[0] & 1) ^ 1 ^ m, 0))
    whole = lambda *dims: pl.BlockSpec(dims, lambda m, sc: (0,) * len(dims))
    return pl.pallas_call(
        mix_kernel,
        grid_spec=pltpu.PrefetchScalarGridSpec(
            num_scalar_prefetch=1,
            grid=(2,),
            in_specs=[
                pl.BlockSpec((owned, local), lambda m, sc: (sc[0] ^ 1 ^ m, 0)),
                part,
                part,
                part,
                whole(ways, local, width),
                whole(owned, width),
                whole(owned, width),
                whole(owned, width),
                whole(1, width),
            ],
            out_specs=[
                pl.BlockSpec((1, owned, width), lambda m, sc: (m, 0, 0)),
                pl.BlockSpec((1, owned, width), lambda m, sc: (m, 0, 0)),
                whole(owned, ways * local),
            ],
        ),
        out_shape=[
            shape((2, owned, width), F32),
            shape((2, owned, width), BF),
            shape((owned, ways * local), BF),
        ],
        compiler_params=params(40),
        cost_estimate=cost(4 * owned * ways * local * width, 12 * MIB),
    )(sc, heads_out, *others, weight, tokens, right, left, gain.reshape(1, width))


def feed_kernel(
    sc_ref, ho_ref, hs_ref, co_ref, cs_ref, gu_own, d_own, gu0, gu1, gu2, gu3, d0, d1, d2, d3,
    a_ref, dg_ref, du_ref, y_ref, dh_ref, gu_s, d_s, y_s, dh_s, sem,
):
    r = pl.program_id(0)
    steps = pl.num_programs(0)
    place, odd = sc_ref[1], sc_ref[2]
    taken = [(gu0, d0), (gu1, d1), (gu2, d2), (gu3, d3)]
    span = d_s.shape[1]

    def fetch(at, slot):
        @pl.when(odd == 0)
        def _():
            first = pl.multiple_of((place ^ at) * span, span)
            pltpu.make_async_copy(
                gu_own.at[:, :, pl.ds(first, span)], gu_s.at[slot], sem.at[0, slot]
            ).start()
            pltpu.make_async_copy(
                d_own.at[pl.ds(first, span)], d_s.at[slot], sem.at[1, slot]
            ).start()

        for k, (gu, d) in enumerate(taken):

            @pl.when((odd == 1) & (at == k))
            def _():
                pltpu.make_async_copy(gu, gu_s.at[slot], sem.at[0, slot]).start()
                pltpu.make_async_copy(d, d_s.at[slot], sem.at[1, slot]).start()

    @pl.when(r == 0)
    def _():
        fetch(0, 0)
        y_s[...] = jnp.zeros_like(y_s)
        dh_s[...] = jnp.zeros_like(dh_s)

    slot = lax.rem(r, 2)

    @pl.when(r + 1 < steps)
    def _():
        fetch(r + 1, 1 - slot)

    pltpu.make_async_copy(gu0, gu_s.at[slot], sem.at[0, slot]).wait()
    pltpu.make_async_copy(d0, d_s.at[slot], sem.at[1, slot]).wait()
    h = jnp.concatenate([hs_ref[0], ho_ref[0]], axis=0)
    ct = jnp.concatenate([cs_ref[0], co_ref[0]], axis=0)
    gate_w, up_w, down_w = gu_s[slot, 0], gu_s[slot, 1], d_s[slot]
    gate = dot(h, gate_w)
    up = dot(h, up_w)
    da = dot(ct, down_w, NT)
    sig = jax.nn.sigmoid(gate)
    act = gate * sig
    a = (act * up).astype(BF)
    dgate = (da * up * sig * (1.0 + gate * (1.0 - sig))).astype(BF)
    dup = (da * act).astype(BF)
    a_ref[...] = a
    dg_ref[...] = dgate
    du_ref[...] = dup
    y_s[...] += dot(a, down_w)
    dh_s[...] += dot(dgate, gate_w, NT) + dot(dup, up_w, NT)

    @pl.when(r == steps - 1)
    def _():
        half = y_ref.shape[1]
        for k in range(2):
            y_ref[k] = y_s[k * half : (k + 1) * half].astype(BF)
            dh_ref[k] = dh_s[k * half : (k + 1) * half].astype(BF)


def feed(m, sc, h_own, h_sib, ct_own, ct_sib, gu_own, d_own, gu_taken, d_taken):
    _, owned, width = h_own.shape
    units = d_own.shape[0]
    span = units // 4
    rows = pl.BlockSpec((1, owned, width), lambda r, sc: (m, 0, 0))
    out = pl.BlockSpec((2 * owned, span), lambda r, sc: (0, sc[1] ^ r))
    whole = pl.BlockSpec((2, owned, width), lambda r, sc: (0, 0, 0))
    return pl.pallas_call(
        feed_kernel,
        grid_spec=pltpu.PrefetchScalarGridSpec(
            num_scalar_prefetch=1,
            grid=(4,),
            in_specs=[rows] * 4 + [ANY] * 10,
            out_specs=[out, out, out, whole, whole],
            scratch_shapes=[
                pltpu.VMEM((2, 2, width, span), BF),
                pltpu.VMEM((2, span, width), BF),
                pltpu.VMEM((2 * owned, width), F32),
                pltpu.VMEM((2 * owned, width), F32),
                pltpu.SemaphoreType.DMA((2, 2)),
            ],
        ),
        out_shape=[shape((2 * owned, units), BF)] * 3 + [shape((2, owned, width), BF)] * 2,
        compiler_params=params(48),
        cost_estimate=cost(36 * owned * width * units, 22 * MIB, 2 * owned * units),
    )(sc, h_own, h_sib, ct_own, ct_sib, gu_own, d_own, *gu_taken, *d_taken)


def feed_grad_kernel(
    sc_ref, ho_ref, hs_ref, co_ref, cs_ref, a0, dg0, du0, a1, dg1, du1, gu_ref, d_ref
):
    h = jnp.concatenate([hs_ref[0], ho_ref[0], hs_ref[1], ho_ref[1]], axis=0)
    ct = jnp.concatenate([cs_ref[0], co_ref[0], cs_ref[1], co_ref[1]], axis=0)
    both = lambda x, y: jnp.concatenate([x[...], y[...]], axis=0)
    gu_ref[0] = dot(h, both(dg0, dg1), TN).astype(BF)
    gu_ref[1] = dot(h, both(du0, du1), TN).astype(BF)
    d_ref[...] = dot(ct, both(a0, a1), TN).astype(BF)


def feed_grad(r, sc, h_own, h_sib, ct_own, ct_sib, first, second):
    _, owned, width = h_own.shape
    units = first[0].shape[1]
    part = width // 4
    cut = 2
    lanes = pl.BlockSpec((2, owned, part), lambda n, sc: (0, 0, sc[1] ^ r))
    right = pl.BlockSpec((2 * owned, units // cut), lambda n, sc: (0, n))
    return pl.pallas_call(
        feed_grad_kernel,
        grid_spec=pltpu.PrefetchScalarGridSpec(
            num_scalar_prefetch=1,
            grid=(cut,),
            in_specs=[lanes] * 4 + [right] * 6,
            out_specs=[
                pl.BlockSpec((2, part, units // cut), lambda n, sc: (0, 0, n)),
                pl.BlockSpec((part, units // cut), lambda n, sc: (0, n)),
            ],
        ),
        out_shape=[shape((2, part, units), BF), shape((part, units), BF)],
        compiler_params=params(40),
        cost_estimate=cost(24 * owned * part * units, 12 * MIB),
    )(sc, h_own, h_sib, ct_own, ct_sib, *first, *second)


def norm_back(dn, v, gain):
    r = lax.rsqrt(jnp.mean(v * v, axis=-1, keepdims=True) + EPSILON)
    scaled = gain * dn
    gain_grad = jnp.sum(dn * (v * r), axis=0, keepdims=True)
    return r * scaled - v * (r * r * r) * jnp.mean(scaled * v, axis=-1, keepdims=True), gain_grad


def turn_back_kernel(
    sc_ref, a_ref, b_ref, z_ref, x2_ref, ct_ref, g_ref, w_ref, dx_ref, db_ref, do_ref, gain_ref
):
    dn = a_ref[0].astype(F32) + b_ref[...].astype(F32) + z_ref[...].astype(F32)
    dv, gain_grad = norm_back(dn, x2_ref[0], g_ref[...])
    gain_ref[...] = gain_grad
    dx = ct_ref[...].astype(F32) + dv
    dx_ref[...] = dx
    low = dx.astype(BF)
    db_ref[...] = low
    for k in range(w_ref.shape[0]):
        do_ref[k] = dot(low, w_ref[k], NT).astype(BF)


def turn_back(sc, mine, core, tp, x2, cotangent, gain, weight):
    owned, width = cotangent.shape
    ways, local, _ = weight.shape
    whole = lambda *dims: pl.BlockSpec(dims, lambda n, sc: (0,) * len(dims))
    own = pl.BlockSpec((1, owned, width), lambda n, sc: (1, 0, 0))
    return pl.pallas_call(
        turn_back_kernel,
        grid_spec=pltpu.PrefetchScalarGridSpec(
            num_scalar_prefetch=1,
            grid=(1,),
            in_specs=[
                own,
                whole(owned, width),
                whole(owned, width),
                own,
                whole(owned, width),
                whole(1, width),
                whole(ways, local, width),
            ],
            out_specs=[
                whole(owned, width),
                whole(owned, width),
                whole(ways, owned, local),
                whole(1, width),
            ],
        ),
        out_shape=[
            shape((owned, width), F32),
            shape((owned, width), BF),
            shape((ways, owned, local), BF),
            shape((1, width), F32),
        ],
        compiler_params=params(40),
        cost_estimate=cost(2 * owned * width * ways * local, 12 * MIB),
    )(sc, mine, core, tp, x2, cotangent, gain.reshape(1, width), weight)


def pair_grad_kernel(kvheads, own_ref, back_ref, c_ref, s_ref, out_ref):
    total = own_ref[...] + back_ref[...].astype(F32)
    cosine, sine = c_ref[...], s_ref[...]
    parts = []
    for n in range(kvheads):
        a = total[:, n * HEAD_DIM : n * HEAD_DIM + HALF]
        b = total[:, n * HEAD_DIM + HALF : (n + 1) * HEAD_DIM]
        parts += [a * cosine + b * sine, b * cosine - a * sine]
    parts.append(total[:, kvheads * HEAD_DIM :])
    out_ref[...] = jnp.concatenate(parts, axis=1).astype(BF)


def pair_grad(own, back, cosine, sine, kvheads):
    rows, wide = own.shape
    row = lambda n: pl.BlockSpec((TILE, n), lambda t: (t, 0))
    return pl.pallas_call(
        lambda *refs: pair_grad_kernel(kvheads, *refs),
        grid=(rows // TILE,),
        in_specs=[row(wide), row(wide), row(HALF), row(HALF)],
        out_specs=row(wide),
        out_shape=shape((rows, wide), BF),
        cost_estimate=cost(MIB, 4 * MIB),
    )(own, back, cosine, sine)


def finish_kernel(
    sc_ref, q0, q1, q2, q3, k0, k1, k2, k3, w_ref, x_ref, g_ref, dx_ref, out_ref, gain_ref, acc
):
    d = pl.program_id(0)

    def chosen(first, rest):
        value = first[0]
        for n, ref in enumerate(rest):
            value = jnp.where(d == n + 1, ref[...], value)
        return value

    left = jnp.concatenate([chosen(q0, (q1, q2, q3)), chosen(k0, (k1, k2, k3))], axis=1)
    term = dot(left, w_ref[0], NT)

    @pl.when(d == 0)
    def _():
        acc[...] = term

    @pl.when(d > 0)
    def _():
        acc[...] += term

    @pl.when(d == pl.num_programs(0) - 1)
    def _():
        dv, gain_grad = norm_back(acc[...], x_ref[...].astype(F32), g_ref[...])
        out_ref[...] = dx_ref[...] + dv
        gain_ref[...] = gain_grad


def finish(sc, query_parts, pair_parts, weight, tokens, gain, dx):
    owned, width = tokens.shape
    ways, _, wide = weight.shape
    local = query_parts[1].shape[1]
    whole = lambda *dims: pl.BlockSpec(dims, lambda d, sc: (0,) * len(dims))
    own = pl.BlockSpec((1, owned, local), lambda d, sc: (sc[0], 0, 0))
    return pl.pallas_call(
        finish_kernel,
        grid_spec=pltpu.PrefetchScalarGridSpec(
            num_scalar_prefetch=1,
            grid=(ways,),
            in_specs=[
                own, whole(owned, local), whole(owned, local), whole(owned, local),
                own, whole(owned, local), whole(owned, local), whole(owned, local),
                pl.BlockSpec((1, width, wide), lambda d, sc: (sc[0] ^ d, 0, 0)),
                whole(owned, width),
                whole(1, width),
                whole(owned, width),
            ],
            out_specs=[whole(owned, width), whole(1, width)],
            scratch_shapes=[pltpu.VMEM((owned, width), F32)],
        ),
        out_shape=[shape((owned, width), F32), shape((1, width), F32)],
        compiler_params=params(32),
        cost_estimate=cost(2 * owned * width * wide * ways, 14 * MIB),
    )(sc, *query_parts, *pair_parts, weight, tokens, gain.reshape(1, width), dx)


def halve(blocks, bits, group):
    for at, bit in enumerate(bits):
        kept = {}
        for r, block in blocks.items():
            if r & bit:
                continue
            came = send(blocks[r | bit].astype(BF), lambda s, t: (s ^ (bit * group), t))
            kept[r] = block.astype(F32) + came.astype(F32)
        blocks = kept
    return blocks[0]


def take(a, index, axis=0):
    return lax.dynamic_index_in_dim(a, index, axis, keepdims=False)


def across(pieces, j, ways, first=None):
    out = []
    for d in range(1, ways):
        out.append(send(take(pieces, j ^ d), lambda s, t: (s, t ^ d)))
    return out


def middle_scatter(a, axis, size, group):
    middle = group // 2
    if middle == 1:
        return a
    groups = [
        [g * group + 2 * m + c for m in range(middle)] for g in range(size // group) for c in (0, 1)
    ]
    return lax.psum_scatter(
        a, "seq", scatter_dimension=axis, tiled=True, axis_index_groups=groups
    )


def gain_sum(part):
    devices = lax.axis_size("seq") * lax.axis_size("tp")
    parts = lax.all_to_all(
        part.reshape(devices, -1), AXES, split_axis=0, concat_axis=0, tiled=True
    )
    return jnp.sum(parts, axis=0)


def body(
    tokens, lengths, first_gain, w_query, w_keyval, w_output, second_gain, w_gateup, w_down,
    cotangent,
):
    size, ways = lax.axis_size("seq"), lax.axis_size("tp")
    owned, width = tokens.shape
    rows = owned * ways
    local = w_query.shape[1]
    qheads = local // HEAD_DIM
    kvheads = w_keyval.shape[2] // HEAD_DIM
    units = w_down.shape[0]
    span = units // 4
    group = size // 4
    i, j = lax.axis_index("seq"), lax.axis_index("tp")
    odd = i & 1
    place = i // group
    sc = jnp.stack([j, place, odd]).astype(jnp.int32)
    sibling = lambda s, t: (s ^ 1, t)
    partner = lambda s, t: (s, t ^ 1)

    right, left = [tokens], [tokens]
    for _ in range(ways - 1):
        right.append(send(right[-1], lambda s, t: (s, t + 1)))
        left.append(send(left[-1], lambda s, t: (s, t - 1)))

    start_id = i * rows
    query_ids = start_id + jnp.arange(rows, dtype=jnp.int32)
    begins = doc_places(lengths, query_ids)
    cosine, sine = rotation_tables(query_ids - begins)
    lo = jnp.maximum(query_ids - (WINDOW - 1), begins) - (start_id - rows)
    lo = lo.reshape(1, rows)
    weight_one = jnp.concatenate(
        [spread_halves(w_query), spread_halves(w_keyval[:, 0]), w_keyval[:, 1]], axis=1
    )
    shares = lambda w: lax.dynamic_slice_in_dim(w, i * (w.shape[0] // size), w.shape[0] // size, 0)
    gathered = lambda w: lax.all_gather(shares(w), ("tp", "seq"), axis=0, tiled=True)
    output_all = gathered(w_output).reshape(ways, local, width)
    gateup_own = jnp.transpose(w_gateup, (1, 0, 2))
    piece = lax.dynamic_slice_in_dim(gateup_own, place * span, span, 2)
    far = lambda s, t: (s, t ^ 2) if s & 1 else None
    hop = lambda bit: lambda s, t: (s ^ (bit * group), t) if s & 1 else None
    g0 = send(piece, far)
    g1, g2 = send(g0, hop(1)), send(g0, hop(2))
    g3 = send(g1, hop(2))
    d0 = send(lax.dynamic_slice_in_dim(w_down, place * span, span, 0), far)
    d1, d2 = send(d0, hop(1)), send(d0, hop(2))
    d3 = send(d2, hop(1))
    ct_own = jnp.stack([send(cotangent, partner), cotangent])
    ct_sib = send(ct_own, sibling)

    inputs_one, queries, pair_here = project(
        sc, right[:1] + right[1:] + left[1:], first_gain, weight_one,
        *lane_tables(cosine, sine), qheads, kvheads,
    )
    pair_before = send(pair_here, lambda s, t: (s + 1, t))
    heads_out, logs = attend(queries, pair_before, pair_here, lo, kvheads)

    near_rows = lambda half: lax.dynamic_slice_in_dim(heads_out, half * 2 * owned, 2 * owned, 0)
    from_far = send(near_rows((j >> 1) ^ 1), lambda s, t: (s, t ^ 2))
    from_near = send(near_rows(j >> 1), partner)
    from_last = send(from_far, partner)
    x2, h_own, heads_rows = mix(
        sc, heads_out, (from_near, from_far, from_last), output_all, tokens, right[1], left[1],
        second_gain,
    )
    h_sib = send(h_own, sibling)

    fed = lambda m: feed(
        m, sc, h_own, h_sib, ct_own, ct_sib, gateup_own, w_down, (g0, g1, g2, g3), (d0, d1, d2, d3)
    )
    a0, dg0, du0, y0, dh0 = fed(0)
    a1, dg1, du1, y1, dh1 = fed(1)

    def to_partner(first):
        came = send(first[0], sibling)
        return send((first[1].astype(F32) + came.astype(F32)).astype(BF), partner)

    dh_z = to_partner(dh0)
    dh_core = send(dh1[0], sibling)
    dx2, low, heads_grad, second_part = turn_back(
        sc, dh1, dh_core, dh_z, x2, cotangent, second_gain, output_all
    )
    grad_parts = [heads_grad] + across(heads_grad, j, ways)
    y_z = to_partner(y0)
    y_core = send(y1[0], sibling)
    result = (x2[1] + (y1[1].astype(F32) + y_core.astype(F32) + y_z.astype(F32))).astype(BF)

    blocks = {}
    for r in (3, 1, 2, 0):
        blocks[r] = feed_grad(
            r, sc, h_own, h_sib, ct_own, ct_sib, (a0, dg0, du0), (a1, dg1, du1)
        )
    gateup_block = halve({r: b[0] for r, b in blocks.items()}, (1, 2), group)
    down_block = halve({r: b[1] for r, b in blocks.items()}, (2, 1), group)

    def own_share(block, axis):
        block = middle_scatter(block, axis, size, group)
        half = block.shape[axis] // 2
        low_block = block.astype(BF)
        cut = lambda a, k: lax.dynamic_slice_in_dim(a, k * half, half, axis)
        crossed = send(cut(low_block, 1 - odd), lambda s, t: (s ^ 1, t ^ 2) if s & 1 else (s ^ 1, t))
        second = send(cut(low_block, 1), far).astype(F32)
        mine = lax.slice_in_dim(block, 0, half, axis=axis)
        return jnp.where(odd == 0, mine, second) + crossed.astype(F32)

    gateup_grad = jnp.transpose(own_share(gateup_block, 1), (1, 0, 2))
    down_grad = jnp.transpose(own_share(down_block, 0))

    share = width // size
    by_core = lambda a: a.reshape(-1, size // 2, 2, share)
    low_parts = by_core(low)
    low_mine = take(low_parts, odd, 2).reshape(owned, -1)
    low_came = send(take(low_parts, 1 - odd, 2).reshape(owned, -1), sibling)
    heads_sib = send(heads_rows, sibling)
    out_grad = dot(
        jnp.concatenate([low_mine, low_came], axis=0),
        jnp.concatenate([heads_rows, heads_sib], axis=0),
        TN,
    ).astype(BF)
    out_grad = out_grad.reshape(4, -1, ways * local)
    cut = ways * local // 2
    relative = lambda a: {r: take(a, place ^ r) for r in range(4)}
    out_block = jnp.concatenate(
        [
            halve(relative(out_grad[..., :cut]), (1, 2), group),
            halve(relative(out_grad[..., cut:]), (2, 1), group),
        ],
        axis=1,
    )
    out_block = middle_scatter(out_block, 0, size, group)
    out_share = out_block[:, :local]
    for d in range(1, ways):
        came = send(
            out_block[:, d * local : (d + 1) * local].astype(BF), lambda s, t: (s, t ^ d)
        )
        out_share = out_share + came.astype(F32)
    output_grad = jnp.transpose(out_share)

    dq, dpair_before, dpair_here = attend_back(
        sc, queries, pair_before, pair_here, lo, heads_out, logs, grad_parts,
        (jnp.transpose(cosine), jnp.transpose(sine)), kvheads,
    )
    returned = send(dpair_before, lambda s, t: (s - 1, t))
    dpair = pair_grad(dpair_here, returned, cosine, sine, kvheads)
    query_rows = dq.reshape(ways, owned, local)
    pair_rows = dpair.reshape(ways, owned, local)
    query_parts = [query_rows] + across(query_rows, j, ways)
    pair_parts = [pair_rows] + across(pair_rows, j, ways)
    weight_flat = jnp.concatenate([w_query, w_keyval.reshape(width, -1)], axis=1)
    weight_all = gathered(weight_flat).reshape(ways, width, 2 * local)
    tokens_grad, first_part = finish(
        sc, query_parts, pair_parts, weight_all, tokens, first_gain, dx2
    )

    def summed(grads, bits):
        full = dot(inputs_one, grads, TN).astype(BF).reshape(4, -1, 2, share, local)
        came = send(take(full, 1 - odd, 2), sibling)
        kept = (take(full, odd, 2).astype(F32) + came.astype(F32)).astype(BF)
        block = halve(relative(kept), bits, group)
        return middle_scatter(block.reshape(-1, local), 0, size, group)

    query_grad = summed(dq, (1, 2))
    keyval_grad = summed(dpair, (2, 1)).reshape(share, 2, -1)
    return (
        result, tokens_grad, gain_sum(first_part), query_grad, keyval_grad, output_grad,
        gain_sum(second_part), gateup_grad, down_grad,
    )


def solution(mesh):
    return jax.shard_map(
        body,
        mesh=mesh,
        in_specs=(
            P(AXES, None), P(), P(), P(None, "tp"), P(None, None, "tp"), P("tp", None), P(),
            P(None, None, "tp"), P("tp", None), P(AXES, None),
        ),
        out_specs=(
            P(AXES, None), P(AXES, None), P(AXES), P("seq", "tp"), P("seq", None, "tp"),
            P("tp", "seq"), P(AXES), P("seq", None, "tp"), P("tp", "seq"),
        ),
        check_vma=False,
    )
```

time: 851 us -> 639 us (0.75)
  waiting for transfers between devices: 547 us -> 136 us
  starting transfers between devices: 5.49 us -> 215 us
  Pallas kernels: 41.7 us -> 122 us
  matrix products: 80.9 us -> 8.54 us
  blocking collectives: 45 us -> 0 us
  local copies, waits for them, and re-layouts: 74.7 us -> 90.4 us
    reduce_scatter x7 -> x0, waiting for transfers between devices: 283 us -> none  [the longest x3 76.9 us: body(): lax.psum_scatter(a, axis, scatter_dimension=dim, tiled=True)]
    all_gather x4 -> x2, waiting for transfers between devices: 184 us -> 0.01 us  [body(): lax.all_gather(shares(w), ('tp', 'seq'), axis=0, tiled=True)]
    ppermute x2 -> x66, starting transfers between devices: 3.96 us -> 185 us  [send(): return lax.ppermute(a, AXES, pairs)]
    ppermute x2 -> x66, waiting for transfers between devices: 2.09 us -> 133 us  [send(): return lax.ppermute(a, AXES, pairs)]
    pallas_call x3 -> x13, Pallas kernels: 41.7 us -> 122 us  [the longest x2 35.2 us: feed(): pl.pallas_call(feed_kernel, grid_spec=pltpu.PrefetchScalarGridSpec(num_sc...]
    unnamed x15 -> x2, waiting for transfers between devices: 78.1 us -> 0.03 us
    dot_general x11 -> x3, matrix products: 80.9 us -> 8.54 us  [dot(): return lax.dot_general(a, b, dims, preferred_element_type=F32)]
    unnamed x1 -> x0, blocking collectives: 45 us -> none
  transfers between devices with their start and end apart: 15 -> 70, of which waited for: 14 -> 17; matrix products, arithmetic and copies ran while one was open for 16% -> 16% of each run, Pallas kernels for 3% -> 19%
where the time goes in v2:
time: 639 us; the launch traced here: 628 us
  starting transfers between devices  215 us (34%)
  waiting for transfers between devices  136 us (21%)
  Pallas kernels  122 us (19%)
  local copies, waits for them, and re-layouts  90.4 us (14%)
  other arithmetic  41 us (6%)
  between operations  15.6 us (2%)
  matrix products  8.54 us (1%)
    ppermute x66, starting transfers between devices, send(): return lax.ppermute(a, AXES, pairs)  185 us
    ppermute x66, waiting for transfers between devices, send(): return lax.ppermute(a, AXES, pairs)  133 us
    unnamed x172, local copies, waits for them, and re-layouts  49.6 us
    pallas_call x2, Pallas kernels, feed(): pl.pallas_call(feed_kernel, grid_spec=pltpu.PrefetchScalarGridSpec(num_sc...  35.2 us
    all_to_all x2, starting transfers between devices, gain_sum(): lax.all_to_all(part.reshape(devices, -1), AXES, split_axis=0, concat_axis...  29.7 us
    pallas_call x1, Pallas kernels, attend_back(): pl.pallas_call(lambda *refs: attend_back_kernel(kvheads, *refs), grid_spe...  23.1 us
    pallas_call x4, Pallas kernels, feed_grad(): pl.pallas_call(feed_grad_kernel, grid_spec=pltpu.PrefetchScalarGridSpec(n...  21 us
    pallas_call x1, Pallas kernels, attend(): pl.pallas_call(lambda *refs: attend_kernel(kvheads, *refs), grid=(kvheads...  13.1 us
  transfers between devices with their start and end apart: 70, of which 17 were waited for; matrix products, arithmetic and copies ran while one was open for 16% of the time, Pallas kernels for 19%

profile of v2, /device:TPU:0, one launch (start us, length us, event | category | flops | bytes accessed | tf_op | source)
XLA Modules:
  0.0 627.9 jit_solution(2885362377377469252)
XLA Ops:
  9.2 5.0 collective-permute-start
  15.5 7.4 %copy.68 = bf16[1536,2,1024]{2,0,1:T(8,128)(2,1)} copy(bf16[1536,2,1024]{2,1,0:T(2,128)(2,1)} %param.17) | data formatting | bytes 12582912 | tf_op args[7]
  27.7 7.9 %collective-permute-done.refs_2_.xr_ref = bf16[256,1536]{1,0:T(8,128)(2,1)S(1)} collective-permute-done((bf16[256,1536]{1,0:T(8,128)(2,1)}, bf16[256,1536]{1,0:T(8,128)(2,1)S(1)}, u32[]{:S(2)}, u32[]{:S(2)}) %collective-permute-start) | collective-permute-done | bytes 786464 | tf_op jit(solution)/shard_map/ppermute | solution.py:52
  35.5 22.9 %collective-permute-start.1 = (bf16[256,1536]{1,0:T(8,128)(2,1)S(1)}, bf16[256,1536]{1,0:T(8,128)(2,1)S(1)}, u32[]{:S(2)}, u32[]{:S(2)}) collective-permute-start(bf16[256,1536]{1,0:T(8,128)(2,1)S(1)} %collective-permute-done.refs_2_.xr_ref), channel_id=1, source_target_pairs={{0,1},{1,2},{2,3},{4,5},{5,6},{6,7},{8,9},{9,10},{10,11},{12,13},{... | collective-permute-start | bytes 2359304 | tf_op jit(solution)/shard_map/ppermute | solution.py:52
  62.1 13.9 %collective-permute-done.1.refs_3_ = bf16[256,1536]{1,0:T(8,128)(2,1)S(1)} collective-permute-done((bf16[256,1536]{1,0:T(8,128)(2,1)S(1)}, bf16[256,1536]{1,0:T(8,128)(2,1)S(1)}, u32[]{:S(2)}, u32[]{:S(2)}) %collective-permute-start.1) | collective-permute-done | bytes 786464 | tf_op jit(solution)/shard_map/ppermute | solution.py:52
  76.0 18.6 %collective-permute-start.2 = (bf16[256,1536]{1,0:T(8,128)(2,1)S(1)}, bf16[256,1536]{1,0:T(8,128)(2,1)}, u32[]{:S(2)}, u32[]{:S(2)}) collective-permute-start(bf16[256,1536]{1,0:T(8,128)(2,1)S(1)} %collective-permute-done.1.refs_3_), channel_id=1, source_target_pairs={{0,1},{1,2},{2,3},{4,5},{5,6},{6,7},{8,9},{9,10},{10,11},{12,13},{... | collective-permute-start | bytes 2359304 | tf_op jit(solution)/shard_map/ppermute | solution.py:52
  119.7 6.9 %shard_map.169 = (bf16[1024,1536]{1,0:T(8,128)(2,1)S(1)}, bf16[1024,512]{1,0:T(8,128)(2,1)S(1)}, bf16[1024,384]{1,0:T(8,128)(2,1)S(1)}) custom-call(s32[3]{0:T(128)S(1)} %pad_add_fusion.refs_0_.sc_ref, bf16[256,1536]{1,0:T(8,128)(2,1)S(1)} %copy-done.19, bf16[256,1536]{1,0:T(8,128)(2,1)S(1)} %collective-permute-done.refs_2_.xr_ref, ...), custom_call_target="tpu_custom_call" | custom-call | flops 3019898880 | bytes 6291456 | tf_op jit(solution)/shard_map/pallas_call | solution.py:140
  129.3 22.0 %collective-permute-start.6 = (bf16[1024,384]{1,0:T(8,128)(2,1)S(1)}, bf16[1024,384]{1,0:T(8,128)(2,1)S(1)}, u32[]{:S(2)}, u32[]{:S(2)}) collective-permute-start(bf16[1024,384]{1,0:T(8,128)(2,1)S(1)} %get-tuple-element.45.refs_2_.refs_3_), channel_id=1, source_target_pairs={{0,4},{1,5},{2,6},{3,7},{4,8},{5,9},{6,10},{7,11},{8,12},{9,13},{1... | collective-permute-start | bytes 2359304 | tf_op jit(solution)/shard_map/ppermute | solution.py:52
  160.8 13.1 %shard_map.170 = (bf16[1024,384]{1,0:T(8,128)(2,1)S(1)}, f32[2,4,1,512]{3,2,1,0:T(1,128)S(1)}) custom-call(bf16[1024,512]{1,0:T(8,128)(2,1)S(1)} %copy-done.57, bf16[1024,384]{1,0:T(8,128)(2,1)S(1)} %collective-permute-done.6.refs_1_.refs_2_, bf16[1024,384]{1,0:T(8,128)(2,1)S(1)} %get-tuple-element.45.refs_2_.refs_3_, ...), custom_call_target="tpu_custom_call" | custom-call | flops 6710886400 | bytes 5242880 | tf_op jit(solution)/shard_map/pallas_call | solution.py:235
  180.5 18.9 %collective-permute-done.8.o2_ref = bf16[512,384]{1,0:T(8,128)(2,1)S(1)} collective-permute-done((bf16[512,384]{1,0:T(8,128)(2,1)S(1)}, bf16[512,384]{1,0:T(8,128)(2,1)S(1)}, u32[]{:S(2)}, u32[]{:S(2)}) %collective-permute-start.8) | collective-permute-done | bytes 393248 | tf_op jit(solution)/shard_map/ppermute | solution.py:52
  221.9 5.5 shard_map.171
  235.6 17.7 %shard_map.173 = (bf16[512,1024]{1,0:T(8,128)(2,1)S(1)}, bf16[512,1024]{1,0:T(8,128)(2,1)S(1)}, bf16[512,1024]{1,0:T(8,128)(2,1)}, bf16[2,256,1536]{2,1,0:T(8,128)(2,1)}, bf16[2,256,1536]{2,1,0:T(8,128)(2,1)}) custom-call(s32[3]{0:T(128)S(1)} %pad_add_fusion.refs_0_.sc_ref, bf16[2,256,1536]{2,1,0:T(8,128)(2,1)} %copy-done.4, ...), custom_call_target="tpu_custom_call" | custom-call | flops 14495514624 | bytes 23068672 | tf_op jit(solution)/shard_map/pallas_call | solution.py:500
  255.4 15.9 %collective-permute-start.22 = (bf16[256,1536]{1,0:T(8,128)(2,1)}, bf16[256,1536]{1,0:T(8,128)(2,1)}, u32[]{:S(2)}, u32[]{:S(2)}) collective-permute-start(bf16[256,1536]{1,0:T(8,128)(2,1)} %slice_bitcast_fusion.2), channel_id=1, source_target_pairs={{0,4},{1,5},{2,6},{3,7},{4,0},{5,1},{6,2},{7,3},{8,12},{9,13},{10,... | collective-permute-start | bytes 2359304 | tf_op jit(solution)/shard_map/ppermute | solution.py:52
  271.3 17.6 %shard_map.172 = (bf16[512,1024]{1,0:T(8,128)(2,1)S(1)}, bf16[512,1024]{1,0:T(8,128)(2,1)S(1)}, bf16[512,1024]{1,0:T(8,128)(2,1)}, bf16[2,256,1536]{2,1,0:T(8,128)(2,1)}, bf16[2,256,1536]{2,1,0:T(8,128)(2,1)}) custom-call(s32[3]{0:T(128)S(1)} %pad_add_fusion.refs_0_.sc_ref, bf16[2,256,1536]{2,1,0:T(8,128)(2,1)} %copy-done.4, ...), custom_call_target="tpu_custom_call" | custom-call | flops 14495514624 | bytes 23068672 | tf_op jit(solution)/shard_map/pallas_call | solution.py:500
  295.8 5.0 shard_map.181
  304.0 5.7 shard_map.180
  309.7 5.0 shard_map.179
  314.8 5.2 shard_map.178
  329.5 8.5 %collective-permute-done.57 = bf16[2,384,1024]{2,1,0:T(8,128)(2,1)S(1)} collective-permute-done((bf16[2,384,1024]{2,1,0:T(8,128)(2,1)S(1)}, bf16[2,384,1024]{2,1,0:T(8,128)(2,1)S(1)}, u32[]{:S(2)}, u32[]{:S(2)}) %collective-permute-start.57) | collective-permute-done | bytes 1572896 | tf_op jit(solution)/shard_map/ppermute | solution.py:52
  343.0 5.5 shard_map.174
  374.8 7.3 %collective-permute-done.28.refs_9_ = bf16[256,384]{1,0:T(8,128)(2,1)} collective-permute-done((bf16[256,384]{1,0:T(8,128)(2,1)}, bf16[256,384]{1,0:T(8,128)(2,1)}, u32[]{:S(2)}, u32[]{:S(2)}) %collective-permute-start.28) | collective-permute-done | bytes 196640 | tf_op jit(solution)/shard_map/ppermute | solution.py:52
  385.9 23.1 %shard_map.175 = (bf16[1024,384]{1,0:T(8,128)(2,1)S(1)}, bf16[1024,384]{1,0:T(8,128)(2,1)S(1)}, f32[1024,384]{1,0:T(8,128)S(1)}) custom-call(s32[3]{0:T(128)S(1)} %pad_add_fusion.refs_0_.sc_ref, bf16[1024,512]{1,0:T(8,128)(2,1)S(1)} %copy-done.58, bf16[1024,384]{1,0:T(8,128)(2,1)S(1)} %copy-done.49, bf16[1024,384]{1,0:T(8,128)(2,1)S(1)} %copy-done.47, ...), custom_call_target="tpu_custom_call" | custom-call | flops 16777216000 | bytes 8388608 | tf_op jit(solution)/shard_map/pallas_call | solution.py:334
  411.8 4.9 collective-permute-start.37
  420.4 4.8 collective-permute-start.48
  435.9 32.7 %collective-permute-done.52 = bf16[192,768]{1,0:T(8,128)(2,1)S(1)} collective-permute-done((bf16[192,768]{1,0:T(8,128)(2,1)S(1)}, bf16[192,768]{1,0:T(8,128)(2,1)S(1)}, u32[]{:S(2)}, u32[]{:S(2)}) %collective-permute-start.52) | collective-permute-done | bytes 294944 | tf_op jit(solution)/shard_map/ppermute | solution.py:52
  468.6 8.7 %collective-permute-start.39 = (bf16[1,192,384]{2,1,0:T(8,128)(2,1)S(1)}, bf16[1,192,384]{2,1,0:T(8,128)(2,1)S(1)}, u32[]{:S(2)}, u32[]{:S(2)}) collective-permute-start(bf16[1,192,384]{2,1,0:T(8,128)(2,1)S(1)} %get-tuple-element.149), channel_id=1, source_target_pairs={{0,8},{1,9},{2,10},{3,11},{4,12},{5,13},{6,14},{7,15},{8,0},{9,1},... | collective-permute-start | bytes 442376 | tf_op jit(solution)/shard_map/ppermute | solution.py:52
  483.2 5.0 shard_map.176
  515.7 4.7 fusion.33
  524.4 8.5 %collective-permute-start.32 = (bf16[256,384]{1,0:T(8,128)(2,1)S(1)}, bf16[256,384]{1,0:T(8,128)(2,1)S(1)}, u32[]{:S(2)}, u32[]{:S(2)}) collective-permute-start(bf16[256,384]{1,0:T(8,128)(2,1)S(1)} %copy-done.76), channel_id=1, source_target_pairs={{0,3},{1,2},{2,1},{3,0},{4,7},{5,6},{6,5},{7,4},{8,11},{9,10},{10,... | collective-permute-start | bytes 589832 | tf_op jit(solution)/shard_map/ppermute | solution.py:52
  532.9 21.3 %collective-permute-done.54 = bf16[192,384]{1,0:T(8,128)(2,1)S(1)} collective-permute-done((bf16[192,384]{1,0:T(8,128)(2,1)S(1)}, bf16[192,384]{1,0:T(8,128)(2,1)S(1)}, u32[]{:S(2)}, u32[]{:S(2)}) %collective-permute-start.54) | collective-permute-done | bytes 147488 | tf_op jit(solution)/shard_map/ppermute | solution.py:52
  578.3 6.4 %shard_map.177 = (f32[256,1536]{1,0:T(8,128)}, f32[1,1536]{1,0:T(1,128)S(1)}) custom-call(s32[3]{0:T(128)S(1)} %pad_add_fusion.refs_0_.sc_ref, bf16[4,256,384]{2,1,0:T(8,128)(2,1)S(1)} %bitcast.139, bf16[256,384]{1,0:T(8,128)(2,1)S(1)} %collective-permute-done.30.q1, bf16[256,384]{1,0:T(8,128)(2,1)S(1)} %collective-permute-done.31.q2, ...), custom_call_target="tpu_custom_call" | custom-call | flops 2415919104 | bytes 14680064 | tf_op jit(solution)/shard_map/pallas_call | solution.py:674
  586.7 26.2 %all-to-all-start = ((f32[32,1,48]{2,1,0:T(1,128)}), f32[32,1,48]{2,1,0:T(1,128)S(1)}, u32[]{:S(2)}, u32[]{:S(2)}) async-start(f32[32,1,48]{2,1,0:T(1,128)} %bitcast.37), calls=%async_computation | async-start | bytes 32768 | tf_op jit(solution)/shard_map/all_to_all | solution.py:733
  (372 shorter events, 230.6 us)
Async XLA Ops:
  7.2 205.8 %all-gather.3.cloned.1.call-start = ((), (), s32[]{:S(2)}) async-start(), calls=%async_computation.2 | async-start | bytes 4866048 | tf_op jit(solution)/shard_map/all_gather | solution.py:774
  9.1 564.1 %all-gather.5.cloned.1.call-start = ((), (), s32[]{:S(2)}) async-start(), calls=%async_computation.3 | async-start | bytes 9732096 | tf_op jit(solution)/shard_map/all_gather | solution.py:774
  14.2 44.2 %collective-permute-start.3 = (bf16[256,1536]{1,0:T(8,128)(2,1)}, bf16[256,1536]{1,0:T(8,128)(2,1)S(1)}, u32[]{:S(2)}, u32[]{:S(2)}) collective-permute-start(bf16[256,1536]{1,0:T(8,128)(2,1)} %x_ref.3), channel_id=1, source_target_pairs={{1,0},{2,1},{3,2},{5,4},{6,5},{7,6},{9,8},{10,9},{11,10},{13,12},{... | collective-permute-start | bytes 2359304 | tf_op jit(solution)/shard_map/ppermute | solution.py:52
  25.6 131.8 %collective-permute-start.13 = (bf16[2,1536,256]{2,1,0:T(8,128)(2,1)}, bf16[2,1536,256]{2,1,0:T(8,128)(2,1)}, u32[]{:S(2)}, u32[]{:S(2)}) collective-permute-start(bf16[2,1536,256]{2,1,0:T(8,128)(2,1)} %dynamic-slice_bitcast_fusion), channel_id=1, source_target_pairs={{4,6},{5,7},{6,4},{7,5},{12,14},{13,15},{14,12},{15,13},{20,22},{2... | collective-permute-start | bytes 4718600 | tf_op jit(solution)/shard_map/ppermute | solution.py:52
  35.5 40.5 %collective-permute-start.1 = (bf16[256,1536]{1,0:T(8,128)(2,1)S(1)}, bf16[256,1536]{1,0:T(8,128)(2,1)S(1)}, u32[]{:S(2)}, u32[]{:S(2)}) collective-permute-start(bf16[256,1536]{1,0:T(8,128)(2,1)S(1)} %collective-permute-done.refs_2_.xr_ref), channel_id=1, source_target_pairs={{0,1},{1,2},{2,3},{4,5},{5,6},{6,7},{8,9},{9,10},{10,11},{12,13},{... | collective-permute-start | bytes 2359304 | tf_op jit(solution)/shard_map/ppermute | solution.py:52
  58.4 37.3 %collective-permute-start.4 = (bf16[256,1536]{1,0:T(8,128)(2,1)S(1)}, bf16[256,1536]{1,0:T(8,128)(2,1)S(1)}, u32[]{:S(2)}, u32[]{:S(2)}) collective-permute-start(bf16[256,1536]{1,0:T(8,128)(2,1)S(1)} %collective-permute-done.3.refs_5_.xl_ref), channel_id=1, source_target_pairs={{1,0},{2,1},{3,2},{5,4},{6,5},{7,6},{9,8},{10,9},{11,10},{13,12},{... | collective-permute-start | bytes 2359304 | tf_op jit(solution)/shard_map/ppermute | solution.py:52
  76.0 42.6 %collective-permute-start.2 = (bf16[256,1536]{1,0:T(8,128)(2,1)S(1)}, bf16[256,1536]{1,0:T(8,128)(2,1)}, u32[]{:S(2)}, u32[]{:S(2)}) collective-permute-start(bf16[256,1536]{1,0:T(8,128)(2,1)S(1)} %collective-permute-done.1.refs_3_), channel_id=1, source_target_pairs={{0,1},{1,2},{2,3},{4,5},{5,6},{6,7},{8,9},{9,10},{10,11},{12,13},{... | collective-permute-start | bytes 2359304 | tf_op jit(solution)/shard_map/ppermute | solution.py:52
  151.3 49.6 %collective-permute-start.11 = (bf16[256,1536]{1,0:T(8,128)(2,1)S(1)}, bf16[256,1536]{1,0:T(8,128)(2,1)}, u32[]{:S(2)}, u32[]{:S(2)}) collective-permute-start(bf16[256,1536]{1,0:T(8,128)(2,1)S(1)} %copy-done.14), channel_id=1, source_target_pairs={{0,1},{1,0},{2,3},{3,2},{4,5},{5,4},{6,7},{7,6},{8,9},{9,8},{10,11... | collective-permute-start | bytes 2359304 | tf_op jit(solution)/shard_map/ppermute | solution.py:52
  157.4 44.9 %collective-permute-start.14 = (bf16[2,1536,256]{2,1,0:T(8,128)(2,1)}, bf16[2,1536,256]{2,1,0:T(8,128)(2,1)}, u32[]{:S(2)}, u32[]{:S(2)}) collective-permute-start(bf16[2,1536,256]{2,1,0:T(8,128)(2,1)} %collective-permute-done.13.gu0), channel_id=1, source_target_pairs={{4,12},{5,13},{6,14},{7,15},{12,4},{13,5},{14,6},{15,7},{20,28},{2... | collective-permute-start | bytes 4718600 | tf_op jit(solution)/shard_map/ppermute | solution.py:52
  178.9 50.1 %collective-permute-start.18 = (bf16[256,1536]{1,0:T(8,128)(2,1)}, bf16[256,1536]{1,0:T(8,128)(2,1)}, u32[]{:S(2)}, u32[]{:S(2)}) collective-permute-start(bf16[256,1536]{1,0:T(8,128)(2,1)} %collective-permute-done.17.d0), channel_id=1, source_target_pairs={{4,12},{5,13},{6,14},{7,15},{12,4},{13,5},{14,6},{15,7},{20,28},{2... | collective-permute-start | bytes 2359304 | tf_op jit(solution)/shard_map/ppermute | solution.py:52
  202.1 33.4 %collective-permute-start.12 = (bf16[2,256,1536]{2,1,0:T(8,128)(2,1)S(1)}, bf16[2,256,1536]{2,1,0:T(8,128)(2,1)}, u32[]{:S(2)}, u32[]{:S(2)}) collective-permute-start(bf16[2,256,1536]{2,1,0:T(8,128)(2,1)S(1)} %pad_maximum_fusion.1.co_ref), channel_id=1, source_target_pairs={{0,4},{1,5},{2,6},{3,7},{4,0},{5,1},{6,2},{7,3},{8,12},{9,13},{10,... | collective-permute-start | bytes 4718600 | tf_op jit(solution)/shard_map/ppermute | solution.py:52
  255.4 71.0 %collective-permute-start.22 = (bf16[256,1536]{1,0:T(8,128)(2,1)}, bf16[256,1536]{1,0:T(8,128)(2,1)}, u32[]{:S(2)}, u32[]{:S(2)}) collective-permute-start(bf16[256,1536]{1,0:T(8,128)(2,1)} %slice_bitcast_fusion.2), channel_id=1, source_target_pairs={{0,4},{1,5},{2,6},{3,7},{4,0},{5,1},{6,2},{7,3},{8,12},{9,13},{10,... | collective-permute-start | bytes 2359304 | tf_op jit(solution)/shard_map/ppermute | solution.py:52
  291.0 38.5 %collective-permute-start.24 = (bf16[256,1536]{1,0:T(8,128)(2,1)}, bf16[256,1536]{1,0:T(8,128)(2,1)S(1)}, u32[]{:S(2)}, u32[]{:S(2)}) collective-permute-start(bf16[256,1536]{1,0:T(8,128)(2,1)} %slice_bitcast_fusion.1), channel_id=1, source_target_pairs={{0,4},{1,5},{2,6},{3,7},{4,0},{5,1},{6,2},{7,3},{8,12},{9,13},{10,... | collective-permute-start | bytes 2359304 | tf_op jit(solution)/shard_map/ppermute | solution.py:52
  300.8 37.3 %collective-permute-start.57 = (bf16[2,384,1024]{2,1,0:T(8,128)(2,1)S(1)}, bf16[2,384,1024]{2,1,0:T(8,128)(2,1)S(1)}, u32[]{:S(2)}, u32[]{:S(2)}) collective-permute-start(bf16[2,384,1024]{2,1,0:T(8,128)(2,1)S(1)} %get-tuple-element.74), channel_id=1, source_target_pairs={{0,8},{1,9},{2,10},{3,11},{4,12},{5,13},{6,14},{7,15},{8,0},{9,1},... | collective-permute-start | bytes 4718600 | tf_op jit(solution)/shard_map/ppermute | solution.py:52
  320.0 39.0 %collective-permute-start.61 = (bf16[384,1024]{1,0:T(8,128)(2,1)}, bf16[384,1024]{1,0:T(8,128)(2,1)}, u32[]{:S(2)}, u32[]{:S(2)}) collective-permute-start(bf16[384,1024]{1,0:T(8,128)(2,1)} %get-tuple-element.76), channel_id=1, source_target_pairs={{0,16},{1,17},{2,18},{3,19},{4,20},{5,21},{6,22},{7,23},{8,24},{9,... | collective-permute-start | bytes 2359304 | tf_op jit(solution)/shard_map/ppermute | solution.py:52
  326.3 34.4 %collective-permute-start.63 = (bf16[384,1024]{1,0:T(8,128)(2,1)}, bf16[384,1024]{1,0:T(8,128)(2,1)}, u32[]{:S(2)}, u32[]{:S(2)}) collective-permute-start(bf16[384,1024]{1,0:T(8,128)(2,1)} %add_convert_fusion.1), channel_id=1, source_target_pairs={{0,8},{1,9},{2,10},{3,11},{4,12},{5,13},{6,14},{7,15},{8,0},{9,1},... | collective-permute-start | bytes 2359304 | tf_op jit(solution)/shard_map/ppermute | solution.py:52
  329.5 35.8 %collective-permute-start.21 = (bf16[256,1536]{1,0:T(8,128)(2,1)}, bf16[256,1536]{1,0:T(8,128)(2,1)}, u32[]{:S(2)}, u32[]{:S(2)}) collective-permute-start(bf16[256,1536]{1,0:T(8,128)(2,1)} %slice_bitcast_fusion.3), channel_id=1, source_target_pairs={{0,4},{1,5},{2,6},{3,7},{4,0},{5,1},{6,2},{7,3},{8,12},{9,13},{10,... | collective-permute-start | bytes 2359304 | tf_op jit(solution)/shard_map/ppermute | solution.py:52
  342.6 69.2 %collective-permute-start.46 = (bf16[256,1536]{1,0:T(8,128)(2,1)}, bf16[256,1536]{1,0:T(8,128)(2,1)}, u32[]{:S(2)}, u32[]{:S(2)}) collective-permute-start(bf16[256,1536]{1,0:T(8,128)(2,1)} %get-tuple-element.63), channel_id=1, source_target_pairs={{0,4},{1,5},{2,6},{3,7},{4,0},{5,1},{6,2},{7,3},{8,12},{9,13},{10,... | collective-permute-start | bytes 2359304 | tf_op jit(solution)/shard_map/ppermute | solution.py:52
  359.0 152.9 %collective-permute-start.56 = (bf16[2,384,1024]{2,1,0:T(8,128)(2,1)}, bf16[2,384,1024]{2,1,0:T(8,128)(2,1)}, u32[]{:S(2)}, u32[]{:S(2)}) collective-permute-start(bf16[2,384,1024]{2,1,0:T(8,128)(2,1)} %copy-done.45), channel_id=1, source_target_pairs={{0,8},{1,9},{2,10},{3,11},{4,12},{5,13},{6,14},{7,15},{8,0},{9,1},... | collective-permute-start | bytes 4718600 | tf_op jit(solution)/shard_map/ppermute | solution.py:52
  374.8 41.9 %collective-permute-start.45 = (bf16[256,768]{0,1:T(8,128)(2,1)}, bf16[256,768]{0,1:T(8,128)(2,1)S(1)}, u32[]{:S(2)}, u32[]{:S(2)}) collective-permute-start(bf16[256,768]{0,1:T(8,128)(2,1)} %bitcast.156), channel_id=1, source_target_pairs={{0,4},{1,5},{2,6},{3,7},{4,0},{5,1},{6,2},{7,3},{8,12},{9,13},{10,... | collective-permute-start | bytes 1179656 | tf_op jit(solution)/shard_map/ppermute | solution.py:52
  382.1 43.9 %collective-permute-start.65 = (bf16[192,1024]{1,0:T(8,128)(2,1)}, bf16[192,1024]{1,0:T(8,128)(2,1)S(1)}, u32[]{:S(2)}, u32[]{:S(2)}) collective-permute-start(bf16[192,1024]{1,0:T(8,128)(2,1)} %get-tuple-element.132), channel_id=1, source_target_pairs={{0,4},{1,5},{2,6},{3,7},{4,2},{5,3},{6,0},{7,1},{8,12},{9,13},{10,... | collective-permute-start | bytes 1179656 | tf_op jit(solution)/shard_map/ppermute | solution.py:52
  382.1 43.9 %collective-permute-start.64 = (bf16[192,1024]{1,0:T(8,128)(2,1)}, bf16[192,1024]{1,0:T(8,128)(2,1)S(1)}, u32[]{:S(2)}, u32[]{:S(2)}) collective-permute-start(bf16[192,1024]{1,0:T(8,128)(2,1)} %get-tuple-element.131), channel_id=1, source_target_pairs={{4,6},{5,7},{6,4},{7,5},{12,14},{13,15},{14,12},{15,13},{20,22},{2... | collective-permute-start | bytes 1179656 | tf_op jit(solution)/shard_map/ppermute | solution.py:52
  425.9 88.0 %collective-permute-start.58 = (bf16[2,384,1024]{2,1,0:T(8,128)(2,1)}, bf16[2,384,1024]{2,1,0:T(8,128)(2,1)}, u32[]{:S(2)}, u32[]{:S(2)}) collective-permute-start(bf16[2,384,1024]{2,1,0:T(8,128)(2,1)} %add_convert_fusion), channel_id=1, source_target_pairs={{0,16},{1,17},{2,18},{3,19},{4,20},{5,21},{6,22},{7,23},{8,24},{9,... | collective-permute-start | bytes 4718600 | tf_op jit(solution)/shard_map/ppermute | solution.py:52
  425.9 55.4 %collective-permute-start.33 = (bf16[1024,384]{1,0:T(8,128)(2,1)S(1)}, bf16[1024,384]{1,0:T(8,128)(2,1)S(1)}, u32[]{:S(2)}, u32[]{:S(2)}) collective-permute-start(bf16[1024,384]{1,0:T(8,128)(2,1)S(1)} %get-tuple-element.57), channel_id=1, source_target_pairs={{4,0},{5,1},{6,2},{7,3},{8,4},{9,5},{10,6},{11,7},{12,8},{13,9},{1... | collective-permute-start | bytes 2359304 | tf_op jit(solution)/shard_map/ppermute | solution.py:52
  432.5 64.2 %collective-permute-start.47 = (bf16[192,768]{1,0:T(8,128)(2,1)}, bf16[192,768]{1,0:T(8,128)(2,1)}, u32[]{:S(2)}, u32[]{:S(2)}) collective-permute-start(bf16[192,768]{1,0:T(8,128)(2,1)} %get-tuple-element.127), channel_id=1, source_target_pairs={{0,8},{1,9},{2,10},{3,11},{4,12},{5,13},{6,14},{7,15},{8,0},{9,1},... | collective-permute-start | bytes 884744 | tf_op jit(solution)/shard_map/ppermute | solution.py:52
  435.0 33.6 %collective-permute-start.52 = (bf16[192,768]{1,0:T(8,128)(2,1)S(1)}, bf16[192,768]{1,0:T(8,128)(2,1)S(1)}, u32[]{:S(2)}, u32[]{:S(2)}) collective-permute-start(bf16[192,768]{1,0:T(8,128)(2,1)S(1)} %get-tuple-element.126), channel_id=1, source_target_pairs={{0,16},{1,17},{2,18},{3,19},{4,20},{5,21},{6,22},{7,23},{8,24},{9,... | collective-permute-start | bytes 884744 | tf_op jit(solution)/shard_map/ppermute | solution.py:52
  511.9 42.3 %collective-permute-start.54 = (bf16[192,384]{1,0:T(8,128)(2,1)S(1)}, bf16[192,384]{1,0:T(8,128)(2,1)S(1)}, u32[]{:S(2)}, u32[]{:S(2)}) collective-permute-start(bf16[192,384]{1,0:T(8,128)(2,1)S(1)} %get-tuple-element.152), channel_id=1, source_target_pairs={{0,2},{1,3},{2,0},{3,1},{4,6},{5,7},{6,4},{7,5},{8,10},{9,11},{10,... | collective-permute-start | bytes 442376 | tf_op jit(solution)/shard_map/ppermute | solution.py:52
  521.7 34.2 %collective-permute-start.50 = (bf16[192,384]{1,0:T(8,128)(2,1)S(1)}, bf16[192,384]{1,0:T(8,128)(2,1)S(1)}, u32[]{:S(2)}, u32[]{:S(2)}) collective-permute-start(bf16[192,384]{1,0:T(8,128)(2,1)S(1)} %slice.109), channel_id=1, source_target_pairs={{0,1},{1,0},{2,3},{3,2},{4,5},{5,4},{6,7},{7,6},{8,9},{9,8},{10,11... | collective-permute-start | bytes 442376 | tf_op jit(solution)/shard_map/ppermute | solution.py:52
  522.7 90.2 %collective-permute-start.60 = (bf16[2,192,1024]{2,1,0:T(8,128)(2,1)}, bf16[2,192,1024]{2,1,0:T(8,128)(2,1)}, u32[]{:S(2)}, u32[]{:S(2)}) collective-permute-start(bf16[2,192,1024]{2,1,0:T(8,128)(2,1)} %get-tuple-element.124), channel_id=1, source_target_pairs={{0,4},{1,5},{2,6},{3,7},{4,2},{5,3},{6,0},{7,1},{8,12},{9,13},{10,... | collective-permute-start | bytes 2359304 | tf_op jit(solution)/shard_map/ppermute | solution.py:52
  522.7 90.2 %collective-permute-start.59 = (bf16[2,192,1024]{2,1,0:T(8,128)(2,1)}, bf16[2,192,1024]{2,1,0:T(8,128)(2,1)}, u32[]{:S(2)}, u32[]{:S(2)}) collective-permute-start(bf16[2,192,1024]{2,1,0:T(8,128)(2,1)} %get-tuple-element.123), channel_id=1, source_target_pairs={{4,6},{5,7},{6,4},{7,5},{12,14},{13,15},{14,12},{15,13},{20,22},{2... | collective-permute-start | bytes 2359304 | tf_op jit(solution)/shard_map/ppermute | solution.py:52
  524.4 33.5 %collective-permute-start.32 = (bf16[256,384]{1,0:T(8,128)(2,1)S(1)}, bf16[256,384]{1,0:T(8,128)(2,1)S(1)}, u32[]{:S(2)}, u32[]{:S(2)}) collective-permute-start(bf16[256,384]{1,0:T(8,128)(2,1)S(1)} %copy-done.76), channel_id=1, source_target_pairs={{0,3},{1,2},{2,1},{3,0},{4,7},{5,6},{6,5},{7,4},{8,11},{9,10},{10,... | collective-permute-start | bytes 589832 | tf_op jit(solution)/shard_map/ppermute | solution.py:52
  586.7 33.4 %all-to-all-start = ((f32[32,1,48]{2,1,0:T(1,128)}), f32[32,1,48]{2,1,0:T(1,128)S(1)}, u32[]{:S(2)}, u32[]{:S(2)}) async-start(f32[32,1,48]{2,1,0:T(1,128)} %bitcast.37), calls=%async_computation | async-start | bytes 32768 | tf_op jit(solution)/shard_map/all_to_all | solution.py:733
  (122 other events, 1564.7 us)
Sparse Core Ops, SparseCore 0:
  11.5 85.9 all-gather.2
  232.1 80.5 all-gather.4

commit v3 on v2

v3 whole, which is shorter than its diff:
```python
import jax
import jax.numpy as jnp
from jax import lax
from jax.experimental import pallas as pl
from jax.experimental.pallas import tpu as pltpu
from jax.sharding import PartitionSpec as P

HEAD_DIM = 96
HALF = HEAD_DIM // 2
LANES = 128
WINDOW = 1024
TILE = 256
EPSILON = 1e-05
THETA = 100000.0
SCALE = HEAD_DIM ** (-0.5)
LOG2E = 1.4426950408889634
SCALE2 = SCALE * LOG2E
BF = jnp.bfloat16
F32 = jnp.float32
NT = (((1,), (1,)), ((), ()))
NN = (((1,), (0,)), ((), ()))
TN = (((0,), (0,)), ((), ()))
MIB = 1 << 20
AXES = ("seq", "tp")
ANY = pl.BlockSpec(memory_space=pl.ANY)


def dot(a, b, dims=NN):
    return lax.dot_general(a, b, dims, preferred_element_type=F32)


def shape(dims, dtype):
    return jax.ShapeDtypeStruct(dims, dtype)


def cost(flops, moved, exps=0):
    return pl.CostEstimate(flops=flops // 16, bytes_accessed=moved // 16, transcendentals=0)


def params(mib):
    return pltpu.CompilerParams(vmem_limit_bytes=mib * MIB)


def send(a, to):
    size, ways = lax.axis_size("seq"), lax.axis_size("tp")
    pairs = []
    for s in range(size):
        for t in range(ways):
            there = to(s, t)
            if there is not None and 0 <= there[0] < size and 0 <= there[1] < ways:
                pairs.append((s * ways + t, there[0] * ways + there[1]))
    return lax.ppermute(a, AXES, pairs)


def doc_places(lengths, token_ids):
    bounds = jnp.cumsum(lengths)
    passed = token_ids[:, None] >= bounds[None, :]
    return jnp.sum(jnp.where(passed, lengths[None, :], 0), axis=1)


def spread_halves(w):
    n = w.shape[0]
    parts = w.reshape(n, -1, 2, HALF)
    parts = jnp.pad(parts, ((0, 0), (0, 0), (0, 0), (0, LANES // 2 - HALF)))
    return parts.reshape(n, -1)


def rotation_tables(places):
    freqs = THETA ** (-2.0 * jnp.arange(HALF, dtype=F32) / HEAD_DIM)
    angles = places.astype(F32)[:, None] * freqs[None, :]
    return jnp.cos(angles), jnp.sin(angles)


def lane_tables(cosine, sine):
    fill = ((0, 0), (0, LANES // 2 - HALF))
    cosine, sine = jnp.pad(cosine, fill), jnp.pad(sine, fill)
    return (
        jnp.concatenate([cosine, cosine], axis=1),
        jnp.concatenate([-sine, sine], axis=1),
    )


def project_kernel(
    sizes, sc_ref, own, r1, r2, r3, l1, l2, l3, g_ref, w_ref, c_ref, s_ref,
    h_ref, q_ref, kv_ref, x_s, sem,
):
    qheads, kvheads, ways = sizes
    o = pl.program_id(0)
    j = sc_ref[0]
    sources = {0: own, -1: r1, -2: r2, -3: r3, 1: l1, 2: l2, 3: l3}

    def fetch(at, slot):
        for d, ref in sources.items():

            @pl.when(at - j == d)
            def _():
                pltpu.make_async_copy(ref, x_s.at[slot], sem.at[slot]).start()

    @pl.when(o == 0)
    def _():
        fetch(0, 0)

    slot = lax.rem(o, 2)

    @pl.when(o + 1 < ways)
    def _():
        fetch(o + 1, 1 - slot)

    pltpu.make_async_copy(own, x_s.at[slot], sem.at[slot]).wait()
    x = x_s[slot].astype(F32)
    scale = lax.rsqrt(jnp.mean(x * x, axis=-1, keepdims=True) + EPSILON)
    h = (x * scale * g_ref[...]).astype(BF)
    h_ref[...] = h
    flat = dot(h, w_ref[...])
    cosine, sine = c_ref[...], s_ref[...]

    def turned(n):
        u = flat[:, n * LANES : (n + 1) * LANES]
        u = u * cosine + pltpu.roll(u, LANES // 2, 1) * sine
        return jnp.concatenate([u[:, :HALF], u[:, LANES // 2 : LANES // 2 + HALF]], axis=1)

    fill = jnp.zeros((x.shape[0], LANES - HEAD_DIM), F32)
    for n in range(qheads):
        q_ref[:, n * LANES : (n + 1) * LANES] = jnp.concatenate([turned(n), fill], axis=1).astype(
            BF
        )
    keys = [turned(qheads + n) for n in range(kvheads)]
    values = [flat[:, (qheads + kvheads) * LANES :]]
    kv_ref[...] = jnp.concatenate(keys + values, axis=1).astype(BF)


def project(sc, shards, gain, weight, cosine, sine, qheads, kvheads):
    owned, width = shards[0].shape
    ways = 4
    rows = owned * ways
    wide = weight.shape[1]
    kvwide = 2 * kvheads * HEAD_DIM
    row = lambda n: pl.BlockSpec((owned, n), lambda o, sc: (o, 0))
    whole = lambda m, n: pl.BlockSpec((m, n), lambda o, sc: (0, 0))
    return pl.pallas_call(
        lambda *refs: project_kernel((qheads, kvheads, ways), *refs),
        grid_spec=pltpu.PrefetchScalarGridSpec(
            num_scalar_prefetch=1,
            grid=(ways,),
            in_specs=[ANY] * 7 + [whole(1, width), whole(width, wide), row(LANES), row(LANES)],
            out_specs=[row(width), row(qheads * LANES), row(kvwide)],
            scratch_shapes=[pltpu.VMEM((2, owned, width), BF), pltpu.SemaphoreType.DMA((2,))],
        ),
        out_shape=[
            shape((rows, width), BF),
            shape((rows, qheads * LANES), BF),
            shape((rows, kvwide), BF),
        ],
        compiler_params=params(60),
        cost_estimate=cost(2 * rows * width * wide, 4 * rows * width),
    )(sc, *shards, gain.reshape(1, width), weight, cosine, sine)


def masked(raw, first_key, lo, diagonal, query_ids):
    keys = first_key + lax.broadcasted_iota(jnp.int32, raw.shape, 0)
    ok = keys >= lo
    if diagonal:
        ok = ok & (keys <= query_ids)
    return jnp.where(ok, raw, -1e30)


def load_pairs(kp_ref, ko_ref, k_s, v_s, head, kvheads):
    rows = ko_ref.shape[0]

    @pl.when(head == 0)
    def _():
        k_s[...] = jnp.zeros_like(k_s)
        v_s[...] = jnp.zeros_like(v_s)

    for n in range(kvheads):

        @pl.when(head == n)
        def _():
            for place, ref in ((0, kp_ref), (rows, ko_ref)):
                at = n * HEAD_DIM
                k_s[place : place + rows, :HEAD_DIM] = ref[:, at : at + HEAD_DIM]
                at = (kvheads + n) * HEAD_DIM
                v_s[place : place + rows, :HEAD_DIM] = ref[:, at : at + HEAD_DIM]


def tile_parts(q_ref, lo_ref, rows, t):
    q = jnp.concatenate([q_ref[:, :LANES], q_ref[:, LANES:]], axis=0)
    lo = jnp.concatenate([lo_ref[...], lo_ref[...]], axis=1)
    ids = rows + t * TILE + lax.broadcasted_iota(jnp.int32, (1, TILE), 1)
    return q, lo, jnp.concatenate([ids, ids], axis=1)


def attend_kernel(kvheads, q_ref, kp_ref, ko_ref, lo_ref, o_ref, l_ref, k_s, v_s):
    head, t = pl.program_id(0), pl.program_id(1)
    rows = ko_ref.shape[0]
    chunks = WINDOW // TILE + 1

    @pl.when(t == 0)
    def _():
        load_pairs(kp_ref, ko_ref, k_s, v_s, head, kvheads)

    q, lo, ids = tile_parts(q_ref, lo_ref, rows, t)
    scores = []
    for c in range(chunks):
        first = pl.multiple_of((t + c) * TILE, TILE)
        raw = dot(k_s[pl.ds(first, TILE)], q, NT)
        scores.append(masked(raw, first, lo, c == chunks - 1, ids))
    top = scores[0].max(axis=0, keepdims=True)
    for s in scores[1:]:
        top = jnp.maximum(top, s.max(axis=0, keepdims=True))
    top = top * SCALE2
    total = jnp.zeros_like(top)
    mixed = jnp.zeros((LANES, 2 * TILE), F32)
    for c in range(chunks):
        first = pl.multiple_of((t + c) * TILE, TILE)
        p = jnp.exp2(scores[c] * SCALE2 - top)
        total = total + jnp.sum(p, axis=0, keepdims=True)
        mixed = mixed + dot(v_s[pl.ds(first, TILE)], p.astype(BF), TN)
    l_ref[0, 0] = top + jnp.log2(total)
    out = jnp.transpose(mixed / total).astype(BF)
    here = pl.ds(pl.multiple_of(t * TILE, TILE), TILE)
    for n in range(kvheads):

        @pl.when(head == n)
        def _():
            for g in range(2):
                at = (2 * n + g) * HEAD_DIM
                o_ref[here, at : at + HEAD_DIM] = out[g * TILE : (g + 1) * TILE, :HEAD_DIM]


def attend(queries, pair_before, pair_here, lo, kvheads):
    rows = queries.shape[0]
    tiles = rows // TILE
    whole = pl.BlockSpec((rows, 2 * kvheads * HEAD_DIM), lambda h, t: (0, 0))
    return pl.pallas_call(
        lambda *refs: attend_kernel(kvheads, *refs),
        grid=(kvheads, tiles),
        in_specs=[
            pl.BlockSpec((TILE, 2 * LANES), lambda h, t: (t, h)),
            whole,
            whole,
            pl.BlockSpec((1, TILE), lambda h, t: (0, t)),
        ],
        out_specs=[whole, pl.BlockSpec((1, 1, 1, 2 * TILE), lambda h, t: (h, t, 0, 0))],
        out_shape=[
            shape((rows, 2 * kvheads * HEAD_DIM), BF),
            shape((kvheads, tiles, 1, 2 * TILE), F32),
        ],
        scratch_shapes=[pltpu.VMEM((2 * rows, LANES), BF), pltpu.VMEM((2 * rows, LANES), BF)],
        compiler_params=params(60),
        cost_estimate=cost(6400 * MIB, 5 * MIB, 5 * MIB),
    )(queries, pair_before, pair_here, lo)


def attend_back_kernel(
    kvheads, q_ref, kp_ref, ko_ref, lo_ref, o_ref, l_ref, do_ref, c_ref, s_ref,
    dq_ref, dp_ref, dkv_ref, k_s, v_s, dk_s, dv_s,
):
    head, t = pl.program_id(0), pl.program_id(1)
    rows = ko_ref.shape[0]
    chunks = WINDOW // TILE + 1

    @pl.when(t == 0)
    def _():
        load_pairs(kp_ref, ko_ref, k_s, v_s, head, kvheads)
        dk_s[...] = jnp.zeros_like(dk_s)
        dv_s[...] = jnp.zeros_like(dv_s)

    def heads_of(both):
        pair = both[:, : 2 * HEAD_DIM]
        for n in range(1, kvheads):
            pair = jnp.where(
                head == n, both[:, 2 * n * HEAD_DIM : 2 * (n + 1) * HEAD_DIM], pair
            )
        fill = jnp.zeros((TILE, LANES - HEAD_DIM), BF)
        first = jnp.concatenate([pair[:, :HEAD_DIM], fill], axis=1)
        second = jnp.concatenate([pair[:, HEAD_DIM:], fill], axis=1)
        return jnp.concatenate([first, second], axis=0)

    q, lo, ids = tile_parts(q_ref, lo_ref, rows, t)
    grad = heads_of(do_ref[...])
    prod = grad.astype(F32) * heads_of(o_ref[...]).astype(F32)
    center = jnp.sum(jnp.transpose(prod), axis=0, keepdims=True)
    logs = l_ref[0, 0]
    dq = jnp.zeros((LANES, 2 * TILE), F32)
    for c in range(chunks):
        first = pl.multiple_of((t + c) * TILE, TILE)
        here = pl.ds(first, TILE)
        keys = k_s[here]
        raw = masked(dot(keys, q, NT), first, lo, c == chunks - 1, ids)
        p = jnp.exp2(raw * SCALE2 - logs)
        dp = dot(v_s[here], grad, NT)
        ds = (p * (dp - center)).astype(BF)
        dv_s[here] += dot(p.astype(BF), grad)
        dk_s[here] += dot(ds, q)
        dq = dq + dot(keys, ds, TN)
    cosine = jnp.concatenate([c_ref[...], c_ref[...]], axis=1)
    sine = jnp.concatenate([s_ref[...], s_ref[...]], axis=1)
    a, b = dq[:HALF] * SCALE, dq[HALF:HEAD_DIM] * SCALE
    fill = jnp.zeros((LANES - HEAD_DIM, 2 * TILE), F32)
    dq = jnp.concatenate([a * cosine + b * sine, b * cosine - a * sine, fill], axis=0)
    dq = jnp.transpose(dq).astype(BF)
    mine = pl.ds(pl.multiple_of(t * TILE, TILE), TILE)
    last = t == pl.num_programs(1) - 1
    for n in range(kvheads):

        @pl.when(head == n)
        def _():
            for g in range(2):
                at = (2 * n + g) * HEAD_DIM
                dq_ref[mine, at : at + HEAD_DIM] = dq[g * TILE : (g + 1) * TILE, :HEAD_DIM]

        @pl.when((head == n) & last)
        def _():
            at = n * HEAD_DIM
            dp_ref[:, at : at + HEAD_DIM] = (dk_s[:rows, :HEAD_DIM] * SCALE).astype(BF)
            dkv_ref[:, at : at + HEAD_DIM] = dk_s[rows:, :HEAD_DIM] * SCALE
            at = (kvheads + n) * HEAD_DIM
            dp_ref[:, at : at + HEAD_DIM] = dv_s[:rows, :HEAD_DIM].astype(BF)
            dkv_ref[:, at : at + HEAD_DIM] = dv_s[rows:, :HEAD_DIM]


def attend_back(queries, pair_before, pair_here, lo, heads_out, logs, grads, tables, kvheads):
    rows = queries.shape[0]
    tiles = rows // TILE
    wide = 2 * kvheads * HEAD_DIM
    whole = pl.BlockSpec((rows, wide), lambda h, t: (0, 0))
    table = pl.BlockSpec((HALF, TILE), lambda h, t: (0, t))
    return pl.pallas_call(
        lambda *refs: attend_back_kernel(kvheads, *refs),
        grid=(kvheads, tiles),
        in_specs=[
            pl.BlockSpec((TILE, 2 * LANES), lambda h, t: (t, h)),
            whole,
            whole,
            pl.BlockSpec((1, TILE), lambda h, t: (0, t)),
            pl.BlockSpec((TILE, wide), lambda h, t: (t, 0)),
            pl.BlockSpec((1, 1, 1, 2 * TILE), lambda h, t: (h, t, 0, 0)),
            pl.BlockSpec((TILE, wide), lambda h, t: (t, 0)),
            table,
            table,
        ],
        out_specs=[whole, whole, whole],
        scratch_shapes=[
            pltpu.VMEM((2 * rows, LANES), BF),
            pltpu.VMEM((2 * rows, LANES), BF),
            pltpu.VMEM((2 * rows, LANES), F32),
            pltpu.VMEM((2 * rows, LANES), F32),
        ],
        out_shape=[shape((rows, wide), BF), shape((rows, wide), BF), shape((rows, wide), F32)],
        compiler_params=params(60),
        cost_estimate=cost(16000 * MIB, 8 * MIB, 5 * MIB),
    )(queries, pair_before, pair_here, lo, heads_out, logs, grads, *tables)


def shard(w_ref, k):
    pieces, _, part, width = w_ref.shape
    return w_ref[:, pl.ds(k, 1)].reshape(pieces * part, width)


def mix_kernel(
    sc_ref, o_ref, w_ref, x_ref, xr_ref, xl_ref, g_ref, x2_ref, h2_ref, row_ref
):
    m = pl.program_id(0)
    j = sc_ref[0]
    ways = o_ref.shape[0]
    acc = dot(o_ref[0], shard(w_ref, j))
    for k in range(1, ways):
        acc = acc + dot(o_ref[k], shard(w_ref, j ^ k))
    other = jnp.where((j & 1) == 1, xr_ref[...], xl_ref[...])
    x2 = jnp.where(m == 1, x_ref[...], other).astype(F32) + acc
    x2_ref[0] = x2
    scale = lax.rsqrt(jnp.mean(x2 * x2, axis=-1, keepdims=True) + EPSILON)
    h2_ref[0] = (x2 * scale * g_ref[...]).astype(BF)

    @pl.when(m == 1)
    def _():
        row_ref[...] = jnp.concatenate([o_ref[k] for k in range(ways)], axis=1)


def mix(sc, parts, weight, tokens, right, left, gain):
    owned, width = tokens.shape
    ways, _, local = parts.shape
    whole = lambda *dims: pl.BlockSpec(dims, lambda m, sc: (0,) * len(dims))
    return pl.pallas_call(
        mix_kernel,
        grid_spec=pltpu.PrefetchScalarGridSpec(
            num_scalar_prefetch=1,
            grid=(2,),
            in_specs=[
                pl.BlockSpec((ways, owned, local), lambda m, sc: (0, (sc[0] & 1) ^ 1 ^ m, 0)),
                whole(*weight.shape),
                whole(owned, width),
                whole(owned, width),
                whole(owned, width),
                whole(1, width),
            ],
            out_specs=[
                pl.BlockSpec((1, owned, width), lambda m, sc: (m, 0, 0)),
                pl.BlockSpec((1, owned, width), lambda m, sc: (m, 0, 0)),
                whole(owned, ways * local),
            ],
        ),
        out_shape=[
            shape((2, owned, width), F32),
            shape((2, owned, width), BF),
            shape((owned, ways * local), BF),
        ],
        compiler_params=params(60),
        cost_estimate=cost(1, 1),
    )(sc, parts, weight, tokens, right, left, gain.reshape(1, width))


def feed_kernel(
    sc_ref, ho_ref, hs_ref, co_ref, cs_ref, gu_own, d_own, w0, w1, w2, w3,
    a_ref, dg_ref, du_ref, sib_dh, own_dh, sib_y, own_y, w_s, y_s, dh_s, sem,
):
    r = pl.program_id(0)
    steps = pl.num_programs(0)
    place, odd = sc_ref[1], sc_ref[2]
    taken = [w0, w1, w2, w3]
    span = w_s.shape[3]

    def fetch(at, slot):
        @pl.when(odd == 0)
        def _():
            part = pl.ds(pl.multiple_of((place ^ at) * span, span), span)
            pltpu.make_async_copy(
                gu_own.at[:, :, part], w_s.at[slot, pl.ds(0, 2)], sem.at[0, slot]
            ).start()
            pltpu.make_async_copy(d_own.at[:, part], w_s.at[slot, 2], sem.at[1, slot]).start()

        for k, w in enumerate(taken):

            @pl.when((odd == 1) & (at == k))
            def _():
                pltpu.make_async_copy(
                    w.at[pl.ds(0, 2)], w_s.at[slot, pl.ds(0, 2)], sem.at[0, slot]
                ).start()
                pltpu.make_async_copy(w.at[2], w_s.at[slot, 2], sem.at[1, slot]).start()

    @pl.when(r == 0)
    def _():
        fetch(0, 0)
        y_s[...] = jnp.zeros_like(y_s)
        dh_s[...] = jnp.zeros_like(dh_s)

    slot = lax.rem(r, 2)

    @pl.when(r + 1 < steps)
    def _():
        fetch(r + 1, 1 - slot)

    pltpu.make_async_copy(w0.at[pl.ds(0, 2)], w_s.at[slot, pl.ds(0, 2)], sem.at[0, slot]).wait()
    pltpu.make_async_copy(w0.at[2], w_s.at[slot, 2], sem.at[1, slot]).wait()
    h = jnp.concatenate([hs_ref[0], ho_ref[0]], axis=0)
    ct = jnp.concatenate([cs_ref[0], co_ref[0]], axis=0)
    gate_w, up_w, down_w = w_s[slot, 0], w_s[slot, 1], w_s[slot, 2]
    gate = dot(h, gate_w)
    up = dot(h, up_w)
    da = dot(ct, down_w)
    sig = jax.nn.sigmoid(gate)
    act = gate * sig
    a = (act * up).astype(BF)
    dgate = (da * up * sig * (1.0 + gate * (1.0 - sig))).astype(BF)
    dup = (da * act).astype(BF)
    a_ref[...] = a
    dg_ref[...] = dgate
    du_ref[...] = dup
    y_s[...] += dot(a, down_w, NT)
    dh_s[...] += dot(dgate, gate_w, NT) + dot(dup, up_w, NT)

    @pl.when(r == steps - 1)
    def _():
        half = sib_dh.shape[0]
        for k, (dh_ref, y_ref) in enumerate(((sib_dh, sib_y), (own_dh, own_y))):
            dh_ref[...] = dh_s[k * half : (k + 1) * half].astype(BF)
            y_ref[...] = y_s[k * half : (k + 1) * half].astype(BF)


def feed(m, sc, h_own, h_sib, ct_own, ct_sib, gu_own, d_own, taken):
    _, owned, width = h_own.shape
    units = d_own.shape[1]
    span = units // 4
    rows = pl.BlockSpec((1, owned, width), lambda r, sc: (m, 0, 0))
    out = pl.BlockSpec((2 * owned, span), lambda r, sc: (0, sc[1] ^ r))
    whole = pl.BlockSpec((owned, width), lambda r, sc: (0, 0))
    return pl.pallas_call(
        feed_kernel,
        grid_spec=pltpu.PrefetchScalarGridSpec(
            num_scalar_prefetch=1,
            grid=(4,),
            in_specs=[rows] * 4 + [ANY] * 6,
            out_specs=[out, out, out] + [whole] * 4,
            scratch_shapes=[
                pltpu.VMEM((2, 3, width, span), BF),
                pltpu.VMEM((2 * owned, width), F32),
                pltpu.VMEM((2 * owned, width), F32),
                pltpu.SemaphoreType.DMA((2, 2)),
            ],
        ),
        out_shape=[shape((2 * owned, units), BF)] * 3 + [shape((owned, width), BF)] * 4,
        compiler_params=params(60),
        cost_estimate=cost(36 * owned * width * units, 22 * MIB, 2 * owned * units),
    )(sc, h_own, h_sib, ct_own, ct_sib, gu_own, d_own, *taken)


def feed_grad_kernel(
    sc_ref, ho0, hs0, co0, cs0, ho1, hs1, co1, cs1, a0, dg0, du0, a1, dg1, du1, out_ref, h_s, ct_s
):
    part = h_s.shape[0] // 2

    @pl.when(pl.program_id(0) == 0)
    def _():
        for k, (own, sib) in enumerate(((ho0, hs0), (ho1, hs1))):
            rows = jnp.concatenate([sib[0], own[0], sib[1], own[1]], axis=0)
            h_s[k * part : (k + 1) * part] = jnp.transpose(rows)
        for k, (own, sib) in enumerate(((co0, cs0), (co1, cs1))):
            rows = jnp.concatenate([sib[0], own[0], sib[1], own[1]], axis=0)
            ct_s[k * part : (k + 1) * part] = jnp.transpose(rows)

    both = lambda x, y: jnp.concatenate([x[...], y[...]], axis=0)
    for n, (left, right) in enumerate(
        ((h_s, both(dg0, dg1)), (h_s, both(du0, du1)), (ct_s, both(a0, a1)))
    ):
        grad = dot(left[...], right).astype(BF)
        for k in range(2):
            out_ref[k, n] = grad[k * part : (k + 1) * part]


def feed_grad(blocks, half, sc, h_own, h_sib, ct_own, ct_sib, first, second):
    _, owned, width = h_own.shape
    units = first[0].shape[1] // 2
    part = width // 4
    cut = 2
    lanes = lambda r: pl.BlockSpec((2, owned, part), lambda n, sc: (0, 0, sc[1] ^ r))
    right = pl.BlockSpec((2 * owned, units // cut), lambda n, sc: (0, half * cut + n))
    return pl.pallas_call(
        feed_grad_kernel,
        grid_spec=pltpu.PrefetchScalarGridSpec(
            num_scalar_prefetch=1,
            grid=(cut,),
            in_specs=[lanes(blocks[0])] * 4 + [lanes(blocks[1])] * 4 + [right] * 6,
            out_specs=pl.BlockSpec((2, 3, part, units // cut), lambda n, sc: (0, 0, 0, n)),
            scratch_shapes=[
                pltpu.VMEM((2 * part, 4 * owned), BF), pltpu.VMEM((2 * part, 4 * owned), BF)
            ],
        ),
        out_shape=shape((2, 3, part, units), BF),
        compiler_params=params(60),
        cost_estimate=cost(48 * owned * part * units, 14 * MIB),
    )(sc, *([h_own, h_sib, ct_own, ct_sib] * 2), *first, *second)


def norm_back(dn, v, gain):
    r = lax.rsqrt(jnp.mean(v * v, axis=-1, keepdims=True) + EPSILON)
    scaled = gain * dn
    gain_grad = jnp.sum(dn * (v * r), axis=0, keepdims=True)
    return r * scaled - v * (r * r * r) * jnp.mean(scaled * v, axis=-1, keepdims=True), gain_grad


def turn_back_kernel(
    sc_ref, a_ref, b_ref, z_ref, x2_ref, ct_ref, g_ref, w_ref, dx_ref, db_ref, gain_ref, do_ref
):
    dn = a_ref[...].astype(F32) + b_ref[...].astype(F32) + z_ref[...].astype(F32)
    dv, gain_grad = norm_back(dn, x2_ref[0], g_ref[...])
    gain_ref[...] = gain_grad
    dx = ct_ref[...].astype(F32) + dv
    dx_ref[...] = dx
    low = dx.astype(BF)
    db_ref[...] = low
    j = sc_ref[0]
    for d in range(do_ref.shape[0]):
        do_ref[j ^ d] = dot(low, shard(w_ref, d), NT).astype(BF)


def turn_back(sc, mine, core, tp, x2, cotangent, gain, weight):
    owned, width = cotangent.shape
    ways, local = weight.shape[1], weight.shape[0] * weight.shape[2]
    whole = lambda *dims: pl.BlockSpec(dims, lambda n, sc: (0,) * len(dims))
    own = pl.BlockSpec((1, owned, width), lambda n, sc: (1, 0, 0))
    return pl.pallas_call(
        turn_back_kernel,
        grid_spec=pltpu.PrefetchScalarGridSpec(
            num_scalar_prefetch=1,
            grid=(1,),
            in_specs=[
                whole(owned, width),
                whole(owned, width),
                whole(owned, width),
                own,
                whole(owned, width),
                whole(1, width),
                whole(*weight.shape),
            ],
            out_specs=[
                whole(owned, width),
                whole(owned, width),
                whole(1, width),
                whole(ways, owned, local),
            ],
        ),
        out_shape=[
            shape((owned, width), F32),
            shape((owned, width), BF),
            shape((1, width), F32),
            shape((ways, owned, local), BF),
        ],
        compiler_params=params(60),
        cost_estimate=cost(2 * owned * width * ways * local, 12 * MIB),
    )(sc, mine, core, tp, x2, cotangent, gain.reshape(1, width), weight)


def pair_grad_kernel(kvheads, own_ref, back_ref, c_ref, s_ref, out_ref):
    total = own_ref[...] + back_ref[...].astype(F32)
    cosine, sine = c_ref[...], s_ref[...]
    parts = []
    for n in range(kvheads):
        a = total[:, n * HEAD_DIM : n * HEAD_DIM + HALF]
        b = total[:, n * HEAD_DIM + HALF : (n + 1) * HEAD_DIM]
        parts += [a * cosine + b * sine, b * cosine - a * sine]
    parts.append(total[:, kvheads * HEAD_DIM :])
    out_ref[...] = jnp.concatenate(parts, axis=1).astype(BF)


def pair_grad(own, back, cosine, sine, kvheads):
    rows, wide = own.shape
    row = lambda n: pl.BlockSpec((TILE, n), lambda t: (t, 0))
    return pl.pallas_call(
        lambda *refs: pair_grad_kernel(kvheads, *refs),
        grid=(rows // TILE,),
        in_specs=[row(wide), row(wide), row(HALF), row(HALF)],
        out_specs=row(wide),
        out_shape=shape((rows, wide), BF),
        compiler_params=params(60),
        cost_estimate=cost(MIB, 4 * MIB),
    )(own, back, cosine, sine)


def finish_kernel(q_ref, k_ref, w_ref, x_ref, g_ref, dx_ref, out_ref, gain_ref, acc):
    d = pl.program_id(0)
    left = jnp.concatenate([q_ref[0], k_ref[0]], axis=1)
    term = dot(left, shard(w_ref, 0))

    @pl.when(d == 0)
    def _():
        acc[...] = term

    @pl.when(d > 0)
    def _():
        acc[...] += term

    @pl.when(d == pl.num_programs(0) - 1)
    def _():
        dv, gain_grad = norm_back(acc[...], x_ref[...].astype(F32), g_ref[...])
        out_ref[...] = dx_ref[...] + dv
        gain_ref[...] = gain_grad


def finish(query_parts, pair_parts, weight, tokens, gain, dx):
    owned, width = tokens.shape
    pieces, ways, part, _ = weight.shape
    wide = pieces * part
    local = query_parts.shape[2]
    whole = lambda *dims: pl.BlockSpec(dims, lambda d: (0,) * len(dims))
    one = pl.BlockSpec((1, owned, local), lambda d: (d, 0, 0))
    return pl.pallas_call(
        finish_kernel,
        grid=(ways,),
        in_specs=[
            one,
            one,
            pl.BlockSpec((pieces, 1, part, width), lambda d: (0, d, 0, 0)),
            whole(owned, width),
            whole(1, width),
            whole(owned, width),
        ],
        out_specs=[whole(owned, width), whole(1, width)],
        scratch_shapes=[pltpu.VMEM((owned, width), F32)],
        out_shape=[shape((owned, width), F32), shape((1, width), F32)],
        compiler_params=params(60),
        cost_estimate=cost(2 * owned * width * wide * ways, 14 * MIB),
    )(query_parts, pair_parts, weight, tokens, gain.reshape(1, width), dx)


def tie(*values):
    return lax.optimization_barrier(values)


def hop(bit, group):
    return lambda s, t: (s ^ (bit * group), t)


def exchanged_sum(pieces, group):
    groups = [[r + k * group for k in range(4)] for r in range(group)]
    came = lax.all_to_all(
        pieces, "seq", split_axis=0, concat_axis=0, axis_index_groups=groups, tiled=True
    )
    return jnp.sum(came.astype(F32), axis=0)


def swapped(pieces):
    return lax.all_to_all(pieces, "tp", split_axis=0, concat_axis=0, tiled=True)


def take(a, index, axis=0):
    return lax.dynamic_index_in_dim(a, index, axis, keepdims=False)


def middle_scatter(a, axis, size, group):
    middle = group // 2
    if middle == 1:
        return a
    groups = [
        [g * group + 2 * m + c for m in range(middle)] for g in range(size // group) for c in (0, 1)
    ]
    return lax.psum_scatter(
        a, "seq", scatter_dimension=axis, tiled=True, axis_index_groups=groups
    )


def gain_sum(part):
    devices = lax.axis_size("seq") * lax.axis_size("tp")
    parts = lax.all_to_all(
        part.reshape(devices, -1), AXES, split_axis=0, concat_axis=0, tiled=True
    )
    return jnp.sum(parts, axis=0)


def body(
    tokens, lengths, first_gain, w_query, w_keyval, w_output, second_gain, w_gateup, w_down,
    cotangent,
):
    size, ways = lax.axis_size("seq"), lax.axis_size("tp")
    owned, width = tokens.shape
    rows = owned * ways
    local = w_query.shape[1]
    qheads = local // HEAD_DIM
    kvheads = w_keyval.shape[2] // HEAD_DIM
    units = w_down.shape[0]
    span = units // 4
    group = size // 4
    i, j = lax.axis_index("seq"), lax.axis_index("tp")
    odd = i & 1
    place = i // group
    sc = jnp.stack([j, place, odd]).astype(jnp.int32)
    sibling = lambda s, t: (s ^ 1, t)
    partner = lambda s, t: (s, t ^ 1)

    near = lambda a: lax.dynamic_slice_in_dim(a, place * span, span, a.ndim - 1)
    far = lambda s, t: (s, t ^ 2) if s & 1 else None
    hop_odd = lambda bit: lambda s, t: (s ^ (bit * group), t) if s & 1 else None
    up = lambda a, k: send(a, lambda s, t: (s, t + 1) if t >= k else None)
    down = lambda a, k: send(a, lambda s, t: (s, t - 1) if t < ways - k else None)
    pieces = 8
    eights = [list(range(k, k + pieces)) for k in range(0, size, pieces)]

    def own_piece(w):
        part = w.shape[0] // pieces
        return lax.dynamic_slice_in_dim(w, (i % pieces) * part, part, 0)

    def gathered(parts):
        return lax.all_gather(parts, "seq", axis=0, axis_index_groups=eights)

    r1, l1 = up(tokens, 0), down(tokens, 0)
    output_mine = own_piece(w_output)
    o1, o2, o3 = (send(output_mine, lambda s, t: (s, t ^ d)) for d in (1, 2, 3))
    gateup_own = jnp.transpose(w_gateup, (1, 0, 2))
    down_own = jnp.transpose(w_down)
    r1, l1, gateup_own, down_own, w_query, w_keyval = tie(
        r1, l1, gateup_own, down_own, w_query, w_keyval
    )
    r2, l2 = up(r1, 1), down(l1, 1)
    piece = jnp.concatenate([near(gateup_own), near(down_own)[None]], axis=0)
    weight_one = jnp.concatenate(
        [spread_halves(w_query), spread_halves(w_keyval[:, 0]), w_keyval[:, 1]], axis=1
    )
    r2, l2, weight_one, piece, lengths, o1, o2, o3 = tie(
        r2, l2, weight_one, piece, lengths, o1, o2, o3
    )
    output_all = gathered(jnp.stack([output_mine, o1, o2, o3]))
    r3, l3 = up(r2, 2), down(l2, 2)
    w0 = send(piece, far)
    start_id = i * rows
    query_ids = start_id + jnp.arange(rows, dtype=jnp.int32)
    begins = doc_places(lengths, query_ids)
    cosine, sine = rotation_tables(query_ids - begins)
    lo = jnp.maximum(query_ids - (WINDOW - 1), begins) - (start_id - rows)
    lo = lo.reshape(1, rows)
    lane_cos, lane_sin = lane_tables(cosine, sine)
    turned_cos, turned_sin = jnp.transpose(cosine), jnp.transpose(sine)
    r3, l3, lane_cos, lane_sin, turned_cos, turned_sin, lo = tie(
        r3, l3, lane_cos, lane_sin, turned_cos, turned_sin, lo
    )
    inputs_one, queries, pair_here = project(
        sc, [tokens, r1, r2, r3, l1, l2, l3], first_gain, weight_one, lane_cos, lane_sin,
        qheads, kvheads,
    )
    pair_before = send(pair_here, lambda s, t: (s + 1, t))
    pair_here, ct_late = tie(pair_here, cotangent)
    ct_partner = send(ct_late, partner)
    heads_out, logs = attend(queries, pair_before, pair_here, lo, kvheads)

    heads_out, w0 = tie(heads_out, w0)
    pairs_of = lambda a: jnp.repeat(a.reshape(2, 2 * owned, local), 2, axis=0)
    head_parts = swapped(pairs_of(heads_out))
    w1, w2, w3 = (send(w0, hop_odd(bit)) for bit in (1, 2, 3))
    flat_mine = own_piece(
        jnp.concatenate(
            [jnp.transpose(w_query), jnp.transpose(w_keyval, (1, 2, 0)).reshape(-1, width)], axis=0
        )
    )
    head_parts, flat_mine = tie(head_parts, flat_mine)
    flat_parts = swapped(jnp.broadcast_to(flat_mine[None], (ways, *flat_mine.shape)))
    x2, h_own, heads_rows = mix(sc, head_parts, output_all, tokens, r1, l1, second_gain)
    ct_own = jnp.stack([ct_partner, cotangent])
    h_own, w1, w2, w3, ct_own = tie(h_own, w1, w2, w3, ct_own)
    h_sib = send(h_own, sibling)
    ct_sib = send(ct_own, sibling)
    h_sib, ct_sib, flat_parts = tie(h_sib, ct_sib, flat_parts)
    weight_all = gathered(flat_parts)

    fed = lambda m, h: feed(
        m, sc, h, h_sib, ct_own, ct_sib, gateup_own, down_own, (w0, w1, w2, w3)
    )
    add = lambda a, b: a.astype(F32) + b.astype(F32)
    a0, dg0, du0, sib_dh0, own_dh0, sib_y0, own_y0 = fed(0, h_own)
    core0 = send(sib_dh0, sibling)
    dh_part = add(own_dh0, core0).astype(BF)
    dh_part, h_next = tie(dh_part, h_own)
    dh_z = send(dh_part, partner)
    a1, dg1, du1, sib_dh1, own_dh1, sib_y1, own_y1 = fed(1, h_next)
    sib_dh1, dh_z = tie(sib_dh1, dh_z)
    core1 = send(sib_dh1, sibling)
    graded = lambda blocks, half, h: feed_grad(
        blocks, half, sc, h, h_sib, ct_own, ct_sib, (a0, dg0, du0), (a1, dg1, du1)
    )
    first_away, core1 = tie(graded((1, 3), 0, h_own), core1)
    first_came = send(first_away, hop(1, group))
    dx2, low, second_part, heads_grad = turn_back(
        sc, own_dh1, core1, dh_z, x2, cotangent, second_gain, output_all
    )
    grad_rows = swapped(heads_grad).reshape(rows, local)

    h_late, heads_rows, low, sib_y0, sib_y1 = tie(h_own, heads_rows, low, sib_y0, sib_y1)
    second_came = send(graded((2, 3), 1, h_late), hop(2, group))
    first_kept = graded((0, 2), 0, h_late)
    second_kept = graded((0, 1), 1, h_late)
    share = width // size
    low_parts = low.reshape(owned, size // 2, 2, share)
    low_mine = take(low_parts, odd, 2).reshape(owned, -1)
    low_came = send(take(low_parts, 1 - odd, 2).reshape(owned, -1), sibling)
    heads_sib = send(heads_rows, sibling)
    core_y = send(jnp.stack([sib_y0, sib_y1]), sibling)
    out_grad = dot(
        jnp.concatenate([low_mine, low_came], axis=0),
        jnp.concatenate([heads_rows, heads_sib], axis=0),
        TN,
    ).astype(BF)

    first_next = add(first_kept[1], first_came[1]).astype(BF)
    grad_rows, first_next, second_kept, out_grad, core_y = tie(
        grad_rows, first_next, second_kept, out_grad, core_y
    )
    first_back = send(first_next, hop(2, group))
    y_z = send(add(own_y0, core_y[0]).astype(BF), partner)
    dq, dpair_before, dpair_here = attend_back(
        queries, pair_before, pair_here, lo, heads_out, logs, grad_rows,
        (turned_cos, turned_sin), kvheads,
    )
    dq, dpair_before, y_z = tie(dq, dpair_before, y_z)
    returned = send(dpair_before, lambda s, t: (s - 1, t))
    query_parts = swapped(dq.reshape(ways, owned, local))
    dpair = pair_grad(dpair_here, returned, cosine, sine, kvheads)
    dpair, query_parts = tie(dpair, query_parts)
    pair_parts = swapped(dpair.reshape(ways, owned, local))

    dpair, second_came, out_grad = tie(dpair, second_came, out_grad)
    second_back = send(add(second_kept[1], second_came[1]).astype(BF), hop(1, group))
    grads = jnp.concatenate([dq, dpair], axis=1)
    full = dot(inputs_one, grads, TN).astype(BF).reshape(4, -1, 2, share, 2 * local)
    full_came = send(take(full, 1 - odd, 2), sibling)
    pair_parts, full_came, out_grad = tie(pair_parts, full_came, out_grad)
    out_block = exchanged_sum(out_grad.reshape(4, -1, ways * local), group)
    tokens_grad, first_part = finish(query_parts, pair_parts, weight_all, tokens, first_gain, dx2)
    devices = size * ways
    parts = jnp.concatenate(
        [first_part.reshape(devices, -1), second_part.reshape(devices, -1)], axis=1
    )
    gains = jnp.sum(
        lax.all_to_all(parts, AXES, split_axis=0, concat_axis=0, tiled=True), axis=0
    )
    own = width // devices

    one_low = add(take(full, odd, 2), full_came).astype(BF)
    one_came = [send(take(one_low, place ^ r), hop(r, group)) for r in (1, 2, 3)]
    block = jnp.concatenate(
        [
            add(first_kept[0], first_came[0]) + first_back.astype(F32),
            add(second_kept[0], second_came[0]) + second_back.astype(F32),
        ],
        axis=2,
    )
    block = middle_scatter(block, 1, size, group)
    low_block = block.astype(BF)
    cut = lambda k: lax.dynamic_slice_in_dim(low_block, k * share, share, 1)
    crossed = send(cut(1 - odd), lambda s, t: (s ^ 1, t ^ 2) if s & 1 else (s ^ 1, t))
    second = send(low_block[:, share:], far)
    out_block = middle_scatter(out_block, 0, size, group)
    out_low = out_block.astype(BF)
    columns = lambda k: lax.dynamic_slice_in_dim(out_low, k * local, local, 1)
    out_came = [send(columns(j ^ d), lambda s, t: (s, t ^ d)) for d in (1, 2, 3)]
    gains, crossed, second = tie(gains, crossed, second)
    block = jnp.where(odd == 0, block[:, :share], second.astype(F32)) + crossed.astype(F32)
    gateup_grad = jnp.transpose(block[:2], (1, 0, 2))
    down_grad = jnp.transpose(block[2])
    total = lambda first, rest: sum((a.astype(F32) for a in rest), first.astype(F32))
    output_grad = jnp.transpose(
        total(lax.dynamic_slice_in_dim(out_block, j * local, local, 1), out_came)
    )
    one_block = total(take(one_low, place), one_came)
    one_block = middle_scatter(one_block.reshape(-1, 2 * local), 0, size, group)
    query_grad = one_block[:, :local]
    keyval_grad = one_block[:, local:].reshape(share, 2, -1)
    result = (x2[1] + (add(own_y1, core_y[1]) + y_z.astype(F32))).astype(BF)
    return (
        result, tokens_grad, gains[:own], query_grad, keyval_grad, output_grad, gains[own:],
        gateup_grad, down_grad,
    )


def solution(mesh):
    return jax.shard_map(
        body,
        mesh=mesh,
        in_specs=(
            P(AXES, None), P(), P(), P(None, "tp"), P(None, None, "tp"), P("tp", None), P(),
            P(None, None, "tp"), P("tp", None), P(AXES, None),
        ),
        out_specs=(
            P(AXES, None), P(AXES, None), P(AXES), P("seq", "tp"), P("seq", None, "tp"),
            P("tp", "seq"), P(AXES), P("seq", None, "tp"), P("tp", "seq"),
        ),
        check_vma=False,
    )
```

time: 639 us -> 515 us (0.81)
  starting transfers between devices: 215 us -> 94.2 us
  local copies, waits for them, and re-layouts: 90.4 us -> 55.1 us
  Pallas kernels: 122 us -> 151 us
    ppermute x66 -> x38, starting transfers between devices: 185 us -> 65.1 us  [send(): return lax.ppermute(a, AXES, pairs)]
    all_to_all x2 -> x7, waiting for transfers between devices: 2.49 us -> 64.6 us  [the longest x5 55 us: swapped(): return lax.all_to_all(pieces, 'tp', split_axis=0, concat_axis=0, tiled=True)]
    ppermute x66 -> x38, waiting for transfers between devices: 133 us -> 75.7 us  [send(): return lax.ppermute(a, AXES, pairs)]
    unnamed x172 -> x81, local copies, waits for them, and re-layouts: 49.6 us -> 22.9 us
    pallas_call x4, Pallas kernels: 21 us -> 32.4 us  [feed_grad(): pl.pallas_call(feed_grad_kernel, grid_spec=pltpu.PrefetchScalarGridSpec(n...]
    convert_element_type x13 -> x8, other arithmetic: 20.8 us -> 13.1 us  [the longest x1 2.87 us: body(): result = (x2[1] + (add(own_y1, core_y[1]) + y_z.astype(F32))).astype(BF)]
    all_to_all x2 -> x7, starting transfers between devices: 29.7 us -> 29 us  [the longest x5 19.7 us: swapped(): return lax.all_to_all(pieces, 'tp', split_axis=0, concat_axis=0, tiled=True)]
  transfers between devices with their start and end apart: 70 -> 47, of which waited for: 17 -> 17; matrix products, arithmetic and copies ran while one was open for 16% -> 18% of each run, Pallas kernels for 19% -> 30%
where the time goes in v3:
time: 515 us; the launch traced here: 507 us
  Pallas kernels  151 us (29%)
  waiting for transfers between devices  140 us (27%)
  starting transfers between devices  94.2 us (18%)
  local copies, waits for them, and re-layouts  55.1 us (11%)
  other arithmetic  43 us (8%)
  between operations  15 us (3%)
  matrix products  9.05 us (2%)
    ppermute x38, waiting for transfers between devices, send(): return lax.ppermute(a, AXES, pairs)  75.7 us
    ppermute x38, starting transfers between devices, send(): return lax.ppermute(a, AXES, pairs)  65.1 us
    all_to_all x5, waiting for transfers between devices, swapped(): return lax.all_to_all(pieces, 'tp', split_axis=0, concat_axis=0, tiled=True)  55 us
    pallas_call x2, Pallas kernels, feed(): pl.pallas_call(feed_kernel, grid_spec=pltpu.PrefetchScalarGridSpec(num_sc...  35.3 us
    pallas_call x4, Pallas kernels, feed_grad(): pl.pallas_call(feed_grad_kernel, grid_spec=pltpu.PrefetchScalarGridSpec(n...  32.4 us
    pallas_call x1, Pallas kernels, attend_back(): pl.pallas_call(lambda *refs: attend_back_kernel(kvheads, *refs), grid=(kv...  24.5 us
    unnamed x81, local copies, waits for them, and re-layouts  22.9 us
    all_to_all x5, starting transfers between devices, swapped(): return lax.all_to_all(pieces, 'tp', split_axis=0, concat_axis=0, tiled=True)  19.7 us
  transfers between devices with their start and end apart: 47, of which 17 were waited for; matrix products, arithmetic and copies ran while one was open for 18% of the time, Pallas kernels for 30%

profile of v3, /device:TPU:0, one launch (start us, length us, event | category | flops | bytes accessed | tf_op | source)
XLA Modules:
  0.0 507.4 jit_solution(11540960499272907216)
XLA Ops:
  7.2 5.1 %collective-permute-start = (bf16[256,1536]{1,0:T(8,128)(2,1)}, bf16[256,1536]{1,0:T(8,128)(2,1)S(1)}, u32[]{:S(2)}, u32[]{:S(2)}) collective-permute-start(bf16[256,1536]{1,0:T(8,128)(2,1)} %x_ref.3), channel_id=1, source_target_pairs={{0,1},{1,2},{2,3},{4,5},{5,6},{6,7},{8,9},{9,10},{10,11},{12,13},{... | collective-permute-start | bytes 2359304 | tf_op jit(solution)/shard_map/ppermute | solution.py:52
  20.4 7.4 %copy.62 = bf16[1536,2,1024]{2,0,1:T(8,128)(2,1)} copy(bf16[1536,2,1024]{2,1,0:T(2,128)(2,1)} %param.17) | data formatting | bytes 12582912 | tf_op args[7]
  27.8 4.7 copy.50
  75.6 13.8 %collective-permute-done.8.refs_7_ = bf16[256,1536]{1,0:T(8,128)(2,1)} collective-permute-done((bf16[256,1536]{1,0:T(8,128)(2,1)}, bf16[256,1536]{1,0:T(8,128)(2,1)}, u32[]{:S(2)}, u32[]{:S(2)}) %collective-permute-start.8) | collective-permute-done | bytes 786464 | tf_op jit(solution)/shard_map/ppermute | solution.py:52
  89.4 10.7 %shard_map.169 = (bf16[1024,1536]{1,0:T(8,128)(2,1)}, bf16[1024,512]{1,0:T(8,128)(2,1)}, bf16[1024,384]{1,0:T(8,128)(2,1)}) custom-call(s32[3]{0:T(128)} %pad_add_fusion.refs_0_.sc_ref, bf16[256,1536]{1,0:T(8,128)(2,1)} %x_ref.3, bf16[256,1536]{1,0:T(8,128)(2,1)} %copy-done.14, bf16[256,1536]{1,0:T(8,128)(2,1)} %collective-permute-done.2.refs_3_, ...), custom_call_target="tpu_custom_call" | custom-call | flops 188743680 | bytes 393216 | tf_op jit(solution)/shard_map/pallas_call | solution.py:140
  100.2 13.3 %collective-permute-start.9 = (bf16[1024,384]{1,0:T(8,128)(2,1)}, bf16[1024,384]{1,0:T(8,128)(2,1)S(1)}, u32[]{:S(2)}, u32[]{:S(2)}) collective-permute-start(bf16[1024,384]{1,0:T(8,128)(2,1)} %get-tuple-element.121.refs_2_), channel_id=1, source_target_pairs={{0,4},{1,5},{2,6},{3,7},{4,8},{5,9},{6,10},{7,11},{8,12},{9,13},{1... | collective-permute-start | bytes 2359304 | tf_op jit(solution)/shard_map/ppermute | solution.py:52
  114.3 15.6 %shard_map.170 = (bf16[1024,384]{1,0:T(8,128)(2,1)}, f32[2,4,1,512]{3,2,1,0:T(1,128)}) custom-call(bf16[1024,512]{1,0:T(8,128)(2,1)} %get-tuple-element.119.refs_0_, bf16[1024,384]{1,0:T(8,128)(2,1)} %copy-done.18, bf16[1024,384]{1,0:T(8,128)(2,1)} %get-tuple-element.121.refs_2_, s32[1,1024]{1,0:T(1,128)} %maximum_subtract_fusion.refs_3_), custom_call_target="tpu_custom_call" | custom-call | flops 419430400 | bytes 327680 | tf_op jit(solution)/shard_map/pallas_call | solution.py:235
  132.3 4.3 all-to-all-start
  146.6 27.6 %all-to-all-done.o_ref = bf16[4,512,384]{2,1,0:T(8,128)(2,1)} async-done(((bf16[4,512,384]{2,1,0:T(8,128)(2,1)}), bf16[4,512,384]{2,1,0:T(8,128)(2,1)}, u32[]{:S(2)}, u32[]{:S(2)}) %all-to-all-start) | async-done | bytes 1572896 | tf_op jit(solution)/shard_map/all_to_all | solution.py:703
  182.9 9.7 %shard_map.171 = (f32[2,256,1536]{2,1,0:T(8,128)}, bf16[2,256,1536]{2,1,0:T(8,128)(2,1)}, bf16[256,1536]{1,0:T(8,128)(2,1)}) custom-call(s32[3]{0:T(128)} %pad_add_fusion.refs_0_.sc_ref, bf16[4,512,384]{2,1,0:T(8,128)(2,1)} %all-to-all-done.o_ref, bf16[8,4,48,1536]{3,2,1,0:T(8,128)(2,1)} %bitcast.93, bf16[256,1536]{1,0:T(8,128)(2,1)} %x_ref.3, ...), custom_call_target="tpu_custom_call" | custom-call | tf_op jit(solution)/shard_map/pallas_call | solution.py:385
  192.7 4.7 collective-permute-start.15
  197.5 12.1 %all-to-all-done.1 = bf16[4,96,1536]{2,1,0:T(8,128)(2,1)} async-done(((bf16[4,96,1536]{2,1,0:T(8,128)(2,1)}), bf16[4,96,1536]{2,1,0:T(8,128)(2,1)}, u32[]{:S(2)}, u32[]{:S(2)}) %all-to-all-start.1) | async-done | bytes 1179680 | tf_op jit(solution)/shard_map/all_to_all | solution.py:703
  210.8 17.6 %shard_map.172 = (bf16[512,1024]{1,0:T(8,128)(2,1)}, bf16[512,1024]{1,0:T(8,128)(2,1)}, bf16[512,1024]{1,0:T(8,128)(2,1)}, bf16[256,1536]{1,0:T(8,128)(2,1)}, bf...) custom-call(s32[3]{0:T(128)} %pad_add_fusion.refs_0_.sc_ref, ...), custom_call_target="tpu_custom_call" | custom-call | flops 905969664 | bytes 1441792 | tf_op jit(solution)/shard_map/pallas_call | solution.py:488
  232.4 17.7 %shard_map.173 = (bf16[512,1024]{1,0:T(8,128)(2,1)}, bf16[512,1024]{1,0:T(8,128)(2,1)}, bf16[512,1024]{1,0:T(8,128)(2,1)}, bf16[256,1536]{1,0:T(8,128)(2,1)}, bf...) custom-call(s32[3]{0:T(128)} %pad_add_fusion.refs_0_.sc_ref, ...), custom_call_target="tpu_custom_call" | custom-call | flops 905969664 | bytes 1441792 | tf_op jit(solution)/shard_map/pallas_call | solution.py:488
  252.0 8.2 %shard_map.174 = bf16[2,3,384,512]{3,2,1,0:T(8,128)(2,1)} custom-call(s32[3]{0:T(128)} %pad_add_fusion.refs_0_.sc_ref, bf16[2,256,1536]{2,1,0:T(8,128)(2,1)} %get-tuple-element.163.ho_ref.ho0.ho1, bf16[2,256,1536]{2,1,0:T(8,128)(2,1)} %copy-done.3, bf16[2,256,1536]{2,1,0:T(8,128)(2,1)} %copy-done.2, ...), custom_call_target="tpu_custom_call" | custom-call | flops 150994944 | bytes 917504 | tf_op jit(solution)/shard_map/pallas_call | solution.py:538
  262.4 8.2 %shard_map.175 = (f32[256,1536]{1,0:T(8,128)}, bf16[256,1536]{1,0:T(8,128)(2,1)}, f32[1,1536]{1,0:T(1,128)}, bf16[4,256,384]{2,1,0:T(8,128)(2,1)}) custom-call(s32[3]{0:T(128)} %pad_add_fusion.refs_0_.sc_ref, bf16[256,1536]{1,0:T(8,128)(2,1)} %get-tuple-element.146.a_ref, bf16[256,1536]{1,0:T(8,128)(2,1)} %copy-done.28, bf16[256,1536]{1,0:T(8,128)(2,1)} %copy-done.27, ...), custom_call_target="tpu_custom_call" | custom-call | flops 75497472 | bytes 786432 | tf_op jit(solution)/shard_map/pallas_call | solution.py:582
  277.9 8.1 %shard_map.180 = bf16[2,3,384,512]{3,2,1,0:T(8,128)(2,1)} custom-call(s32[3]{0:T(128)} %pad_add_fusion.refs_0_.sc_ref, bf16[2,256,1536]{2,1,0:T(8,128)(2,1)} %get-tuple-element.163.ho_ref.ho0.ho1, bf16[2,256,1536]{2,1,0:T(8,128)(2,1)} %copy-done.3, bf16[2,256,1536]{2,1,0:T(8,128)(2,1)} %copy-done.2, ...), custom_call_target="tpu_custom_call" | custom-call | flops 150994944 | bytes 917504 | tf_op jit(solution)/shard_map/pallas_call | solution.py:538
  288.0 8.1 %shard_map.176 = bf16[2,3,384,512]{3,2,1,0:T(8,128)(2,1)} custom-call(s32[3]{0:T(128)} %pad_add_fusion.refs_0_.sc_ref, bf16[2,256,1536]{2,1,0:T(8,128)(2,1)} %get-tuple-element.163.ho_ref.ho0.ho1, bf16[2,256,1536]{2,1,0:T(8,128)(2,1)} %copy-done.3, bf16[2,256,1536]{2,1,0:T(8,128)(2,1)} %copy-done.2, ...), custom_call_target="tpu_custom_call" | custom-call | flops 150994944 | bytes 917504 | tf_op jit(solution)/shard_map/pallas_call | solution.py:538
  296.1 8.1 %shard_map.177 = bf16[2,3,384,512]{3,2,1,0:T(8,128)(2,1)} custom-call(s32[3]{0:T(128)} %pad_add_fusion.refs_0_.sc_ref, bf16[2,256,1536]{2,1,0:T(8,128)(2,1)} %get-tuple-element.163.ho_ref.ho0.ho1, bf16[2,256,1536]{2,1,0:T(8,128)(2,1)} %copy-done.3, bf16[2,256,1536]{2,1,0:T(8,128)(2,1)} %copy-done.2, ...), custom_call_target="tpu_custom_call" | custom-call | flops 150994944 | bytes 917504 | tf_op jit(solution)/shard_map/pallas_call | solution.py:538
  304.2 4.3 convolution_convert_fusion.1
  308.5 8.2 %collective-permute-done.20 = bf16[2,3,384,512]{3,2,1,0:T(8,128)(2,1)} collective-permute-done((bf16[2,3,384,512]{3,2,1,0:T(8,128)(2,1)}, bf16[2,3,384,512]{3,2,1,0:T(8,128)(2,1)}, u32[]{:S(2)}, u32[]{:S(2)}) %collective-permute-start.20) | collective-permute-done | bytes 2359328 | tf_op jit(solution)/shard_map/ppermute | solution.py:52
  322.2 24.5 %shard_map.178 = (bf16[1024,384]{1,0:T(8,128)(2,1)}, bf16[1024,384]{1,0:T(8,128)(2,1)}, f32[1024,384]{1,0:T(8,128)}) custom-call(bf16[1024,512]{1,0:T(8,128)(2,1)} %get-tuple-element.119.refs_0_, bf16[1024,384]{1,0:T(8,128)(2,1)} %copy-done.18, bf16[1024,384]{1,0:T(8,128)(2,1)} %get-tuple-element.121.refs_2_, s32[1,1024]{1,0:T(1,128)} %maximum_subtract_fusion.refs_3_, ...), custom_call_target="tpu_custom_call" | custom-call | flops 1048576000 | bytes 524288 | tf_op jit(solution)/shard_map/pallas_call | solution.py:329
  356.5 5.0 shard_map.179
  361.5 9.9 %all-to-all-done.3.q_ref = bf16[4,256,384]{2,1,0:T(8,128)(2,1)S(1)} async-done(((bf16[4,256,384]{2,1,0:T(8,128)(2,1)}), bf16[4,256,384]{2,1,0:T(8,128)(2,1)S(1)}, u32[]{:S(2)}, u32[]{:S(2)}) %all-to-all-start.3) | async-done | bytes 786464 | tf_op jit(solution)/shard_map/all_to_all | solution.py:703
  375.0 4.7 convolution_convert_fusion
  390.0 5.4 %all-to-all-done.4.k_ref = bf16[4,256,384]{2,1,0:T(8,128)(2,1)S(1)} async-done(((bf16[4,256,384]{2,1,0:T(8,128)(2,1)}), bf16[4,256,384]{2,1,0:T(8,128)(2,1)S(1)}, u32[]{:S(2)}, u32[]{:S(2)}) %all-to-all-start.4) | async-done | bytes 786464 | tf_op jit(solution)/shard_map/all_to_all | solution.py:703
  396.3 4.5 all-to-all-start.6
  400.8 10.6 %collective-permute-done.28 = bf16[3,384,512]{2,1,0:T(8,128)(2,1)} collective-permute-done((bf16[3,384,512]{2,1,0:T(8,128)(2,1)}, bf16[3,384,512]{2,1,0:T(8,128)(2,1)}, u32[]{:S(2)}, u32[]{:S(2)}) %collective-permute-start.28) | collective-permute-done | bytes 1179680 | tf_op jit(solution)/shard_map/ppermute | solution.py:52
  426.4 20.9 %collective-permute-done.34 = bf16[1,192,768]{2,1,0:T(8,128)(2,1)S(1)} collective-permute-done((bf16[1,192,768]{2,1,0:T(8,128)(2,1)S(1)}, bf16[1,192,768]{2,1,0:T(8,128)(2,1)S(1)}, u32[]{:S(2)}, u32[]{:S(2)}) %collective-permute-start.34) | collective-permute-done | bytes 294944 | tf_op jit(solution)/shard_map/ppermute | solution.py:52
  464.0 9.3 %shard_map.181 = (f32[256,1536]{1,0:T(8,128)}, f32[1,1536]{1,0:T(1,128)}) custom-call(bf16[4,256,384]{2,1,0:T(8,128)(2,1)} %copy-done.19, bf16[4,256,384]{2,1,0:T(8,128)(2,1)} %copy-done.20, bf16[8,4,96,1536]{3,2,1,0:T(8,128)(2,1)} %bitcast.95, bf16[256,1536]{1,0:T(8,128)(2,1)} %x_ref.3, f32[1,1536]{1,0:T(1,128)} %reshape.197.refs_8_.g_ref, ...), custom_call_target="tpu_custom_call" | custom-call | flops 150994944 | bytes 917504 | tf_op jit(solution)/shard_map/pallas_call | solution.py:667
  477.4 4.8 all-to-all-start.5
  484.1 9.7 %all-to-all-done.5 = f32[32,1,96]{2,1,0:T(1,128)S(1)} async-done(((f32[32,1,96]{2,1,0:T(1,128)}), f32[32,1,96]{2,1,0:T(1,128)S(1)}, u32[]{:S(2)}, u32[]{:S(2)}) %all-to-all-start.5) | async-done | bytes 12320 | tf_op jit(solution)/shard_map/all_to_all | solution.py:891
  (228 shorter events, 165.6 us)
Async XLA Ops:
  7.2 175.7 %all-gather.5.cloned.1.call-start = ((), (), s32[]{:S(2)}) async-start(), calls=%async_computation.7 | async-start | bytes 5308416 | tf_op jit(solution)/shard_map/all_gather | solution.py:763
  7.2 26.0 %collective-permute-start = (bf16[256,1536]{1,0:T(8,128)(2,1)}, bf16[256,1536]{1,0:T(8,128)(2,1)S(1)}, u32[]{:S(2)}, u32[]{:S(2)}) collective-permute-start(bf16[256,1536]{1,0:T(8,128)(2,1)} %x_ref.3), channel_id=1, source_target_pairs={{0,1},{1,2},{2,3},{4,5},{5,6},{6,7},{8,9},{9,10},{10,11},{12,13},{... | collective-permute-start | bytes 2359304 | tf_op jit(solution)/shard_map/ppermute | solution.py:52
  12.4 24.9 %collective-permute-start.1 = (bf16[256,1536]{1,0:T(8,128)(2,1)}, bf16[256,1536]{1,0:T(8,128)(2,1)}, u32[]{:S(2)}, u32[]{:S(2)}) collective-permute-start(bf16[256,1536]{1,0:T(8,128)(2,1)} %x_ref.3), channel_id=1, source_target_pairs={{1,0},{2,1},{3,2},{5,4},{6,5},{7,6},{9,8},{10,9},{11,10},{13,12},{... | collective-permute-start | bytes 2359304 | tf_op jit(solution)/shard_map/ppermute | solution.py:52
  14.4 43.7 %collective-permute-start.4 = (bf16[48,1536]{1,0:T(8,128)(2,1)}, bf16[48,1536]{1,0:T(8,128)(2,1)}, u32[]{:S(2)}, u32[]{:S(2)}) collective-permute-start(bf16[48,1536]{1,0:T(8,128)(2,1)} %constant_dynamic-slice_fusion.6), channel_id=1, source_target_pairs={{0,1},{1,0},{2,3},{3,2},{4,5},{5,4},{6,7},{7,6},{8,9},{9,8},{10,11... | collective-permute-start | bytes 442376 | tf_op jit(solution)/shard_map/ppermute | solution.py:52
  17.0 41.0 %collective-permute-start.5 = (bf16[48,1536]{1,0:T(8,128)(2,1)}, bf16[48,1536]{1,0:T(8,128)(2,1)}, u32[]{:S(2)}, u32[]{:S(2)}) collective-permute-start(bf16[48,1536]{1,0:T(8,128)(2,1)} %constant_dynamic-slice_fusion.6), channel_id=1, source_target_pairs={{0,2},{1,3},{2,0},{3,1},{4,6},{5,7},{6,4},{7,5},{8,10},{9,11},{10,... | collective-permute-start | bytes 442376 | tf_op jit(solution)/shard_map/ppermute | solution.py:52
  20.4 37.6 %collective-permute-start.6 = (bf16[48,1536]{1,0:T(8,128)(2,1)}, bf16[48,1536]{1,0:T(8,128)(2,1)}, u32[]{:S(2)}, u32[]{:S(2)}) collective-permute-start(bf16[48,1536]{1,0:T(8,128)(2,1)} %constant_dynamic-slice_fusion.6), channel_id=1, source_target_pairs={{0,3},{1,2},{2,1},{3,0},{4,7},{5,6},{6,5},{7,4},{8,11},{9,10},{10,... | collective-permute-start | bytes 442376 | tf_op jit(solution)/shard_map/ppermute | solution.py:52
  64.3 65.5 %collective-permute-start.10 = (bf16[3,1536,256]{2,1,0:T(8,128)(2,1)}, bf16[3,1536,256]{2,1,0:T(8,128)(2,1)}, u32[]{:S(2)}, u32[]{:S(2)}) collective-permute-start(bf16[3,1536,256]{2,1,0:T(8,128)(2,1)} %pad_maximum_fusion.2), channel_id=1, source_target_pairs={{4,6},{5,7},{6,4},{7,5},{12,14},{13,15},{14,12},{15,13},{20,22},{2... | collective-permute-start | bytes 7077896 | tf_op jit(solution)/shard_map/ppermute | solution.py:52
  132.3 41.9 %all-to-all-start = ((bf16[4,512,384]{2,1,0:T(8,128)(2,1)}), bf16[4,512,384]{2,1,0:T(8,128)(2,1)}, u32[]{:S(2)}, u32[]{:S(2)}) async-start(bf16[4,512,384]{2,1,0:T(8,128)(2,1)} %bitcast.98), calls=%async_computation | async-start | bytes 3145728 | tf_op jit(solution)/shard_map/all_to_all | solution.py:703
  136.7 56.0 %collective-permute-start.11 = (bf16[3,1536,256]{2,1,0:T(8,128)(2,1)}, bf16[3,1536,256]{2,1,0:T(8,128)(2,1)}, u32[]{:S(2)}, u32[]{:S(2)}) collective-permute-start(bf16[3,1536,256]{2,1,0:T(8,128)(2,1)} %collective-permute-done.10.w0), channel_id=1, source_target_pairs={{4,12},{5,13},{6,14},{7,15},{12,4},{13,5},{14,6},{15,7},{20,28},{2... | collective-permute-start | bytes 7077896 | tf_op jit(solution)/shard_map/ppermute | solution.py:52
  138.7 53.9 %collective-permute-start.12 = (bf16[3,1536,256]{2,1,0:T(8,128)(2,1)}, bf16[3,1536,256]{2,1,0:T(8,128)(2,1)}, u32[]{:S(2)}, u32[]{:S(2)}) collective-permute-start(bf16[3,1536,256]{2,1,0:T(8,128)(2,1)} %collective-permute-done.10.w0), channel_id=1, source_target_pairs={{4,20},{5,21},{6,22},{7,23},{12,28},{13,29},{14,30},{15,31},{20,4}... | collective-permute-start | bytes 7077896 | tf_op jit(solution)/shard_map/ppermute | solution.py:52
  140.8 51.8 %collective-permute-start.13 = (bf16[3,1536,256]{2,1,0:T(8,128)(2,1)}, bf16[3,1536,256]{2,1,0:T(8,128)(2,1)}, u32[]{:S(2)}, u32[]{:S(2)}) collective-permute-start(bf16[3,1536,256]{2,1,0:T(8,128)(2,1)} %collective-permute-done.10.w0), channel_id=1, source_target_pairs={{4,28},{5,29},{6,30},{7,31},{12,20},{13,21},{14,22},{15,23},{20,12... | collective-permute-start | bytes 7077896 | tf_op jit(solution)/shard_map/ppermute | solution.py:52
  142.9 38.5 %collective-permute-start.14 = (bf16[256,1536]{1,0:T(8,128)(2,1)}, bf16[256,1536]{1,0:T(8,128)(2,1)}, u32[]{:S(2)}, u32[]{:S(2)}) collective-permute-start(bf16[256,1536]{1,0:T(8,128)(2,1)} %ct_ref.1), channel_id=1, source_target_pairs={{0,1},{1,0},{2,3},{3,2},{4,5},{5,4},{6,7},{7,6},{8,9},{9,8},{10,11... | collective-permute-start | bytes 2359304 | tf_op jit(solution)/shard_map/ppermute | solution.py:52
  175.5 34.2 %all-to-all-start.1 = ((bf16[4,96,1536]{2,1,0:T(8,128)(2,1)}), bf16[4,96,1536]{2,1,0:T(8,128)(2,1)}, u32[]{:S(2)}, u32[]{:S(2)}) async-start(bf16[4,96,1536]{2,1,0:T(8,128)(2,1)} %broadcast_in_dim.33), calls=%async_computation.1 | async-start | bytes 2359296 | tf_op jit(solution)/shard_map/all_to_all | solution.py:703
  179.7 284.3 %all-gather.7.cloned.1.call-start = ((), (), s32[]{:S(2)}) async-start(), calls=%async_computation.8 | async-start | bytes 10616832 | tf_op jit(solution)/shard_map/all_gather | solution.py:763
  260.2 56.5 %collective-permute-start.20 = (bf16[2,3,384,512]{3,2,1,0:T(8,128)(2,1)}, bf16[2,3,384,512]{3,2,1,0:T(8,128)(2,1)}, u32[]{:S(2)}, u32[]{:S(2)}) collective-permute-start(bf16[2,3,384,512]{3,2,1,0:T(8,128)(2,1)} %shard_map.174), channel_id=1, source_target_pairs={{0,8},{1,9},{2,10},{3,11},{4,12},{5,13},{6,14},{7,15},{8,0},{9,1},... | collective-permute-start | bytes 7077896 | tf_op jit(solution)/shard_map/ppermute | solution.py:52
  271.8 47.6 %collective-permute-start.23 = (bf16[2,256,1536]{2,1,0:T(8,128)(2,1)}, bf16[2,256,1536]{2,1,0:T(8,128)(2,1)S(1)}, u32[]{:S(2)}, u32[]{:S(2)}) collective-permute-start(bf16[2,256,1536]{2,1,0:T(8,128)(2,1)} %pad_maximum_fusion.4), channel_id=1, source_target_pairs={{0,4},{1,5},{2,6},{3,7},{4,0},{5,1},{6,2},{7,3},{8,12},{9,13},{10,... | collective-permute-start | bytes 4718600 | tf_op jit(solution)/shard_map/ppermute | solution.py:52
  271.9 32.2 %collective-permute-start.22 = (bf16[256,1536]{1,0:T(8,128)(2,1)}, bf16[256,1536]{1,0:T(8,128)(2,1)}, u32[]{:S(2)}, u32[]{:S(2)}) collective-permute-start(bf16[256,1536]{1,0:T(8,128)(2,1)} %get-tuple-element.166), channel_id=1, source_target_pairs={{0,4},{1,5},{2,6},{3,7},{4,0},{5,1},{6,2},{7,3},{8,12},{9,13},{10,... | collective-permute-start | bytes 2359304 | tf_op jit(solution)/shard_map/ppermute | solution.py:52
  272.3 47.1 %all-to-all-start.2 = ((bf16[4,256,384]{2,1,0:T(8,128)(2,1)}), bf16[4,256,384]{2,1,0:T(8,128)(2,1)S(1)}, u32[]{:S(2)}, u32[]{:S(2)}) async-start(bf16[4,256,384]{2,1,0:T(8,128)(2,1)} %get-tuple-element.158), calls=%async_computation.2 | async-start | bytes 1572864 | tf_op jit(solution)/shard_map/all_to_all | solution.py:703
  277.7 26.5 %collective-permute-start.21 = (bf16[256,768]{0,1:T(8,128)(2,1)S(1)}, bf16[256,768]{0,1:T(8,128)(2,1)S(1)}, u32[]{:S(2)}, u32[]{:S(2)}) collective-permute-start(bf16[256,768]{0,1:T(8,128)(2,1)S(1)} %bitcast.113), channel_id=1, source_target_pairs={{0,4},{1,5},{2,6},{3,7},{4,0},{5,1},{6,2},{7,3},{8,12},{9,13},{10,... | collective-permute-start | bytes 1179656 | tf_op jit(solution)/shard_map/ppermute | solution.py:52
  286.0 89.0 %collective-permute-start.26 = (bf16[2,3,384,512]{3,2,1,0:T(8,128)(2,1)}, bf16[2,3,384,512]{3,2,1,0:T(8,128)(2,1)}, u32[]{:S(2)}, u32[]{:S(2)}) collective-permute-start(bf16[2,3,384,512]{3,2,1,0:T(8,128)(2,1)} %shard_map.180), channel_id=1, source_target_pairs={{0,16},{1,17},{2,18},{3,19},{4,20},{5,21},{6,22},{7,23},{8,24},{9,... | collective-permute-start | bytes 7077896 | tf_op jit(solution)/shard_map/ppermute | solution.py:52
  320.7 26.0 %collective-permute-start.24 = (bf16[256,1536]{1,0:T(8,128)(2,1)}, bf16[256,1536]{1,0:T(8,128)(2,1)S(1)}, u32[]{:S(2)}, u32[]{:S(2)}) collective-permute-start(bf16[256,1536]{1,0:T(8,128)(2,1)} %fusion.11), channel_id=1, source_target_pairs={{0,1},{1,0},{2,3},{3,2},{4,5},{5,4},{6,7},{7,6},{8,9},{9,8},{10,11... | collective-permute-start | bytes 2359304 | tf_op jit(solution)/shard_map/ppermute | solution.py:52
  347.6 23.8 %all-to-all-start.3 = ((bf16[4,256,384]{2,1,0:T(8,128)(2,1)}), bf16[4,256,384]{2,1,0:T(8,128)(2,1)S(1)}, u32[]{:S(2)}, u32[]{:S(2)}) async-start(bf16[4,256,384]{2,1,0:T(8,128)(2,1)} %bitcast.109), calls=%async_computation.3 | async-start | bytes 1572864 | tf_op jit(solution)/shard_map/all_to_all | solution.py:703
  371.4 23.9 %all-to-all-start.4 = ((bf16[4,256,384]{2,1,0:T(8,128)(2,1)}), bf16[4,256,384]{2,1,0:T(8,128)(2,1)S(1)}, u32[]{:S(2)}, u32[]{:S(2)}) async-start(bf16[4,256,384]{2,1,0:T(8,128)(2,1)} %bitcast.102), calls=%async_computation.4 | async-start | bytes 1572864 | tf_op jit(solution)/shard_map/all_to_all | solution.py:703
  382.2 29.1 %collective-permute-start.28 = (bf16[3,384,512]{2,1,0:T(8,128)(2,1)}, bf16[3,384,512]{2,1,0:T(8,128)(2,1)}, u32[]{:S(2)}, u32[]{:S(2)}) collective-permute-start(bf16[3,384,512]{2,1,0:T(8,128)(2,1)} %fusion.15), channel_id=1, source_target_pairs={{0,16},{1,17},{2,18},{3,19},{4,20},{5,21},{6,22},{7,23},{8,24},{9,... | collective-permute-start | bytes 3538952 | tf_op jit(solution)/shard_map/ppermute | solution.py:52
  386.5 32.7 %collective-permute-start.29 = (bf16[3,384,512]{2,1,0:T(8,128)(2,1)}, bf16[3,384,512]{2,1,0:T(8,128)(2,1)}, u32[]{:S(2)}, u32[]{:S(2)}) collective-permute-start(bf16[3,384,512]{2,1,0:T(8,128)(2,1)} %fusion.16), channel_id=1, source_target_pairs={{0,8},{1,9},{2,10},{3,11},{4,12},{5,13},{6,14},{7,15},{8,0},{9,1},... | collective-permute-start | bytes 3538952 | tf_op jit(solution)/shard_map/ppermute | solution.py:52
  396.3 57.5 %all-to-all-start.6 = ((bf16[4,192,1536]{2,1,0:T(8,128)(2,1)}), bf16[4,192,1536]{2,1,0:T(8,128)(2,1)}, u32[]{:S(2)}, u32[]{:S(2)}) async-start(bf16[4,192,1536]{2,1,0:T(8,128)(2,1)} %bitcast.51), calls=%async_computation.6 | async-start | bytes 4718592 | tf_op jit(solution)/shard_map/all_to_all | solution.py:696
  415.6 31.7 %collective-permute-start.34 = (bf16[1,192,768]{2,1,0:T(8,128)(2,1)S(1)}, bf16[1,192,768]{2,1,0:T(8,128)(2,1)S(1)}, u32[]{:S(2)}, u32[]{:S(2)}) collective-permute-start(bf16[1,192,768]{2,1,0:T(8,128)(2,1)S(1)} %get-tuple-element.240), channel_id=1, source_target_pairs={{0,24},{1,25},{2,26},{3,27},{4,28},{5,29},{6,30},{7,31},{8,16},{9,... | collective-permute-start | bytes 884744 | tf_op jit(solution)/shard_map/ppermute | solution.py:52
  417.1 31.7 %collective-permute-start.33 = (bf16[1,192,768]{2,1,0:T(8,128)(2,1)S(1)}, bf16[1,192,768]{2,1,0:T(8,128)(2,1)S(1)}, u32[]{:S(2)}, u32[]{:S(2)}) collective-permute-start(bf16[1,192,768]{2,1,0:T(8,128)(2,1)S(1)} %get-tuple-element.241), channel_id=1, source_target_pairs={{0,16},{1,17},{2,18},{3,19},{4,20},{5,21},{6,22},{7,23},{8,24},{9,... | collective-permute-start | bytes 884744 | tf_op jit(solution)/shard_map/ppermute | solution.py:52
  419.1 33.7 %collective-permute-start.32 = (bf16[1,192,768]{2,1,0:T(8,128)(2,1)S(1)}, bf16[1,192,768]{2,1,0:T(8,128)(2,1)S(1)}, u32[]{:S(2)}, u32[]{:S(2)}) collective-permute-start(bf16[1,192,768]{2,1,0:T(8,128)(2,1)S(1)} %get-tuple-element.239), channel_id=1, source_target_pairs={{0,8},{1,9},{2,10},{3,11},{4,12},{5,13},{6,14},{7,15},{8,0},{9,1},... | collective-permute-start | bytes 884744 | tf_op jit(solution)/shard_map/ppermute | solution.py:52
  424.7 69.0 %collective-permute-start.30 = (bf16[3,192,1024]{2,1,0:T(8,128)(2,1)}, bf16[3,192,1024]{2,1,0:T(8,128)(2,1)}, u32[]{:S(2)}, u32[]{:S(2)}) collective-permute-start(bf16[3,192,1024]{2,1,0:T(8,128)(2,1)} %get-tuple-element.238), channel_id=1, source_target_pairs={{0,4},{1,5},{2,6},{3,7},{4,2},{5,3},{6,0},{7,1},{8,12},{9,13},{10,... | collective-permute-start | bytes 3538952 | tf_op jit(solution)/shard_map/ppermute | solution.py:52
  424.7 69.0 %collective-permute-start.31 = (bf16[3,192,1024]{2,1,0:T(8,128)(2,1)}, bf16[3,192,1024]{2,1,0:T(8,128)(2,1)}, u32[]{:S(2)}, u32[]{:S(2)}) collective-permute-start(bf16[3,192,1024]{2,1,0:T(8,128)(2,1)} %get-tuple-element.237), channel_id=1, source_target_pairs={{4,6},{5,7},{6,4},{7,5},{12,14},{13,15},{14,12},{15,13},{20,22},{2... | collective-permute-start | bytes 3538952 | tf_op jit(solution)/shard_map/ppermute | solution.py:52
  456.8 25.4 %collective-permute-start.37 = (bf16[192,384]{1,0:T(8,128)(2,1)}, bf16[192,384]{1,0:T(8,128)(2,1)}, u32[]{:S(2)}, u32[]{:S(2)}) collective-permute-start(bf16[192,384]{1,0:T(8,128)(2,1)} %get-tuple-element.245), channel_id=1, source_target_pairs={{0,3},{1,2},{2,1},{3,0},{4,7},{5,6},{6,5},{7,4},{8,11},{9,10},{10,... | collective-permute-start | bytes 442376 | tf_op jit(solution)/shard_map/ppermute | solution.py:52
  (55 other events, 487.0 us)
Sparse Core Ops, SparseCore 0:
  63.8 40.0 all-gather.4
  209.8 60.2 all-gather.6
